TPU v7x, 32 devices: a whole 2x2x4 slice. The times are simulated.
32 devices in a mesh: seq: 16 (over z, y, core), mlp: 2 (over x).
Axes of the slice: x: 2, y: 2, z: 4, core: 2. Of those that a mesh axis runs over, the one named last changes fastest.
Arguments:
- frames: bfloat16 [32768, 512], P(('seq', 'mlp')), may hold values from -6 to 6
- cotangent: bfloat16 [32768, 512], P(('seq', 'mlp')), may hold values from -6 to 6
- lengths: int32 [36], replicated, may hold values from 200 to 2304, as said below
- owners: int32 [16], replicated, may hold values from 0 to 15, as said below
- attn_master: float32 [32, 128, 512], P('seq')
- attn_first: float32 [32, 128, 512], P('seq'), may hold values from -64 to 64
- attn_second: float32 [32, 128, 512], P('seq'), may hold values from 8.192 to 32.768
- attn_average: float32 [32, 128, 512], P('seq'), may hold values from -1 to 1
- small_master: float32 [17, 512], replicated
- small_first: float32 [17, 512], replicated, may hold values from -128 to 128
- small_second: float32 [17, 512], replicated, may hold values from 32.768 to 131.072
- small_average: float32 [17, 512], replicated, may hold values from -3 to 3
- mlp_master: float32 [2, 512, 2048], P(None, None, 'mlp'), may hold values from -0.25 to 0.25
- mlp_first: float32 [2, 512, 2048], P(None, None, 'mlp'), may hold values from -48 to 48
- mlp_second: float32 [2, 512, 2048], P(None, None, 'mlp'), may hold values from 5.24288 to 20.97152
- mlp_average: float32 [2, 512, 2048], P(None, None, 'mlp'), may hold values from -0.25 to 0.25
- bias_master: float32 [2048], P('mlp'), may hold values from -3 to 3
- bias_first: float32 [2048], P('mlp'), may hold values from -32 to 32
- bias_second: float32 [2048], P('mlp'), may hold values from 2.94912 to 11.79648
- bias_average: float32 [2048], P('mlp'), may hold values from -3 to 3
Outputs:
- output: bfloat16 [32768, 512], P(('seq', 'mlp'))
- in_grad: bfloat16 [32768, 512], P(('seq', 'mlp'))
- attn_weights: float32 [32, 128, 512], P('seq')
- attn_moment: float32 [32, 128, 512], P('seq')
- attn_square: float32 [32, 128, 512], P('seq')
- attn_mean: float32 [32, 128, 512], P('seq')
- small_weights: float32 [17, 512], replicated
- small_moment: float32 [17, 512], replicated
- small_square: float32 [17, 512], replicated
- small_mean: float32 [17, 512], replicated
- mlp_weights: float32 [2, 512, 2048], P(None, None, 'mlp')
- mlp_moment: float32 [2, 512, 2048], P(None, None, 'mlp')
- mlp_square: float32 [2, 512, 2048], P(None, None, 'mlp')
- mlp_mean: float32 [2, 512, 2048], P(None, None, 'mlp')
- bias_weights: float32 [2048], P('mlp')
- bias_moment: float32 [2048], P('mlp')
- bias_square: float32 [2048], P('mlp')
- bias_mean: float32 [2048], P('mlp')
Inputs may be any that keep to these rules, and one draw needn't show every extreme that they name: `lengths`: videos lie end to end from frame 0 in this order; their total falls within the last 1024 frames, at least 8 short of 32768. `owners`: no owner holds more than 2 tiles, and some owner holds exactly 2.
All inputs are finite; a program needn't handle non-finite values.
Results may differ from a plain program's by a relative error of at most 0.014.
Values may be sent and summed in bfloat16 or wider, within the bound.
No kernel may reach another device: no remote copies, remote signals or barrier semaphores. Data moves between devices by JAX's collectives and lax.ppermute only.
A program may use at most 192 MiB of HBM per device.

v0:
```python
import jax
import jax.numpy as jnp
from jax import lax
from jax.sharding import PartitionSpec as P

HEADS = 4
HEAD = 128
HALF = 9
TILE = 128
TILES = 16
CAP = 2
STEP = 7


HIGH = lax.Precision.HIGHEST
NORM_EPS = 1e-05
MASKED = -1e30
BETA_ONE = 0.9
BETA_TWO = 0.999
ADAM_EPS = 1e-08
MATRIX_RATE = 0.03
MATRIX_DECAY = 0.05
SMALL_RATE = 0.3
AVERAGE_RATE = 0.8


def padded_2(array, sides, width):
    for axis, dim in sides:
        devices, length = (lax.axis_size(axis), array.shape[dim])
        up = [(i, (i + 1) % devices) for i in range(devices - 1)]
        down = [(j, i) for i, j in up]
        last = lax.slice_in_dim(array, length - width, length, axis=dim)
        initial = lax.slice_in_dim(array, 0, width, axis=dim)
        before = lax.ppermute(last, axis, up)
        after = lax.ppermute(initial, axis, down)
        array = jnp.concatenate([before, array, after], axis=dim)
    return array


def frame_tables(lengths, positions):
    ends = jnp.cumsum(lengths)
    video = jnp.sum((positions[:, None] >= ends[None, :]).astype(jnp.int32), axis=1)
    valid = (positions >= 0) & (positions < ends[-1])
    return (video, valid)


def conv_keeps(video, valid):
    keep_prev = valid[1:-1] & valid[:-2] & (video[1:-1] == video[:-2])
    keep_after = valid[1:-1] & valid[2:] & (video[1:-1] == video[2:])
    return (keep_prev.astype(jnp.float32), keep_after.astype(jnp.float32))


def norm_rows(values, gain, bias):
    mean = jnp.mean(values, axis=-1, keepdims=True)
    centred = values - mean
    spread = jnp.mean(centred * centred, axis=-1, keepdims=True)
    return centred * lax.rsqrt(spread + NORM_EPS) * gain + bias


def conv_three(padded, taps, keep_prev, keep_after):
    before = padded[:-2] * keep_prev[:, None]
    middle = padded[1:-1]
    after = padded[2:] * keep_after[:, None]
    return taps[:, 0, None, :] * before + taps[:, 1, None, :] * middle + taps[:, 2, None, :] * after


def window_mask(query_pos, key_pos, query_video, key_video, query_valid, key_valid):
    offset = query_pos[:, None] - key_pos[None, :]
    band = jnp.abs(offset) <= HALF
    same = (query_video[:, None] == key_video[None, :]) & query_valid[:, None] & key_valid[None, :]
    return band & (same | (offset == 0))


def tile_slots(owners):
    index = jnp.arange(owners.shape[0], dtype=jnp.int32)
    earlier = (owners[None, :] == owners[:, None]) & (index[None, :] < index[:, None])
    return owners * CAP + jnp.sum(earlier.astype(jnp.int32), axis=1)


def adamw(weight, grad, first, second, average, rate, decay):
    first_new = BETA_ONE * first + (1.0 - BETA_ONE) * grad
    second_new = BETA_TWO * second + (1.0 - BETA_TWO) * grad * grad
    ratio = (
        first_new
        / (1.0 - BETA_ONE**STEP)
        / (jnp.sqrt(second_new / (1.0 - BETA_TWO**STEP)) + ADAM_EPS)
    )
    weight_new = weight - rate * (ratio + decay * weight)
    average_new = AVERAGE_RATE * average + (1.0 - AVERAGE_RATE) * weight_new
    return (weight_new, first_new, second_new, average_new)


def contract_rows(left, right):
    return lax.dot_general(
        left, right, (((0,), (0,)), ((), ())), preferred_element_type=jnp.float32
    )


def contract_cols(left, right):
    return lax.dot_general(
        left, right, (((1,), (1,)), ((), ())), preferred_element_type=jnp.float32
    )


def gelu_exact(values):
    return jax.nn.gelu(values, approximate=False)


def feed_local(second, grad_rows, weights, bias):
    hidden = jnp.dot(second, weights[0], preferred_element_type=jnp.float32) + bias.astype(
        jnp.float32
    )
    active, gelu_pull = jax.vjp(gelu_exact, hidden)
    active = active.astype(jnp.bfloat16)
    active_grad = jnp.dot(grad_rows, weights[1], preferred_element_type=jnp.float32)
    hidden_grad = gelu_pull(active_grad)[0].astype(jnp.bfloat16)
    weight_grads = jnp.stack([contract_rows(second, hidden_grad), contract_rows(grad_rows, active)])
    bias_grad = jnp.sum(hidden_grad, axis=0, dtype=jnp.float32)
    return (active, hidden_grad, weight_grads, bias_grad)


def shards(
    frames,
    cotangent,
    lengths,
    owners,
    attn_master,
    attn_first,
    attn_second,
    attn_average,
    small_master,
    small_first,
    small_second,
    small_average,
    mlp_master,
    mlp_first,
    mlp_second,
    mlp_average,
    bias_master,
    bias_first,
    bias_second,
    bias_average,
):
    local = frames.shape[0]
    width = frames.shape[1]
    block = min(512, local)
    blocks = local // block
    span = block + 2 * HALF
    scale = HEAD ** (-0.5)
    anchor = lax.axis_index(("seq", "mlp")) * local
    wide_pos = anchor - HALF - 1 + jnp.arange(local + 2 * HALF + 2, dtype=jnp.int32)
    wide_video, wide_valid = frame_tables(lengths, wide_pos)
    wide_prev, wide_after = conv_keeps(wide_video, wide_valid)
    key_video = wide_video[1:-1]
    key_valid = wide_valid[1:-1]
    own_video = key_video[HALF : HALF + local]
    own_valid = key_valid[HALF : HALF + local]
    keep_prev = wide_prev[HALF : HALF + local]
    keep_after = wide_after[HALF : HALF + local]
    valid_rows = own_valid.astype(jnp.float32)[:, None]
    gathered = lax.all_gather(attn_master, "seq", axis=0, tiled=True)
    slots = tile_slots(owners)
    matrices = jnp.take(gathered, slots, axis=0).reshape(4, width, width)
    rounded = matrices.astype(jnp.bfloat16)
    taps = small_master[8:17].reshape(3, 3, width)
    inputs = frames.astype(jnp.float32)
    first = norm_rows(inputs, small_master[0], small_master[1]).astype(jnp.bfloat16)
    near = padded_2(first, ((("seq", "mlp"), 0),), 1)
    convs = conv_three(near.astype(jnp.float32), taps, keep_prev, keep_after).astype(jnp.bfloat16)
    keys_own = jnp.dot(convs[1], rounded[1], preferred_element_type=jnp.float32).astype(
        jnp.bfloat16
    )
    values_own = (
        jnp.dot(convs[2], rounded[2], preferred_element_type=jnp.float32) + small_master[5]
    ).astype(jnp.bfloat16)
    paired = padded_2(jnp.stack([keys_own, values_own]), ((("seq", "mlp"), 1),), HALF)
    keys_wide = paired[0]
    values_wide = paired[1]
    query = (
        jnp.dot(convs[0], rounded[0], preferred_element_type=jnp.float32) + small_master[4]
    ).astype(jnp.bfloat16)
    query3 = query.reshape(local, HEADS, HEAD)
    keys3 = keys_wide.reshape(local + 2 * HALF, HEADS, HEAD)
    values3 = values_wide.reshape(local + 2 * HALF, HEADS, HEAD)
    starts = jnp.arange(blocks, dtype=jnp.int32) * block

    def block_scores(start):
        query_part = lax.dynamic_slice_in_dim(query3, start, block, 0)
        key_part = lax.dynamic_slice_in_dim(keys3, start, span, 0)
        value_part = lax.dynamic_slice_in_dim(values3, start, span, 0)
        query_pos = anchor + start + jnp.arange(block, dtype=jnp.int32)
        key_pos = anchor - HALF + start + jnp.arange(span, dtype=jnp.int32)
        allowed = window_mask(
            query_pos,
            key_pos,
            lax.dynamic_slice_in_dim(own_video, start, block, 0),
            lax.dynamic_slice_in_dim(key_video, start, span, 0),
            lax.dynamic_slice_in_dim(own_valid, start, block, 0),
            lax.dynamic_slice_in_dim(key_valid, start, span, 0),
        )
        scores = (
            jnp.einsum("qhd,khd->hqk", query_part, key_part, preferred_element_type=jnp.float32)
            * scale
        )
        return (query_part, key_part, value_part, jnp.where(allowed[None], scores, MASKED))

    def forward_block(start):
        query_part, key_part, value_part, masked = block_scores(start)
        top = jnp.max(masked, axis=-1, keepdims=True)
        expo = jnp.exp(masked - top)
        total = jnp.sum(expo, axis=-1, keepdims=True)
        probs_low = (expo / total).astype(jnp.bfloat16)
        mixed_part = jnp.einsum(
            "hqk,khd->qhd", probs_low, value_part, preferred_element_type=jnp.float32
        )
        return (mixed_part.reshape(block, width), (top + jnp.log(total))[:, :, 0])

    mixed_blocks, log_totals = lax.map(forward_block, starts)
    mixed_low = mixed_blocks.reshape(local, width).astype(jnp.bfloat16)
    branch = jnp.dot(mixed_low, rounded[3], preferred_element_type=jnp.float32) + small_master[6]
    middle = inputs + valid_rows * branch
    second = norm_rows(middle, small_master[2], small_master[3]).astype(jnp.bfloat16)
    grad_rows = cotangent * own_valid.astype(jnp.bfloat16)[:, None]
    local_weights = mlp_master.astype(jnp.bfloat16)
    gathered_rows = lax.all_gather(second, "mlp", axis=0, tiled=True)
    gathered_grads = lax.all_gather(grad_rows, "mlp", axis=0, tiled=True)
    active, hidden_grad, weight_parts, bias_part = feed_local(
        gathered_rows, gathered_grads, local_weights, bias_master.astype(jnp.bfloat16)
    )
    result = lax.psum_scatter(
        contract_cols(active, local_weights[1]), "mlp", scatter_dimension=0, tiled=True
    )
    second_grad = lax.psum_scatter(
        contract_cols(hidden_grad, local_weights[0]), "mlp", scatter_dimension=0, tiled=True
    )
    weight_sum, bias_sum = lax.psum((weight_parts, bias_part), "seq")
    output = (middle + valid_rows * (result + small_master[7])).astype(jnp.bfloat16)
    _, pull_two = jax.vjp(norm_rows, middle, small_master[2], small_master[3])
    back_middle, gain_two, bias_two = pull_two(second_grad)
    middle_grad = cotangent.astype(jnp.float32) + back_middle
    branch_grad = (valid_rows * middle_grad).astype(jnp.bfloat16)
    mixed_grad = contract_cols(branch_grad, rounded[3]).astype(jnp.bfloat16)
    mixed_grad3 = mixed_grad.reshape(local, HEADS, HEAD)

    def back_block(carry, inputs_pair):
        start, log_total = inputs_pair
        key_acc, value_acc = carry
        query_part, key_part, value_part, masked = block_scores(start)
        probs = jnp.exp(masked - log_total[:, :, None])
        probs_low = probs.astype(jnp.bfloat16)
        grad_part = lax.dynamic_slice_in_dim(mixed_grad3, start, block, 0)
        prob_grad = jnp.einsum(
            "qhd,khd->hqk", grad_part, value_part, preferred_element_type=jnp.float32
        )
        value_add = jnp.einsum(
            "hqk,qhd->khd", probs_low, grad_part, preferred_element_type=jnp.float32
        )
        score_grad = (
            probs * (prob_grad - jnp.sum(probs * prob_grad, axis=-1, keepdims=True))
        ).astype(jnp.bfloat16)
        query_add = (
            jnp.einsum("hqk,khd->qhd", score_grad, key_part, preferred_element_type=jnp.float32)
            * scale
        )
        key_add = (
            jnp.einsum("hqk,qhd->khd", score_grad, query_part, preferred_element_type=jnp.float32)
            * scale
        )
        key_acc = lax.dynamic_update_slice_in_dim(
            key_acc, lax.dynamic_slice_in_dim(key_acc, start, span, 0) + key_add, start, 0
        )
        value_acc = lax.dynamic_update_slice_in_dim(
            value_acc, lax.dynamic_slice_in_dim(value_acc, start, span, 0) + value_add, start, 0
        )
        return ((key_acc, value_acc), query_add)

    empty = jnp.zeros((local + 2 * HALF, HEADS, HEAD), jnp.float32)
    (key_grad, value_grad), query_grads = lax.scan(back_block, (empty, empty), (starts, log_totals))
    grads_wide = jnp.stack([key_grad.reshape(-1, width), value_grad.reshape(-1, width)])
    edges = jnp.concatenate([grads_wide[:, :HALF], grads_wide[:, local + HALF :]], axis=1)
    arrived = padded_2(edges, ((("seq", "mlp"), 1),), HALF)
    own_grads = grads_wide[:, HALF : HALF + local]
    own_grads = (
        own_grads.at[:, :HALF]
        .add(arrived[:, :HALF])
        .at[:, local - HALF :]
        .add(arrived[:, 3 * HALF :])
    )
    key_low = own_grads[0].astype(jnp.bfloat16)
    value_low = own_grads[1].astype(jnp.bfloat16)
    query_low = query_grads.reshape(local, width).astype(jnp.bfloat16)
    matrix_grads = jnp.stack(
        [
            contract_rows(convs[0], query_low),
            contract_rows(convs[1], key_low),
            contract_rows(convs[2], value_low),
            contract_rows(mixed_low, branch_grad),
        ]
    )
    conv_grads = jnp.stack(
        [
            contract_cols(query_low, rounded[0]),
            contract_cols(key_low, rounded[1]),
            contract_cols(value_low, rounded[2]),
        ]
    )

    def conv_apply(padded, weights):
        return conv_three(padded, weights, keep_prev, keep_after)

    _, conv_pull = jax.vjp(conv_apply, near.astype(jnp.float32), taps)
    near_grad, taps_grad = conv_pull(conv_grads)
    rim_grads = jnp.stack([near_grad[0], near_grad[-1]])
    landed = padded_2(rim_grads, ((("seq", "mlp"), 0),), 1)
    first_grad = near_grad[1:-1].at[0].add(landed[0]).at[-1].add(landed[3])
    _, pull_one = jax.vjp(norm_rows, inputs, small_master[0], small_master[1])
    back_input, gain_one, bias_one = pull_one(first_grad)
    in_grad = (middle_grad + back_input).astype(jnp.bfloat16)
    small_grad = jnp.concatenate(
        [
            jnp.stack(
                [
                    gain_one,
                    bias_one,
                    gain_two,
                    bias_two,
                    jnp.sum(query_low, axis=0, dtype=jnp.float32),
                    jnp.sum(value_low, axis=0, dtype=jnp.float32),
                    jnp.sum(branch_grad, axis=0, dtype=jnp.float32),
                    jnp.sum(grad_rows, axis=0, dtype=jnp.float32),
                ]
            ),
            taps_grad.reshape(9, width),
        ],
        axis=0,
    )
    matrix_sum, small_sum = lax.psum((matrix_grads, small_grad), ("seq", "mlp"))
    seat = lax.axis_index("seq")
    seats = seat * CAP + jnp.arange(CAP, dtype=jnp.int32)
    hits = (slots[None, :] == seats[:, None]).astype(jnp.float32)
    filled = jnp.sum(hits, axis=1)[:, None, None]
    slot_grads = jnp.dot(
        hits, matrix_sum.reshape(TILES, -1), precision=HIGH, preferred_element_type=jnp.float32
    ).reshape(CAP, TILE, width)
    attn_new = adamw(
        attn_master, slot_grads, attn_first, attn_second, attn_average, MATRIX_RATE, MATRIX_DECAY
    )
    small_new = adamw(
        small_master, small_sum, small_first, small_second, small_average, SMALL_RATE, 0.0
    )
    mlp_new = adamw(
        mlp_master, weight_sum, mlp_first, mlp_second, mlp_average, MATRIX_RATE, MATRIX_DECAY
    )
    bias_new = adamw(bias_master, bias_sum, bias_first, bias_second, bias_average, SMALL_RATE, 0.0)
    return (
        output,
        in_grad,
        attn_new[0] * filled,
        attn_new[1] * filled,
        attn_new[2] * filled,
        attn_new[3] * filled,
        small_new[0],
        small_new[1],
        small_new[2],
        small_new[3],
        mlp_new[0],
        mlp_new[1],
        mlp_new[2],
        mlp_new[3],
        bias_new[0],
        bias_new[1],
        bias_new[2],
        bias_new[3],
    )


def solution(mesh):
    in_specs = (
        P(("seq", "mlp"), None),
        P(("seq", "mlp"), None),
        P(),
        P(),
        P("seq", None, None),
        P("seq", None, None),
        P("seq", None, None),
        P("seq", None, None),
        P(),
        P(),
        P(),
        P(),
        P(None, None, "mlp"),
        P(None, None, "mlp"),
        P(None, None, "mlp"),
        P(None, None, "mlp"),
        P("mlp"),
        P("mlp"),
        P("mlp"),
        P("mlp"),
    )
    out_specs = (
        P(("seq", "mlp"), None),
        P(("seq", "mlp"), None),
        P("seq", None, None),
        P("seq", None, None),
        P("seq", None, None),
        P("seq", None, None),
        P(),
        P(),
        P(),
        P(),
        P(None, None, "mlp"),
        P(None, None, "mlp"),
        P(None, None, "mlp"),
        P(None, None, "mlp"),
        P("mlp"),
        P("mlp"),
        P("mlp"),
        P("mlp"),
    )
    return jax.shard_map(shards, mesh=mesh, in_specs=in_specs, out_specs=out_specs, check_vma=False)
```

profile of v0, /device:TPU:0, one launch (start us, length us, event | category | flops | bytes accessed | tf_op | source)
XLA Modules:
  0.0 737.5 jit_solution(13123107208626648463)
XLA Ops:
  12.9 4.8 collective-permute-start
  21.6 3.3 collective-permute-done.1
  28.9 2.8 slice_multiply_fusion.1
  33.7 3.7 copy.180
  37.4 3.0 copy.178
  40.4 5.6 add_convert_fusion.1
  46.0 19.2 %all-gather.4.cloned.1.call-done = bf16[32,128,512]{2,1,0:T(8,128)(2,1)} async-done(((bf16[2,128,512]{2,1,0:T(8,128)(2,1)}), bf16[32,128,512]{2,1,0:T(8,128)(2,1)}) %all-gather.4.cloned.1.call-update) | async-done | bytes 4194320 | tf_op jit(solution)/shard_map/all_gather | solution.py:161
  65.1 2.9 gather_fusion
  71.3 3.4 collective-permute-start.2
  80.5 9.5 %concatenate.18 = bf16[2,1042,512]{2,1,0:T(8,128)(2,1)S(1)} concatenate(bf16[2,9,512]{2,1,0:T(8,128)(2,1)S(1)} %collective-permute-done.2, bf16[2,1024,512]{2,1,0:T(8,128)(2,1)} %pad_maximum_fusion.3, bf16[2,9,512]{2,1,0:T(8,128)(2,1)S(1)} %collective-permute-done.3), dimensions={1} | concatenate | bytes 4268032 | tf_op jit(solution)/shard_map/concatenate | solution.py:36
  91.5 2.4 reshape_squeeze.6
  95.5 24.0 %while.34 = (s32[]{:T(128)}, bf16[2,512,512]{2,1,0:T(8,128)(2,1)}, f32[2,4,512]{2,1,0:T(4,128)S(1)}, s32[2]{0:T(128)S(1)}, bf16[1042,4,128]{2,0,1:T(8,128)(2,1)}...) while((s32[]{:T(128)}, bf16[2,512,512]{2,1,0:T(8,128)(2,1)}, ...), condition=%wide.region_8.9_spmd, body=%wide.region_5.8_spmd.sunk | while | flops 571211776 | bytes 18447052 | solution.py:218
  103.7 2.7 fusion.151
  115.7 2.7 fusion.151
  119.5 2.5 fusion.113
  127.3 3.8 convert_element_type.149
  131.2 26.4 %all-gather.6.cloned.1.call-done = bf16[2048,512]{0,1:T(8,128)(2,1)} async-done(((bf16[1024,512]{0,1:T(8,128)(2,1)}), bf16[2048,512]{0,1:T(8,128)(2,1)}) %all-gather.6.cloned.1.call-update) | async-done | bytes 2097168 | tf_op jit(solution)/shard_map/all_gather | solution.py:225
  157.5 23.3 %multiply_convert_fusion.1 = (bf16[2048,1024]{1,0:T(8,128)(2,1)}, f32[2048,1024]{1,0:T(8,128)}, f32[2048,1024]{1,0:T(8,128)}) fusion(f32[1024]{0:T(1024)S(1)} %convert_convert_fusion, bf16[2048,512]{0,1:T(8,128)(2,1)} %all-gather.6.cloned.1.call-done, bf16[2,512,1024]{2,1,0:T(8,128)(2,1)} %convert_element_type.149), kind=kOutput, calls=%fused_computation.73 | convolution fusion | flops 2285895680 | bytes 24121344 | tf_op jit(solution)/shard_map/dot_general | solution.py:110
  180.8 12.0 %all-gather.8.cloned.1.call-done = bf16[2048,512]{1,0:T(8,128)(2,1)} async-done(((bf16[1024,512]{1,0:T(8,128)(2,1)}), bf16[2048,512]{1,0:T(8,128)(2,1)}) %all-gather.8.cloned.1.call-update) | async-done | bytes 2097168 | tf_op jit(solution)/shard_map/all_gather | solution.py:226
  192.8 5.3 convolution_bitcast_fusion.3
  199.3 7.9 %convert_reduce_fusion = (f32[1024]{0:T(1024)S(1)}, bf16[2048,1024]{1,0:T(8,128)(2,1)S(1)}) fusion(f32[2048,1024]{1,0:T(8,128)S(1)} %copy-done.76, bf16[2048,512]{1,0:T(8,128)(2,1)S(1)} %copy-done.73, bf16[2,512,1024]{2,1,0:T(8,128)(2,1)S(1)} %copy-done.32, f32[2048,1024]{1,0:T(8,128)} %get-tuple-element.772, f32[1024]{0:T(1024)S(1)} %convert_convert_fusion), kind=kOutput, calls=%fused_computation.71 | convolution fusion | flops 2183134208 | bytes 24125440 | tf_op jit(solution)/shard_map/dot_general | solution.py:115
  207.2 2.3 convolution_bitcast_fusion.4
  209.6 2.5 pad_maximum_fusion.2
  212.3 6.9 fusion.76
  219.2 6.9 fusion.78
  227.9 33.9 %psum.31 = f32[1024]{0:T(1024)S(1)} all-reduce(f32[1024]{0:T(1024)S(1)} %get-tuple-element.773), channel_id=1, replica_groups=mesh['seq'=16,'mlp'=2] {'seq'}, use_global_device_ids=true, to_apply=%region_39.40 | all-reduce | flops 1024 | bytes 8192 | tf_op jit(solution)/shard_map/psum | solution.py:236
  262.5 61.3 %all-reduce.11.cloned.1.call-done = f32[2,512,1024]{2,1,0:T(8,128)} async-done(((f32[2,512,1024]{2,1,0:T(8,128)}), f32[2,512,1024]{2,1,0:T(8,128)}) %all-reduce.11.cloned.1.call-update) | async-done | bytes 4194320 | tf_op jit(solution)/shard_map/psum | solution.py:236
  323.8 14.4 %multiply_add_fusion = (f32[2,512,1024]{2,1,0:T(8,128)}, f32[2,512,1024]{2,1,0:T(8,128)}, f32[2,512,1024]{2,1,0:T(8,128)}, f32[2,512,1024]{2,1,0:T(8,128)}) fusion(f32[2,512,1024]{2,1,0:T(8,128)} %param.47, f32[2,512,1024]{2,1,0:T(8,128)} %param.44, f32[2,512,1024]{2,1,0:T(8,128)} %all-reduce.11.cloned.1.call-done, f32[2,512,1024]{2,1,0:T(8,128)} %param.45, ...), kind=kLoop, calls=%fused_computation.102 | loop fusion | flops 18874368 | bytes 37748736 | tf_op jit(solution)/shard_map/add | solution.py:89
  338.2 41.1 %reduce-scatter.5.cloned.1.call-done = f32[1024,512]{0,1:T(8,128)} async-done(((f32[2048,512]{0,1:T(8,128)}), f32[1024,512]{0,1:T(8,128)}) %reduce-scatter.5.cloned.1.call-update) | async-done | bytes 2097168 | tf_op jit(solution)/shard_map/reduce_scatter | solution.py:233
  379.3 3.0 multiply_reduce_fusion.7
  382.3 53.5 %reduce-scatter.3.cloned.1.call-done = f32[1024,512]{0,1:T(8,128)} async-done(((f32[2048,512]{0,1:T(8,128)}), f32[1024,512]{0,1:T(8,128)}) %reduce-scatter.3.cloned.1.call-update) | async-done | bytes 2097168 | tf_op jit(solution)/shard_map/reduce_scatter | solution.py:230
  435.8 4.7 fusion.104
  441.0 2.0 convolution_convert_fusion
  447.8 46.8 %while.35 = (s32[]{:T(128)}, f32[1042,4,128]{2,1,0:T(4,128)}, f32[1042,4,128]{2,1,0:T(4,128)}, bf16[2,512,4,128]{1,3,2,0:T(8,128)(2,1)}, s32[2]{0:T(128)S(1)}, /...) while((s32[]{:T(128)}, f32[1042,4,128]{2,1,0:T(4,128)}, ...), condition=%wide.region_17.18_spmd, body=%wide.region_15.17_spmd.sunk | while | flops 1409162240 | bytes 107382736 | solution.py:278
  451.8 2.8 fusion.160
  458.3 3.8 fusion.162
  462.1 2.7 multiply_reduce_fusion.11
  475.1 2.8 fusion.160
  481.6 3.8 fusion.162
  485.4 2.7 multiply_reduce_fusion.11
  496.3 3.2 convolution_bitcast_fusion.2
  499.5 3.1 convolution_bitcast_fusion.8
  502.6 2.3 stack_reshape.6
  504.8 3.3 constant_dynamic-update-slice_fusion.2
  508.1 2.3 stack_reshape.7
  510.4 3.2 constant_dynamic-update-slice_fusion.1
  514.5 2.6 collective-permute-start.4
  517.4 4.8 slice.359
  527.3 3.0 collective-permute-done.5
  532.7 2.6 convolution_bitcast_fusion
  535.7 1.9 convolution_bitcast_fusion.1
  538.1 7.4 %multiply_reduce_fusion.1 = (f32[3,512]{1,0:T(4,128)S(1)}, f32[1024,512]{1,0:T(8,128)}, f32[3,512]{1,0:T(4,128)S(1)}, f32[1024,512]{1,0:T(8,128)}, f32[1024,512]{1,0:T(8,128)}, /*index=5*/f32[3,512]{1,0:T(4,128)S(1)}) fusion(f32[1024,512]{1,0:T(8,128)S(1)} %copy-done.19, f32[1,1024,512]{2,1,0:T(8,128)S(1)} %convolution_bitcast_fusion, ...), kind=kLoop, calls=%fused_computation.89 | loop fusion | flops 20442624 | bytes 18911232 | tf_op jit(solution)/shard_map/transpose(jvp())/reduce_sum | solution.py:64
  545.5 3.1 copy.197
  550.4 1.9 copy.198
  552.4 3.8 broadcast_multiply_fusion
  563.4 2.7 collective-permute-start.6
  567.4 2.6 pad_maximum_fusion.1
  570.0 4.0 reshape.533
  574.0 4.8 copy.281
  586.0 2.0 add_convert_fusion.2
  588.0 2.3 copy.205
  590.4 44.7 %psum.29 = f32[17,512]{1,0:T(8,128)S(1)} all-reduce(f32[17,512]{1,0:T(8,128)S(1)} %concatenate.19), channel_id=1, replica_groups=mesh['seq'=16,'mlp'=2] {'seq','mlp'}, use_global_device_ids=true, to_apply=%region_36.37 | all-reduce | flops 8704 | bytes 69632 | tf_op jit(solution)/shard_map/psum | solution.py:337
  635.8 88.4 %all-reduce.9.cloned.1.call-done = f32[128,512,16]{1,2,0:T(8,128)} async-done(((f32[128,512,16]{1,2,0:T(8,128)}), f32[128,512,16]{1,2,0:T(8,128)}) %all-reduce.9.cloned.1.call-update) | async-done | bytes 4194320 | tf_op jit(solution)/shard_map/psum | solution.py:337
  724.2 3.7 fusion.96
  (358 shorter events, 101.5 us)
Async XLA Ops:
  7.2 57.9 %all-gather.4.cloned.1.call-start = ((), (), s32[]{:S(2)}) async-start(), calls=%async_computation.2 | async-start | bytes 4456448 | tf_op jit(solution)/shard_map/all_gather | solution.py:161
  9.0 148.5 %all-gather.6.cloned.1.call-start = ((), (), s32[]{:S(2)}) async-start(), calls=%async_computation.3 | async-start | bytes 3145728 | tf_op jit(solution)/shard_map/all_gather | solution.py:225
  10.6 8.5 %copy-start.71 = (s32[36]{0:T(128)S(1)}, s32[36]{0:T(128)}, u32[]{:S(2)}) copy-start(s32[36]{0:T(128)} %param.34) | copy-start | bytes 436
  10.8 9.1 %slice-start.2 = ((f32[17,512]{1,0:T(8,128)}), f32[9,512]{1,0:T(8,128)S(1)}, s32[]{:S(2)}) async-start(f32[17,512]{1,0:T(8,128)} %param.40), calls=%async_computation.11 | async-start | bytes 65536 | tf_op jit(solution)/shard_map/slice | solution.py:165
  10.8 9.1 %copy-start.70 = (s32[16]{0:T(128)S(1)}, s32[16]{0:T(128)}, u32[]{:S(2)}) copy-start(s32[16]{0:T(128)} %param.35) | copy-start | bytes 196
  10.8 10.8 %copy-start.41 = (f32[1024]{0:T(1024)}, f32[1024]{0:T(1024)S(1)}, u32[]{:S(2)}) copy-start(f32[1024]{0:T(1024)S(1)} %broadcast_multiply_fusion.7) | copy-start | bytes 12292
  12.9 8.7 %collective-permute-start = (bf16[1,512]{0,1:T(8,128)(2,1)S(1)}, bf16[1,512]{0,1:T(8,128)(2,1)S(1)}, u32[]{:S(2)}, u32[]{:S(2)}) collective-permute-start(bf16[1,512]{0,1:T(8,128)(2,1)S(1)} %get-tuple-element.747), channel_id=1, source_target_pairs={{0,1},{1,2},{2,3},{3,4},{4,5},{5,6},{6,7},{7,8},{8,9},{9,10},{10,1... | collective-permute-start | bytes 3080 | tf_op jit(solution)/shard_map/ppermute | solution.py:34
  17.8 7.2 collective-permute-start.1
  21.4 7.5 %copy-start.56 = (f32[1024]{0:T(1024)}, f32[1024]{0:T(1024)S(1)}, u32[]{:S(2)}) copy-start(f32[1024]{0:T(1024)S(1)} %get-tuple-element.759) | copy-start | bytes 12292
  21.4 7.5 %copy-start.58 = (f32[1024]{0:T(1024)}, f32[1024]{0:T(1024)S(1)}, u32[]{:S(2)}) copy-start(f32[1024]{0:T(1024)S(1)} %get-tuple-element.760) | copy-start | bytes 12292
  21.5 18.8 %copy-start.43 = (f32[3,1,512]{2,0,1:T(4,128)}, f32[3,1,512]{2,0,1:T(4,128)S(1)}, u32[]{:S(2)}) copy-start(f32[3,1,512]{2,0,1:T(4,128)S(1)} %copy.282) | copy-start | bytes 18436
  21.5 18.8 %copy-start.45 = (f32[3,1,512]{2,0,1:T(4,128)}, f32[3,1,512]{2,0,1:T(4,128)S(1)}, u32[]{:S(2)}) copy-start(f32[3,1,512]{2,0,1:T(4,128)S(1)} %copy.283) | copy-start | bytes 18436
  21.6 18.8 %copy-start.47 = (f32[3,1,512]{2,0,1:T(4,128)}, f32[3,1,512]{2,0,1:T(4,128)S(1)}, u32[]{:S(2)}) copy-start(f32[3,1,512]{2,0,1:T(4,128)S(1)} %copy.284) | copy-start | bytes 18436
  33.7 6.7 copy-start.16
  69.9 6.4 copy-start.25
  71.3 7.9 %collective-permute-start.2 = (bf16[2,9,512]{2,1,0:T(8,128)(2,1)S(1)}, bf16[2,9,512]{2,1,0:T(8,128)(2,1)S(1)}, u32[]{:S(2)}, u32[]{:S(2)}) collective-permute-start(bf16[2,9,512]{2,1,0:T(8,128)(2,1)S(1)} %get-tuple-element.743), channel_id=1, source_target_pairs={{0,1},{1,2},{2,3},{3,4},{4,5},{5,6},{6,7},{7,8},{8,9},{9,10},{10,1... | collective-permute-start | bytes 55304 | tf_op jit(solution)/shard_map/ppermute | solution.py:34
  74.7 5.8 collective-permute-start.3
  91.5 3.5 copy-start.26
  124.8 68.0 %all-gather.8.cloned.1.call-start = ((), (), s32[]{:S(2)}) async-start(), calls=%async_computation.5 | async-start | bytes 3145728 | tf_op jit(solution)/shard_map/all_gather | solution.py:226
  126.7 197.1 %all-reduce.11.cloned.1.call-start = ((), (), s32[]{:S(2)}) async-start(), calls=%async_computation.8 | async-start | bytes 8388608 | tf_op jit(solution)/shard_map/psum | solution.py:236
  192.8 5.3 copy-start.32
  192.8 5.3 copy-start.73
  192.8 6.5 copy-start.76
  199.3 7.9 %copy-start.72 = (bf16[2048,512]{0,1:T(8,128)(2,1)S(1)}, bf16[2048,512]{0,1:T(8,128)(2,1)}, u32[]{:S(2)}) copy-start(bf16[2048,512]{0,1:T(8,128)(2,1)} %all-gather.6.cloned.1.call-done) | copy-start | bytes 6291460
  212.1 167.3 %reduce-scatter.5.cloned.1.call-start = ((), (), s32[]{:S(2)}) async-start(), calls=%async_computation.6 | async-start | bytes 6291456 | tf_op jit(solution)/shard_map/reduce_scatter | solution.py:233
  219.2 216.6 %reduce-scatter.3.cloned.1.call-start = ((), (), s32[]{:S(2)}) async-start(), calls=%async_computation.4 | async-start | bytes 6291456 | tf_op jit(solution)/shard_map/reduce_scatter | solution.py:230
  226.1 35.8 %copy-start.65 = (f32[1024]{0:T(1024)S(1)}, f32[1024]{0:T(1024)}, u32[]{:S(2)}) copy-start(f32[1024]{0:T(1024)} %param.51) | copy-start | bytes 12292
  226.1 35.8 %copy-start.66 = (f32[1024]{0:T(1024)S(1)}, f32[1024]{0:T(1024)}, u32[]{:S(2)}) copy-start(f32[1024]{0:T(1024)} %param.49) | copy-start | bytes 12292
  226.1 35.8 %copy-start.67 = (f32[1024]{0:T(1024)S(1)}, f32[1024]{0:T(1024)}, u32[]{:S(2)}) copy-start(f32[1024]{0:T(1024)} %param.50) | copy-start | bytes 12292
  226.1 498.1 %all-reduce.9.cloned.1.call-start = ((), (), s32[]{:S(2)}) async-start(), calls=%async_computation.7 | async-start | bytes 8388608 | tf_op jit(solution)/shard_map/psum | solution.py:337
  227.7 212.8 %copy-start.20 = (bf16[1024,512]{0,1:T(8,128)(2,1)}, bf16[1024,512]{0,1:T(8,128)(2,1)S(1)}, u32[]{:S(2)}) copy-start(bf16[1024,512]{0,1:T(8,128)(2,1)S(1)} %copy.188) | copy-start | bytes 3145732
  338.2 97.6 %copy-start.64 = (f32[1,512]{1,0:T(1,128)S(1)}, f32[1,512]{1,0:T(1,128)}, u32[]{:S(2)}) copy-start(f32[1,512]{1,0:T(1,128)} %get-tuple-element.748) | copy-start | bytes 6148
  456.8 5.3 slice-start
  458.3 3.8 slice-start.1
  480.2 5.3 slice-start
  481.6 3.8 slice-start.1
  499.5 3.1 copy-start.6
  504.8 3.3 copy-start.9
  510.4 6.8 copy-start.30
  514.5 10.3 %collective-permute-start.4 = (f32[2,9,512]{2,1,0:T(8,128)S(1)}, f32[2,9,512]{2,1,0:T(8,128)S(1)}, u32[]{:S(2)}, u32[]{:S(2)}) collective-permute-start(f32[2,9,512]{2,1,0:T(8,128)S(1)} %get-tuple-element.736), channel_id=1, source_target_pairs={{0,1},{1,2},{2,3},{3,4},{4,5},{5,6},{6,7},{7,8},{8,9},{9,10},{10,1... | collective-permute-start | bytes 110600 | tf_op jit(solution)/shard_map/ppermute | solution.py:34
  517.4 4.9 copy-start.31
  522.2 15.4 %copy-start.19 = (f32[1024,512]{1,0:T(8,128)S(1)}, f32[1024,512]{1,0:T(8,128)}, u32[]{:S(2)}) copy-start(f32[1024,512]{1,0:T(8,128)} %copy.178) | copy-start | bytes 6291460
  523.5 6.8 collective-permute-start.5
  532.7 3.0 copy-start.2
  545.5 3.1 copy-start.24
  552.4 5.2 copy-start.10
  556.2 3.5 copy-start.23
  562.8 4.6 copy-start.34
  562.8 4.6 copy-start.35
  563.4 15.5 %collective-permute-start.6 = (f32[1,512]{0,1:T(8,128)S(1)}, f32[1,512]{0,1:T(8,128)}, u32[]{:S(2)}, u32[]{:S(2)}) collective-permute-start(f32[1,512]{0,1:T(8,128)S(1)} %get-tuple-element.730), channel_id=1, source_target_pairs={{0,1},{1,2},{2,3},{3,4},{4,5},{5,6},{6,7},{7,8},{8,9},{9,10},{10,1... | collective-permute-start | bytes 6152 | tf_op jit(solution)/shard_map/ppermute | solution.py:34
  566.1 15.1 %collective-permute-start.7 = (f32[1,512]{0,1:T(8,128)}, f32[1,512]{0,1:T(8,128)}, u32[]{:S(2)}, u32[]{:S(2)}) collective-permute-start(f32[1,512]{0,1:T(8,128)} %get-tuple-element.729), channel_id=1, source_target_pairs={{1,0},{2,1},{3,2},{4,3},{5,4},{6,5},{7,6},{8,7},{9,8},{10,9},{11,1... | collective-permute-start | bytes 6152 | tf_op jit(solution)/shard_map/ppermute | solution.py:35
  578.9 4.6 copy-start.42
  578.9 4.6 copy-start.52
  580.2 3.4 copy-start.1
  581.2 3.0 copy-start.50
  586.0 4.4 copy-start.63
  588.0 47.1 %copy-start.40 = (f32[17,512]{1,0:T(8,128)S(1)}, f32[17,512]{1,0:T(8,128)}, u32[]{:S(2)}) copy-start(f32[17,512]{1,0:T(8,128)} %param.40) | copy-start | bytes 104452
  588.0 47.1 %copy-start.53 = (f32[17,512]{1,0:T(8,128)S(1)}, f32[17,512]{1,0:T(8,128)}, u32[]{:S(2)}) copy-start(f32[17,512]{1,0:T(8,128)} %param.43) | copy-start | bytes 104452
  588.0 47.1 %copy-start.54 = (f32[17,512]{1,0:T(8,128)S(1)}, f32[17,512]{1,0:T(8,128)}, u32[]{:S(2)}) copy-start(f32[17,512]{1,0:T(8,128)} %param.41) | copy-start | bytes 104452
  588.0 47.1 %copy-start.55 = (f32[17,512]{1,0:T(8,128)S(1)}, f32[17,512]{1,0:T(8,128)}, u32[]{:S(2)}) copy-start(f32[17,512]{1,0:T(8,128)} %param.42) | copy-start | bytes 104452
  635.8 92.2 %copy-start.33 = (f32[2,128,512]{2,1,0:T(8,128)S(1)}, f32[2,128,512]{2,1,0:T(8,128)}, u32[]{:S(2)}) copy-start(f32[2,128,512]{2,1,0:T(8,128)} %param.36) | copy-start | bytes 1572868
  635.8 92.2 %copy-start.36 = (f32[2,128,512]{2,1,0:T(8,128)S(1)}, f32[2,128,512]{2,1,0:T(8,128)}, u32[]{:S(2)}) copy-start(f32[2,128,512]{2,1,0:T(8,128)} %param.39) | copy-start | bytes 1572868
  635.8 92.2 %copy-start.37 = (f32[2,128,512]{2,1,0:T(8,128)S(1)}, f32[2,128,512]{2,1,0:T(8,128)}, u32[]{:S(2)}) copy-start(f32[2,128,512]{2,1,0:T(8,128)} %param.38) | copy-start | bytes 1572868
  635.8 92.2 %copy-start.38 = (f32[2,128,512]{2,1,0:T(8,128)S(1)}, f32[2,128,512]{2,1,0:T(8,128)}, u32[]{:S(2)}) copy-start(f32[2,128,512]{2,1,0:T(8,128)} %param.37) | copy-start | bytes 1572868
  (39 other events, 70.2 us)
Sparse Core Ops, SparseCore 0:
  10.8 54.3 all-gather.3
  124.9 32.5 all-gather.5
  159.7 33.1 all-gather.7
  212.2 111.5 all-reduce.10
  326.1 53.2 reduce-scatter.4
  381.5 54.2 reduce-scatter.2
  579.0 145.2 all-reduce.8
where the time goes:
time: 746 us; the launch traced here: 738 us
  waiting for transfers between devices  310 us (42%)
  local copies, waits for them, and re-layouts  107 us (14%)
  matrix products  106 us (14%)
  other arithmetic  82.2 us (11%)
  blocking collectives  78.6 us (11%)
  starting transfers between devices  20 us (3%)
  loops' own time  18.5 us (2%)
  between operations  15.5 us (2%)
    psum x1, waiting for transfers between devices, shards(): matrix_sum, small_sum = lax.psum((matrix_grads, small_grad), ('seq', 'mlp'))  88.4 us
    psum x1, waiting for transfers between devices, shards(): weight_sum, bias_sum = lax.psum((weight_parts, bias_part), 'seq')  61.3 us
    reduce_scatter x1, waiting for transfers between devices, shards(): lax.psum_scatter(contract_cols(active, local_weights[1]), 'mlp', scatter_...  53.5 us
    psum x1, blocking collectives, shards(): matrix_sum, small_sum = lax.psum((matrix_grads, small_grad), ('seq', 'mlp'))  44.7 us
    reduce_scatter x1, waiting for transfers between devices, shards(): lax.psum_scatter(contract_cols(hidden_grad, local_weights[0]), 'mlp', sca...  41.1 us
    psum x1, blocking collectives, shards(): weight_sum, bias_sum = lax.psum((weight_parts, bias_part), 'seq')  33.9 us
    all_gather x1, waiting for transfers between devices, shards(): gathered_rows = lax.all_gather(second, 'mlp', axis=0, tiled=True)  26.4 us
    dot_general x6, matrix products, contract_cols(): lax.dot_general(left, right, (((1,), (1,)), ((), ())), preferred_element_...  23.4 us
  transfers between devices with their start and end apart: 15, of which 10 were waited for; matrix products, arithmetic and copies ran while one was open for 17% of the time, Pallas kernels for 0%

commit v1 on v0

v1 whole, which is shorter than its diff:
```python
import functools

import jax
import jax.numpy as jnp
from jax import lax
from jax.experimental import pallas as pl
from jax.experimental.pallas import tpu as pltpu
from jax.sharding import Mesh
from jax.sharding import PartitionSpec as P

HEADS = 4
HEAD = 128
HALF = 9
TILE = 128
TILES = 16
CAP = 2
STEP = 7
NSMALL = 17
NSMALL_ROWS = 32

NORM_EPS = 1e-05
MASKED = -1e30
BETA_ONE = 0.9
BETA_TWO = 0.999
ADAM_EPS = 1e-08
MATRIX_RATE = 0.03
MATRIX_DECAY = 0.05
SMALL_RATE = 0.3
AVERAGE_RATE = 0.8

F32 = jnp.float32
BF16 = jnp.bfloat16

KEY_RIM = 32
ROW_RIM = 16
QUERY_BLOCK = 96
KEY_SPAN = 128
FF_BLOCK = 512
FF_ROWS = 3
CHUNK = 128
NARROW = 64
SCALE = HEAD ** (-0.5)
GROUPS = ("z", "y", "core", "mlp")
SEATS = ("z", "y", "core")


def adamw(weight, grad, first, second, average, rate, decay):
    first_new = BETA_ONE * first + (1.0 - BETA_ONE) * grad
    second_new = BETA_TWO * second + (1.0 - BETA_TWO) * grad * grad
    scaled = second_new * (1.0 / (1.0 - BETA_TWO**STEP))
    root = scaled * lax.rsqrt(scaled)
    ratio = first_new * (1.0 / (1.0 - BETA_ONE**STEP)) / (root + ADAM_EPS)
    weight_new = weight - rate * (ratio + decay * weight)
    average_new = AVERAGE_RATE * average + (1.0 - AVERAGE_RATE) * weight_new
    return (weight_new, first_new, second_new, average_new)


def dot_nn(left, right):
    return lax.dot_general(left, right, (((1,), (0,)), ((), ())), preferred_element_type=F32)


def dot_nt(left, right):
    return lax.dot_general(left, right, (((1,), (1,)), ((), ())), preferred_element_type=F32)


def dot_tn(left, right):
    return lax.dot_general(left, right, (((0,), (0,)), ((), ())), preferred_element_type=F32)


def normal_parts(values):
    mean = jnp.mean(values, axis=-1, keepdims=True)
    centred = values - mean
    spread = jnp.mean(centred * centred, axis=-1, keepdims=True)
    inverse = lax.rsqrt(spread + NORM_EPS)
    return (centred * inverse, inverse)


def normal_back(unit, inverse, grad, gain):
    inner = grad * gain
    return inverse * (
        inner
        - jnp.mean(inner, axis=-1, keepdims=True)
        - unit * jnp.mean(inner * unit, axis=-1, keepdims=True)
    )


def fold_rows(values):
    return jnp.sum(values.reshape(-1, 8, values.shape[-1]), axis=0)


def conv_kernel(
    before, frames, after, cotangent, cols, small,
    conv_out, first_out, wide_out, cot_out, grad_rows_out, grad_t_out, rows,
):
    local = frames.shape[0]
    wide = local + 2 * KEY_RIM
    gain = small[0:1, :]
    bias = small[1:2, :]

    def norm_to(piece, start):
        unit, _ = normal_parts(piece.astype(F32))
        low = (unit * gain + bias).astype(BF16)
        first_out[pl.ds(start, piece.shape[0]), :] = low
        rows[pl.ds(start + 8, piece.shape[0]), :] = low.astype(F32)

    zero = jnp.zeros((8, rows.shape[1]), F32)
    rows[0:8, :] = zero
    rows[wide + 8 : wide + 16, :] = zero
    norm_to(before[0:KEY_RIM, :], 0)
    norm_to(after[0:KEY_RIM, :], KEY_RIM + local)

    def norm_step(step, carry):
        start = pl.multiple_of(step * CHUNK, CHUNK)
        norm_to(frames[pl.ds(start, CHUNK), :], pl.multiple_of(start + KEY_RIM, 32))
        return carry

    lax.fori_loop(0, local // CHUNK, norm_step, 0, unroll=2)
    wide_out[0:ROW_RIM, :] = before[KEY_RIM - ROW_RIM : KEY_RIM, :]
    wide_out[ROW_RIM : ROW_RIM + local, :] = frames[...]
    wide_out[ROW_RIM + local :, :] = after[0:ROW_RIM, :]
    cot_out[0:ROW_RIM, :] = before[KEY_RIM:, :]
    cot_out[ROW_RIM : ROW_RIM + local, :] = cotangent[...]
    cot_out[ROW_RIM + local :, :] = after[KEY_RIM:, :]

    def mask_step(step, carry):
        span = pl.ds(pl.multiple_of(step * QUERY_BLOCK, 32), QUERY_BLOCK)
        flags = cols[pl.ds(pl.multiple_of(step * QUERY_BLOCK + ROW_RIM, 16), QUERY_BLOCK), 2:3]
        grad_rows_out[span, :] = (cot_out[span, :].astype(F32) * flags).astype(BF16)
        return carry

    lax.fori_loop(0, cot_out.shape[0] // QUERY_BLOCK, mask_step, 0)
    grad_t_out[...] = grad_rows_out[ROW_RIM : ROW_RIM + local, :].T

    def conv_step(step, carry):
        start = pl.multiple_of(step * NARROW, NARROW)
        window = rows[pl.ds(start, NARROW + 16), :]
        flags = cols[pl.ds(start, NARROW), :]
        past = pltpu.roll(window, 1, 0)[8 : 8 + NARROW] * flags[:, 0:1]
        here = window[8 : 8 + NARROW]
        later = pltpu.roll(window, NARROW + 15, 0)[8 : 8 + NARROW] * flags[:, 1:2]
        for c in range(3):
            row = 8 + 3 * c
            mixed = (
                small[row : row + 1, :] * past
                + small[row + 1 : row + 2, :] * here
                + small[row + 2 : row + 3, :] * later
            )
            conv_out[c, pl.ds(start, NARROW), :] = mixed.astype(BF16)
        return carry

    lax.fori_loop(0, wide // NARROW, conv_step, 0)


def edges_kernel(tiles, head, tail, cot_head, cot_tail, first_out, second_out, up_out, down_out):
    first_out[...] = tiles[0].astype(BF16)
    second_out[...] = tiles[1].astype(BF16)
    up_out[0:KEY_RIM, :] = tail[...]
    up_out[KEY_RIM:, :] = cot_tail[...]
    down_out[0:KEY_RIM, :] = head[...]
    down_out[KEY_RIM:, :] = cot_head[...]


def matrices_kernel(master, low_out):
    size = master.shape[1]
    rows = pl.ds(pl.multiple_of(pl.program_id(0) * size, size), size)
    low_out[:, rows, :] = master[...].astype(BF16)


def half_kernel(place, master, bias, half_out):
    step = pl.program_id(0)
    size, units = master.shape[1:]
    half_out[pl.ds(pl.multiple_of(step * size, size), size), :] = master[0].astype(BF16)

    @pl.when(step == 0)
    def _():
        width = half_out.shape[0] - 16
        half_out[width:, :] = jnp.broadcast_to(bias[...], (16, units)).astype(BF16)


def tables_kernel(place, lengths, cols_out, codes_out):
    wide = cols_out.shape[0]
    blocks = (wide - KEY_SPAN) // QUERY_BLOCK + 1
    local = wide - 2 * KEY_RIM
    anchor = place[4] * local
    chunks = -(-wide // 128)
    height = -(-max(chunks, blocks) // 8) * 8
    row = lax.broadcasted_iota(jnp.int32, (height, 128), 0)
    lane = lax.broadcasted_iota(jnp.int32, (height, 128), 1)
    start = anchor - KEY_RIM + lane
    frame = start + row * 128
    key = start + row * QUERY_BLOCK
    zero = jnp.zeros((height, 128), jnp.int32)

    def count(j, carry):
        end, video, key_video, starts, stops = carry
        end = end + lengths[j]
        return (
            end,
            video + (frame >= end).astype(jnp.int32),
            key_video + (key >= end).astype(jnp.int32),
            starts + (frame == end).astype(jnp.int32),
            stops + (frame + 1 == end).astype(jnp.int32),
        )

    last, video, key_video, starts, stops = lax.fori_loop(
        0, lengths.shape[0], count, (jnp.int32(0), zero, zero, zero, zero)
    )
    valid = (frame >= 0) & (frame < last)
    key_valid = (key >= 0) & (key < last)
    prev = valid & (frame >= 1) & (starts == 0)
    after = valid & (frame + 1 < last) & (stops == 0)
    codes_out[...] = jnp.where(key_valid, key_video, -2).astype(F32)
    values = [prev.astype(F32), after.astype(F32), valid.astype(F32)]
    values.append(jnp.where(valid, video, -1).astype(F32))
    for c in range(chunks):
        size = min(128, wide - c * 128)
        columns = jnp.concatenate([value[c : c + 1] for value in values] * 2, axis=0).T
        cols_out[c * 128 : c * 128 + size, :] = columns[0:size]


def slots_of(owners):
    found = [owners[i] for i in range(TILES)]
    return [
        (found[i], sum([jnp.where(found[j] == found[i], 1, 0) for j in range(i)], jnp.int32(0)))
        for i in range(TILES)
    ]


def head_lanes(h):
    return slice(h * HEAD, (h + 1) * HEAD)


def head_rows(h):
    return slice(h * QUERY_BLOCK, (h + 1) * QUERY_BLOCK)


def attend_kernel(
    place, owners, *refs
):
    tiles, refs = (refs[:6], refs[6:])
    conv, cols, codes, small, *refs = refs
    weights_out, query_out, key_out, value_out, probs_out, mixed_out = refs
    rows, width = mixed_out.shape
    wide = conv.shape[1]
    depth = tiles[0].shape[0]
    for i, (owner, slot) in enumerate(slots_of(owners)):
        spot = pl.ds(i * TILE, TILE)
        core_away = (owner + place[2]) % 2
        y_away = (owner // 2 + place[1]) % 2
        z_away = place_of(place[0] ^ (owner // 4), depth)
        for r, source in enumerate(tiles[:4]):

            @pl.when((slot == 0) & (core_away * 2 + y_away == r))
            def _(source=source):
                weights_out[spot, :] = source[z_away]

        for r, source in enumerate(tiles[4:]):

            @pl.when((slot == 1) & (core_away == r))
            def _(source=source):
                weights_out[spot, :] = source[z_away, y_away]

    def matrix(c):
        return weights_out[c * width : (c + 1) * width, :]

    part = wide // 2
    for j in range(2):
        span = pl.ds(j * part, part)
        query_out[span, :] = (dot_nn(conv[0, span, :], matrix(0)) + small[4:5, :]).astype(BF16)
        key_out[span, :] = dot_nn(conv[1, span, :], matrix(1)).astype(BF16)
        value_out[span, :] = (dot_nn(conv[2, span, :], matrix(2)) + small[5:6, :]).astype(BF16)

    query_index = lax.broadcasted_iota(jnp.int32, (QUERY_BLOCK, KEY_SPAN), 0)
    key_index = lax.broadcasted_iota(jnp.int32, (QUERY_BLOCK, KEY_SPAN), 1)
    offset = query_index - key_index + (KEY_RIM - ROW_RIM)
    band = jnp.abs(offset) <= HALF
    same = offset == 0

    for step in range(rows // QUERY_BLOCK):
        start = step * QUERY_BLOCK
        query_start = start + ROW_RIM
        query_code = cols[pl.ds(query_start, QUERY_BLOCK), 3:4]
        key_code = codes[step : step + 1, :]
        allowed = band & (same | (query_code == key_code))
        scores = [
            jnp.where(
                allowed,
                dot_nt(
                    query_out[pl.ds(query_start, QUERY_BLOCK), head_lanes(h)],
                    key_out[pl.ds(start, KEY_SPAN), head_lanes(h)],
                )
                * SCALE,
                MASKED,
            )
            for h in range(HEADS)
        ]
        masked = jnp.concatenate(scores, axis=0)
        top = jnp.max(masked, axis=-1, keepdims=True)
        expo = jnp.exp(masked - top)
        probs = expo / jnp.sum(expo, axis=-1, keepdims=True)
        probs_out[step] = probs
        low = probs.astype(BF16)
        for h in range(HEADS):
            values = value_out[pl.ds(start, KEY_SPAN), head_lanes(h)]
            mixed = dot_nn(low[head_rows(h)], values)
            mixed_out[pl.ds(start, QUERY_BLOCK), head_lanes(h)] = mixed.astype(BF16)


def middle_kernel(mixed, weights, wide_rows, cols, small, middle_out, second_out, second_t_out):
    rows, width = wide_rows.shape
    part = rows // 3
    for j in range(3):
        span = pl.ds(j * part, part)
        branch = dot_nn(mixed[span, :], weights[3 * width : 4 * width, :]) + small[6:7, :]
        valid = cols[pl.ds(ROW_RIM + j * part, part), 2:3]
        middle = wide_rows[span, :].astype(F32) + valid * branch
        middle_out[span, :] = middle
        unit, _ = normal_parts(middle)
        second_out[span, :] = (unit * small[2:3, :] + small[3:4, :]).astype(BF16)
    second_t_out[...] = second_out[ROW_RIM : rows - ROW_RIM, :].T


def feed_kernel(first_call, *refs):
    place, first_matrix, second_matrix, hidden_bias, second, grad_rows, second_t, grad_t, *refs = refs
    if not first_call:
        result_in, second_grad_in, *refs = refs
    keep_out, send_out, bias_out, result, second_grad, up, down, active, hidden_grad = refs
    ways, _, units = first_matrix.shape
    width, block = up.shape
    per_piece = units // block
    rows = second.shape[0]
    local = rows - 2 * ROW_RIM
    own = slice(ROW_RIM, ROW_RIM + local)
    even = place[2] == 0
    straight = even if first_call else place[2] >= 0
    slabs, height = keep_out.shape[2:4]
    depth = slabs // 2
    if first_call:
        result[...] = jnp.zeros(result.shape, F32)
        second_grad[...] = jnp.zeros(second_grad.shape, F32)
    else:
        result[...] = result_in[...]
        second_grad[...] = second_grad_in[...]

    def block_step(step, carry):
        piece = step // per_piece
        lanes = pl.ds(pl.multiple_of((step % per_piece) * block, block), block)

        @pl.when(straight)
        def _():
            up[...] = first_matrix[piece, 0:width, lanes]
            down[...] = second_matrix[piece, 0:width, lanes]

        @pl.when(jnp.logical_not(straight))
        def _():
            up[...] = second_matrix[piece, 0:width, lanes]
            down[...] = first_matrix[piece, 0:width, lanes]

        if first_call:
            bias = first_matrix[piece, width : width + 16, lanes][0:1].astype(F32)
        else:
            bias = hidden_bias[0:1, lanes].astype(BF16).astype(F32)
        part = rows // FF_ROWS
        for j in range(FF_ROWS):
            span = pl.ds(j * part, part)
            value = dot_nn(second[span, :], up[...]) + bias
            active_grad = dot_nn(grad_rows[span, :], down[...])
            phi = 0.5 * (1.0 + lax.erf(value * (0.5**0.5)))
            density = jnp.exp(value * value * -0.5) * 0.3989422804014327
            active[span, :] = (value * phi).astype(BF16)
            hidden_grad[span, :] = (active_grad * (phi + value * density)).astype(BF16)
        result[...] += dot_nt(active[...], down[...])
        second_grad[...] += dot_nt(hidden_grad[...], up[...])
        up_grad = dot_nn(second_t[...], hidden_grad[own, :])
        down_grad = dot_nn(grad_t[...], active[own, :])
        bias_out[piece, :, lanes] = jnp.sum(
            hidden_grad[own, :].astype(F32), axis=0, keepdims=True
        )
        kept = jnp.where(even, up_grad, down_grad).astype(BF16)
        sent = jnp.where(even, down_grad, up_grad).astype(BF16)
        for slab in range(slabs):
            target = (slab // depth + place[1]) % 2 * depth + (slab % depth - place[0] + depth) % depth
            for half in range(2):
                start = (2 * slab + half) * height
                keep_out[piece, half, target, :, lanes] = kept[start : start + height]
                send_out[piece, half, target, :, lanes] = sent[start : start + height]
        return carry

    lax.fori_loop(0, ways * per_piece, block_step, 0)


def update_kernel(core_away, y_away, place, column, *refs):
    states, outs = refs[:4], refs[-8:-4]
    came, left, came_sems, left_sems = refs[-4:]
    depth, height, _ = column.shape
    matrix = (place[2] + core_away) % 2
    first_row = (place[1] + y_away) % 2 * (depth * height)

    def rows(j):
        return pl.ds(pl.multiple_of(first_row + j * height, height), height)

    def fetch(j, k):
        return pltpu.make_async_copy(
            states[k].at[matrix, rows(j)], came.at[j, k], came_sems.at[j, k]
        )

    def store(j, k):
        return pltpu.make_async_copy(
            left.at[j, k], outs[k].at[matrix, rows(j)], left_sems.at[j, k]
        )

    def start(j, carry):
        for k in range(4):
            fetch(j, k).start()
        return carry

    def update(j, carry):
        for k in range(4):
            fetch(j, k).wait()
        grad = column[(place[0] - j + depth) % depth].astype(F32)
        new = adamw(came[j, 0], grad, came[j, 1], came[j, 2], came[j, 3], MATRIX_RATE, MATRIX_DECAY)
        for k, value in enumerate(new):
            left[j, k] = value
            store(j, k).start()
        return carry

    def finish(j, carry):
        for k in range(4):
            store(j, k).wait()
        return carry

    lax.fori_loop(0, depth, start, 0)
    lax.fori_loop(0, depth, update, 0)
    lax.fori_loop(0, depth, finish, 0)


def middle_back_kernel(
    middle, cot, grad_rows, result_sum, second_sum, mixed, weights, cols, small,
    output_out, middle_grad_out, mixed_grad_out, out_grad_out, rows_out, branch,
):
    rows, width = middle.shape
    local = rows - 2 * ROW_RIM
    own = slice(ROW_RIM, ROW_RIM + local)
    rows_out[...] = jnp.zeros(rows_out.shape, F32)

    def finish(start, size, own_rows):
        span = pl.ds(start, size)
        here = middle[span, :]
        valid = cols[pl.ds(start + ROW_RIM, size), 2:3]
        unit, inverse = normal_parts(here)
        incoming = second_sum[span, :]
        back = normal_back(unit, inverse, incoming, small[2:3, :])
        middle_grad = cot[span, :].astype(F32) + back
        branch_grad = (valid * middle_grad).astype(BF16)
        branch[span, :] = branch_grad
        if own_rows:
            target = pl.ds(start - ROW_RIM, size)
            result = result_sum[span, :] + small[7:8, :]
            output_out[target, :] = (here + valid * result).astype(BF16)
            middle_grad_out[target, :] = middle_grad
            rows_out[0:8, :] += fold_rows(incoming * unit)
            rows_out[8:16, :] += fold_rows(incoming)
            rows_out[16:24, :] += fold_rows(branch_grad.astype(F32))
            rows_out[24:32, :] += fold_rows(grad_rows[span, :].astype(F32))

    finish(0, ROW_RIM, False)
    finish(ROW_RIM + local, ROW_RIM, False)

    def finish_step(j, carry):
        finish(pl.multiple_of(j * CHUNK + ROW_RIM, 16), CHUNK, True)
        return carry

    lax.fori_loop(0, local // CHUNK, finish_step, 0)
    mixed_grad_out[...] = dot_nt(branch[...], weights[3 * width : 4 * width, :]).astype(BF16)
    out_grad_out[...] = dot_tn(mixed[own, :], branch[own, :]).astype(BF16)


def scores_back_kernel(
    first_head, place, owners, query, keys, values, probs, mixed_grad, conv, out_grad,
    query_grad, key_grad, value_grad, keep_out, send_out,
    key_acc, value_acc, grads,
):
    rows, width = mixed_grad.shape
    columns = key_acc.shape[1]
    heads = columns // HEAD
    local = rows - 2 * ROW_RIM
    own = slice(ROW_RIM, ROW_RIM + local)
    wide_own = slice(KEY_RIM, KEY_RIM + local)
    key_acc[...] = jnp.zeros(key_acc.shape, F32)
    value_acc[...] = jnp.zeros(value_acc.shape, F32)
    keep_out[...] = jnp.zeros(keep_out.shape, BF16)
    send_out[...] = jnp.zeros(send_out.shape, BF16)

    for step in range(rows // QUERY_BLOCK):
        start = step * QUERY_BLOCK
        here = pl.ds(start, QUERY_BLOCK)
        span = pl.ds(start, KEY_SPAN)
        quest = pl.ds(start + ROW_RIM, QUERY_BLOCK)
        first_row = first_head * QUERY_BLOCK
        probs_here = probs[step, first_row : first_row + heads * QUERY_BLOCK, :]
        prob_grad = jnp.concatenate(
            [
                dot_nt(mixed_grad[here, head_lanes(h)], values[span, head_lanes(h)])
                for h in range(first_head, first_head + heads)
            ],
            axis=0,
        )
        inner = jnp.sum(probs_here * prob_grad, axis=-1, keepdims=True)
        score_grad = (probs_here * (prob_grad - inner)).astype(BF16)
        low = probs_here.astype(BF16)
        for h in range(heads):
            lanes, whole_lanes = head_lanes(h), head_lanes(first_head + h)
            score = score_grad[head_rows(h)]
            query_grad[here, lanes] = (dot_nn(score, keys[span, whole_lanes]) * SCALE).astype(BF16)
            key_acc[span, lanes] += dot_tn(score, query[quest, whole_lanes])
            value_acc[span, lanes] += dot_tn(low[head_rows(h)], mixed_grad[here, whole_lanes])

    inside = slice(ROW_RIM, ROW_RIM + rows)
    key_grad[...] = (key_acc[inside, :] * SCALE).astype(BF16)
    value_grad[...] = value_acc[inside, :].astype(BF16)

    for c, grad in enumerate((query_grad, key_grad, value_grad)):
        grads[c * width : (c + 1) * width, :] = dot_tn(conv[c, wide_own, :], grad[own, :]).astype(BF16)
    grads[3 * width :, :] = out_grad[:, first_head * HEAD : first_head * HEAD + columns]

    share = keep_out.shape[1]
    parts = TILE // share
    ways = CAP * parts
    depth = keep_out.shape[0] // (2 * ways)
    for i, (owner, slot) in enumerate(slots_of(owners)):
        away = (owner + place[2]) % 2
        y_away = (owner // 2 + place[1]) % 2
        z_away = (owner // 4) ^ place[0]
        for part in range(parts):
            way = (place[3] - slot * parts - part + ways) % ways
            target = (way * 2 + y_away) * depth + z_away
            here = pl.ds(i * TILE + part * share, share)

            @pl.when(away == 0)
            def _(target=target, here=here):
                keep_out[target] = grads[here, :]

            @pl.when(away == 1)
            def _(target=target, here=here):
                send_out[target] = grads[here, :]


def conv_grad_kernel(*refs):
    weights, conv_grad = refs[-2:]
    rows, columns = refs[0].shape
    width = weights.shape[1]
    part = rows // 2
    for j in range(2):
        span = pl.ds(j * part, part)
        for c in range(3):
            matrix = slice(c * width, (c + 1) * width)
            conv_grad[c, span, :] = dot_nt(refs[c][span, :], weights[matrix, 0:columns]) + dot_nt(
                refs[3 + c][span, :], weights[matrix, columns:]
            )


def conv_back_kernel(
    place, query_grad_0, value_grad_0, query_grad_1, value_grad_1, conv_grad, first, frames, feed_rows, near_bias, far_bias, cols, small,
    incoming_out, totals_out, sums,
):
    rows, columns = query_grad_0.shape
    width = frames.shape[1]
    local = rows - 2 * ROW_RIM
    sums[...] = jnp.zeros(sums.shape, F32)

    def conv_step(step, carry):
        start = pl.multiple_of(step * CHUNK, CHUNK)
        window = CHUNK + 16
        flags = cols[pl.ds(pl.multiple_of(start + KEY_RIM - 8, 8), window), :]
        span = pl.ds(pl.multiple_of(start + ROW_RIM - 8, 8), window)
        grads = [conv_grad[c, span, :] for c in range(3)]
        past = sum(small[8 + 3 * c : 9 + 3 * c, :] * grads[c] for c in range(3)) * flags[:, 0:1]
        later = sum(small[10 + 3 * c : 11 + 3 * c, :] * grads[c] for c in range(3)) * flags[:, 1:2]
        middle = slice(8, 8 + CHUNK)
        incoming = (
            sum(small[9 + 3 * c : 10 + 3 * c, :] * grads[c][middle] for c in range(3))
            + pltpu.roll(past, window - 1, 0)[middle]
            + pltpu.roll(later, 1, 0)[middle]
        )
        low = first[pl.ds(pl.multiple_of(start + KEY_RIM - 16, 16), window + 16), :].astype(F32)
        inner = slice(16, 16 + CHUNK)
        low_here = low[inner]
        low_past = pltpu.roll(low, 1, 0)[inner] * flags[middle, 0:1]
        low_later = pltpu.roll(low, window + 15, 0)[inner] * flags[middle, 1:2]
        for c in range(3):
            grad = grads[c][middle]
            base = 8 * (8 + 3 * c)
            sums[base : base + 8, :] += fold_rows(grad * low_past)
            sums[base + 8 : base + 16, :] += fold_rows(grad * low_here)
            sums[base + 16 : base + 24, :] += fold_rows(grad * low_later)
        unit, _ = normal_parts(frames[pl.ds(start, CHUNK), :].astype(F32))
        incoming_out[pl.ds(start, CHUNK), :] = incoming
        sums[0:8, :] += fold_rows(incoming * unit)
        sums[8:16, :] += fold_rows(incoming)
        here = pl.ds(pl.multiple_of(start + ROW_RIM, 16), CHUNK)
        for lanes, query_grad, value_grad in (
            (slice(0, columns), query_grad_0, value_grad_0),
            (slice(columns, width), query_grad_1, value_grad_1),
        ):
            sums[32:40, lanes] += fold_rows(query_grad[here, :].astype(F32))
            sums[40:48, lanes] += fold_rows(value_grad[here, :].astype(F32))
        return carry

    lax.fori_loop(0, local // CHUNK, conv_step, 0)
    sums[16:32, :] = feed_rows[0:16, :]
    sums[48:64, :] = feed_rows[16:32, :]
    totals_out[0:24, :] = jnp.sum(sums[...].reshape(24, 8, width), axis=1)
    totals_out[24:, :] = jnp.zeros((totals_out.shape[0] - 24, width), F32)
    units = near_bias.shape[2]
    ways = 1 + far_bias.shape[0]
    chunk = min(units, width)
    for piece in range(ways):
        source = near_bias if piece == 0 else far_bias
        for j in range(units // chunk):
            offset = (place[3] - piece + ways) % ways * units + j * chunk
            lanes = pl.ds(pl.multiple_of(offset % width, chunk), chunk)
            totals_out[pl.ds(24 + offset // width, 1), lanes] = source[
                max(piece - 1, 0), :, j * chunk : (j + 1) * chunk
            ]


def add_kernel(inputs, kinds, *refs):
    for out, parts in zip(refs[-len(kinds) :], inputs):
        count = out.shape[0]

        def step(j, carry, out=out, parts=parts, count=count):
            total = 0.0
            for index, start, *stride in parts:
                run = stride[0] // 2 if stride else count
                total = total + refs[index][start + j // run * 2 * run + j % run].astype(F32)
            out[j] = total.astype(out.dtype)
            return carry

        lax.fori_loop(0, count, step, 0)


def add_into(name, arrays, outputs, micros=0.1):
    outs = [in_place((count,) + arrays[0].shape[1:], BF16) for count, _ in outputs]
    kernel = functools.partial(add_kernel, [parts for _, parts in outputs], outs)
    return call(kernel, name, outs, micros, 8)(*arrays)


def join_kernel(first, second, out):
    count = first.shape[0]
    out[0:count] = first[...]
    out[count:] = second[...]


def joined(first, second):
    out = in_place((first.shape[0] + second.shape[0],) + first.shape[1:], first.dtype)
    return call(join_kernel, "joined", (out,), 0.1, 4)(first, second)[0]


def flipped(array, axis, bit):
    return lax.ppermute(array, axis, [(i, i ^ bit) for i in range(lax.axis_size(axis))])


def place_of(index, count):
    bits = count.bit_length() - 1
    return sum(((index >> k) & 1) << (bits - 1 - k) for k in range(bits))


def stack_kernel(*refs):
    for j, ref in enumerate(refs[:-1]):
        refs[-1][j] = ref[...]


def stacked(*arrays):
    out = in_place((len(arrays),) + arrays[0].shape, arrays[0].dtype)
    return call(stack_kernel, "stacked", (out,), 0.1, 4)(*arrays)[0]


def line_kernel(ways, *refs):
    first, second_got, totals, totals_got = refs[:ways], refs[ways : ways + 2], refs[ways + 2], refs[ways + 3]
    first_out, line_out, *second_out = refs[ways + 4 :]
    depth, piece, width = first_out.shape
    for j in range(depth):
        first_out[j] = sum(part[j].astype(F32) for part in first).astype(BF16)
        total = sum(part[depth + j].astype(F32) for part in first)
        line_out[j * piece : (j + 1) * piece, :] = total.astype(BF16)
        for d, out in enumerate(second_out):
            total = sum(part[d * depth + j].astype(F32) for part in second_got)
            out[j] = total.astype(BF16)
    low = (totals[...] + totals_got[...]).astype(BF16)
    edge = depth * piece
    line_out[edge : edge + NSMALL_ROWS, :] = low[:, 0:width]
    line_out[edge + NSMALL_ROWS :, :] = low[:, width:]


def flat_kernel(first, line, line_got, *refs):
    depth, share, width = first.shape
    second, (keep_out, send_out) = refs[:-2], refs[-2:]
    for j in range(depth):
        rows = slice(j * share, (j + 1) * share)
        left = first[j].astype(F32) + line_got[rows, :].astype(F32)
        right = sum(part[j].astype(F32) for part in second)
        if j % 2:
            out = slice(j // 2 * share, (j // 2 + 1) * share)
            send_out[out, 0:width] = left.astype(BF16)
            send_out[out, width:] = right.astype(BF16)
        else:
            keep_out[j // 2, :, 0:width] = left.astype(BF16)
            keep_out[j // 2, :, width:] = right.astype(BF16)
    edge, small = (depth * share, NSMALL_ROWS)
    low = (line[edge:, :].astype(F32) + line_got[edge:, :].astype(F32)).astype(BF16)
    send_out[depth // 2 * share :, 0:width] = low[0:small]
    send_out[depth // 2 * share :, width:] = low[small:]


def halve_kernel(keep, sent, got, keep_out, send_out):
    count, share, _ = keep.shape
    for j in range(count):
        rows = slice(j * share, (j + 1) * share)
        total = (keep[j].astype(F32) + got[rows, :].astype(F32)).astype(BF16)
        if j % 2:
            send_out[j // 2 * share : (j // 2 + 1) * share, :] = total
        else:
            keep_out[j // 2] = total
    low = sent[count * share :, :].astype(F32) + got[count * share :, :].astype(F32)
    send_out[count // 2 * share :, :] = low.astype(BF16)


def mine_kernel(keep, sent, got, out):
    share = keep.shape[1]
    out[0:share, :] = (keep[0].astype(F32) + got[0:share, :].astype(F32)).astype(BF16)
    out[share:, :] = (sent[share:, :].astype(F32) + got[share:, :].astype(F32)).astype(BF16)


def feed_line_kernel(*refs):
    depth = refs[0].shape[0]
    height = refs[0].shape[1]
    parts, outs = refs[:-depth], refs[-depth:]
    for j, out in enumerate(outs):
        out[0:height, :] = sum(part[j].astype(F32) for part in parts[:2]).astype(BF16)
        out[height:, :] = sum(part[j].astype(F32) for part in parts[2:]).astype(BF16)


def ordered_sum(parts, index):
    count = len(parts)
    total = 0.0
    for j in range(count):
        for d in range(count):
            total = total + jnp.where((index - d + count) % count == j, parts[d], 0.0)
    return total


def update_rest_kernel(place, owners, *refs):
    ways = len(refs) - 18
    shares = refs[:ways]
    attn, small = refs[ways : ways + 4], refs[ways + 4 : ways + 8]
    attn_out, small_out, bias_out, grads = refs[ways + 8 : ways + 12], refs[ways + 12 : ways + 16], refs[-2], refs[-1]
    share = shares[0].shape[0] - NSMALL_ROWS
    width = shares[0].shape[1]
    for d in range(ways):
        grads[(place[3] - d + ways) % ways] = shares[d][0:share, :]
    totals = ordered_sum([part[share:, :].astype(F32) for part in shares], place[3])
    new = adamw(*[small[0][...], totals[0:NSMALL]], *[ref[...] for ref in small[1:]], SMALL_RATE, 0.0)
    for out, value in zip(small_out, new):
        out[...] = value
    bias_out[...] = totals[24:]
    seat = (place[0] * 2 + place[1]) * 2 + place[2]
    parts = TILE // share
    held = sum(jnp.where(owners[i] == seat, 1, 0) for i in range(TILES))
    for k in range(CAP):
        for part in range(parts):
            rows = slice(part * share, (part + 1) * share)
            grad = grads[k * parts + part].astype(F32)
            old = [ref[k, rows, :] for ref in attn]
            new = adamw(old[0], grad, *old[1:], MATRIX_RATE, MATRIX_DECAY)
            for out, value in zip(attn_out, new):
                out[k, rows, :] = jnp.where(held > k, value, 0.0)


def in_grad_kernel(incoming, frames, middle_grad, small, in_grad_out):
    size = CHUNK

    def step_of(step, carry):
        rows = pl.ds(pl.multiple_of(step * size, size), size)
        unit, inverse = normal_parts(frames[rows, :].astype(F32))
        back = normal_back(unit, inverse, incoming[rows, :], small[0:1, :])
        in_grad_out[rows, :] = (middle_grad[rows, :] + back).astype(BF16)
        return carry

    lax.fori_loop(0, incoming.shape[0] // size, step_of, 0)


def in_vmem(count):
    return [pl.BlockSpec(memory_space=pltpu.VMEM)] * count


def in_smem(count):
    return [pl.BlockSpec(memory_space=pltpu.SMEM)] * count


def shape(dims, kind):
    return jax.ShapeDtypeStruct(dims, kind)


def swap(array, axis):
    return lax.ppermute(array, axis, [(0, 1), (1, 0)])


def shifted(array, axis, distance):
    count = lax.axis_size(axis)
    return lax.ppermute(array, axis, [(i, (i + distance) % count) for i in range(count)])


def added(*parts):
    return functools.reduce(jnp.add, [part.astype(F32) for part in parts])


def together(*arrays):
    return lax.optimization_barrier(arrays)


def cost(micros):
    return pl.CostEstimate(
        flops=int(micros * 1.1e9), bytes_accessed=int(micros * 3.6e6), transcendentals=0
    )


def far_away(array):
    return pltpu.with_memory_space_constraint(array, pltpu.HBM)


def call(kernel, name, outs, micros, limit, scratch=(), smem=0, fetched=()):
    def run(*arrays):
        arrays = list(arrays[:smem]) + [
            far_away(array) if index in fetched else kept(array)
            for index, array in enumerate(arrays[smem:])
        ]
        return pl.pallas_call(
            kernel,
            out_shape=tuple(outs),
            in_specs=in_smem(smem) + in_vmem(len(arrays) - smem),
            out_specs=tuple(in_vmem(len(outs))),
            scratch_shapes=list(scratch),
            compiler_params=pltpu.CompilerParams(vmem_limit_bytes=limit * 1024 * 1024),
            cost_estimate=cost(micros),
            name=name,
        )(*arrays)

    return run


def kept(array):
    return pltpu.with_memory_space_constraint(array, pltpu.VMEM)


def in_place(dims, kind):
    return pltpu.VMEM(dims, kind)


def feed(place, slabs, first_matrix, second_matrix, bias, second, grad_rows, second_t, grad_t, *sums):
    ways, _, units = first_matrix.shape
    rows, width = second.shape
    block = min(FF_BLOCK, units)
    grads = in_place((ways, 2, slabs, width // slabs // 2, units), BF16)
    return call(
        functools.partial(feed_kernel, not sums),
        "feed",
        (
            grads,
            grads,
            in_place((ways, 1, units), F32),
            in_place((rows, width), F32),
            in_place((rows, width), F32),
        ),
        14,
        8,
        (
            pltpu.VMEM((width, block), BF16),
            pltpu.VMEM((width, block), BF16),
            pltpu.VMEM((rows, block), BF16),
            pltpu.VMEM((rows, block), BF16),
        ),
        smem=1,
    )(place, first_matrix, second_matrix, bias, second, grad_rows, second_t, grad_t, *sums)


def update_feed(place, core_away, y_away, column, states, done=()):
    depth, height, units = column.shape
    anywhere = pl.BlockSpec(memory_space=pl.ANY)
    return pl.pallas_call(
        functools.partial(update_kernel, core_away, y_away),
        out_shape=tuple(shape(state.shape, F32) for state in states),
        in_specs=in_smem(1) + in_vmem(1) + [anywhere] * (4 + len(done)),
        out_specs=(anywhere,) * 4,
        input_output_aliases={6 + j: j for j in range(len(done))},
        scratch_shapes=[
            pltpu.VMEM((depth, 4, height, units), F32),
            pltpu.VMEM((depth, 4, height, units), F32),
            pltpu.SemaphoreType.DMA((depth, 4)),
            pltpu.SemaphoreType.DMA((depth, 4)),
        ],
        compiler_params=pltpu.CompilerParams(vmem_limit_bytes=12 * 1024 * 1024),
        cost_estimate=cost(0.3),
        name="update_feed",
    )(place, kept(column), *[far_away(state) for state in states], *done)


def shards(
    frames,
    cotangent,
    lengths,
    owners,
    attn_master,
    attn_first,
    attn_second,
    attn_average,
    small_master,
    small_first,
    small_second,
    small_average,
    mlp_master,
    mlp_first,
    mlp_second,
    mlp_average,
    bias_master,
    bias_first,
    bias_second,
    bias_average,
):
    local, width = frames.shape
    wide = local + 2 * KEY_RIM
    rows = local + 2 * ROW_RIM
    blocks = rows // QUERY_BLOCK
    assert blocks * QUERY_BLOCK == rows and local % CHUNK == 0
    units = mlp_master.shape[2]
    ways = lax.axis_size("mlp")
    depth = lax.axis_size("z")
    devices = lax.axis_size(GROUPS)
    share = CAP * TILE // ways
    way = lax.axis_index("mlp")
    place = jnp.stack([lax.axis_index(name) for name in GROUPS + (GROUPS,)]).astype(jnp.int32)

    last = local // KEY_RIM - 1
    last_cot = local // ROW_RIM - 1
    rim = KEY_RIM + ROW_RIM
    first_tile, second_tile, to_next, to_past = pl.pallas_call(
        edges_kernel,
        grid=(1,),
        out_shape=(
            in_place((TILE, width), BF16),
            in_place((TILE, width), BF16),
            in_place((rim, width), BF16),
            in_place((rim, width), BF16),
        ),
        in_specs=[
            pl.BlockSpec((CAP, TILE, width), lambda i: (0, 0, 0)),
            pl.BlockSpec((KEY_RIM, width), lambda i: (0, 0)),
            pl.BlockSpec((KEY_RIM, width), lambda i: (last, 0)),
            pl.BlockSpec((ROW_RIM, width), lambda i: (0, 0)),
            pl.BlockSpec((ROW_RIM, width), lambda i: (last_cot, 0)),
        ],
        out_specs=tuple(in_vmem(4)),
        compiler_params=pltpu.CompilerParams(vmem_limit_bytes=8 * 1024 * 1024),
        cost_estimate=cost(1),
        name="edges",
    )(*[far_away(array) for array in (attn_master, frames, frames, cotangent, cotangent)])
    second_tile_y = swap(second_tile, "y")
    pair_b = stacked(second_tile, second_tile_y)[None]
    bits = [1 << k for k in range(depth.bit_length() - 1)][::-1]
    column_a, column_b = (first_tile[None], pair_b)

    up = [(i, i + 1) for i in range(devices - 1)]
    down = [(i + 1, i) for i in range(devices - 1)]
    before = lax.ppermute(to_next, GROUPS, up)
    after = lax.ppermute(to_past, GROUPS, down)

    edges = (before, after)
    for bit in bits[:-1]:
        got_a, got_b = (flipped(column_a, "z", bit), flipped(column_b, "z", bit))
        column_a = joined(column_a, got_a)
        column_a, column_b, edges, place_late = together(column_a, column_b, edges, place)
        column_b = joined(column_b, got_b)
    before, after = edges

    bias_row = bias_master.reshape(1, units)
    cut_rows = width // 2
    half = pl.pallas_call(
        half_kernel,
        grid_spec=pltpu.PrefetchScalarGridSpec(
            num_scalar_prefetch=1,
            grid=(2,),
            in_specs=[
                pl.BlockSpec((1, cut_rows, units), lambda i, place: (place[2], i, 0)),
                pl.BlockSpec((1, units), lambda i, place: (0, 0)),
            ],
            out_specs=pl.BlockSpec(memory_space=pltpu.VMEM),
        ),
        out_shape=in_place((width + 16, units), BF16),
        compiler_params=pltpu.CompilerParams(vmem_limit_bytes=8 * 1024 * 1024),
        cost_estimate=cost(1),
        name="half",
    )(place_late, far_away(mlp_master), bias_row)
    half_got = [shifted(half, "mlp", d) for d in range(1, ways)]
    column_a = joined(column_a, flipped(column_a, "z", 1))
    column_a, mlp_late = together(column_a, mlp_master)
    column_a_y = swap(column_a, "y")
    low_mlp = pl.pallas_call(
        matrices_kernel,
        grid=(2,),
        out_shape=in_place((2, width, units), BF16),
        in_specs=[pl.BlockSpec((2, cut_rows, units), lambda i: (0, i, 0))],
        out_specs=pl.BlockSpec(memory_space=pltpu.VMEM),
        compiler_params=pltpu.CompilerParams(vmem_limit_bytes=12 * 1024 * 1024),
        cost_estimate=cost(0.5),
        name="matrices",
    )(far_away(mlp_late))

    height = -(-max(-(-wide // 128), blocks) // 8) * 8
    cols, codes = pl.pallas_call(
        tables_kernel,
        out_shape=(in_place((wide, 8), F32), in_place((height, 128), F32)),
        in_specs=in_smem(2),
        out_specs=tuple(in_vmem(2)),
        cost_estimate=cost(1),
        name="tables",
    )(place, lengths)

    column_b_z = flipped(column_b, "z", 1)
    conv, first, wide_rows, cot, grad_rows, grad_t = call(
        conv_kernel,
        "norm_conv",
        (
            in_place((3, wide, width), BF16),
            in_place((wide, width), BF16),
            in_place((rows, width), BF16),
            in_place((rows, width), BF16),
            in_place((rows, width), BF16),
            in_place((width, local), BF16),
        ),
        0.5,
        6,
        (pltpu.VMEM((wide + 16, width), F32),),
        fetched=(1, 3),
    )(before, frames, after, cotangent, cols, small_master)

    column_b, column_a_y, conv, half_got, low_mlp = together(
        column_b, column_a_y, conv, half_got, low_mlp
    )
    column_b = joined(column_b, column_b_z)
    columns = [column_a, column_a_y, column_b]
    away = [swap(column, "core") for column in columns]
    tiles = columns[:2] + away[:2] + columns[2:] + away[2:]

    weights, query, keys, values, probs, mixed = call(
        attend_kernel,
        "attend",
        (
            in_place((4 * width, width), BF16),
            in_place((wide, width), BF16),
            in_place((wide, width), BF16),
            in_place((wide, width), BF16),
            in_place((blocks, HEADS * QUERY_BLOCK, KEY_SPAN), F32),
            in_place((rows, width), BF16),
        ),
        0.5,
        8,
        smem=2,
    )(place, owners, *tiles, conv, cols, codes, small_master)
    half_got, mixed = together(half_got, mixed)
    halves = half_got[0][None] if ways == 2 else stacked(*half_got)
    others = swap(halves, "core")
    middle, second, second_t = call(
        middle_kernel,
        "middle",
        (
            in_place((rows, width), F32),
            in_place((rows, width), BF16),
            in_place((width, local), BF16),
        ),
        20,
        8,
    )(mixed, weights, wide_rows, cols, small_master)

    rest = (second, grad_rows, second_t, grad_t)
    far_keep, far_send, far_bias, *sums = feed(
        place, 2 * depth, halves, others, bias_row, *rest
    )
    far_got = swap(far_send, "core")
    near_keep, near_send, near_bias, *sums = feed(
        place, 2 * depth, low_mlp[0][None], low_mlp[1][None], bias_row, *rest, *sums
    )
    near_got = swap(near_send, "core")
    pieces = range(1, ways)
    height = width // (4 * depth)

    def halves_of(array):
        return array.reshape(-1, height, units)

    def row(piece, half, y_away=0):
        return ((piece * 2 + half) * 2 + y_away) * depth

    far = add_into(
        "far_sum",
        (halves_of(far_keep), halves_of(far_got)),
        [(2 * depth, [(i, row(d - 1, 0)) for i in range(2)]) for d in pieces]
        + [(depth, [(i, row(d - 1, 1)) for i in range(2)]) for d in pieces]
        + [(depth, [(i, row(d - 1, 1, 1)) for i in range(2)]) for d in pieces],
        0.1,
    )
    far, sums = together(far, sums)
    far_x = [shifted(far[d - 1], "mlp", -d) for d in pieces]
    far_y = [swap(far[2 * (ways - 1) + d - 1], "y") for d in pieces]

    output, middle_grad, mixed_grad, out_grad, feed_rows = call(
        middle_back_kernel,
        "middle_back",
        (
            shape((local, width), BF16),
            in_place((local, width), F32),
            in_place((rows, width), BF16),
            in_place((width, width), BF16),
            in_place((32, width), F32),
        ),
        0.5,
        8,
        (pltpu.VMEM((rows, width), BF16),),
    )(middle, cot, grad_rows, *sums, mixed, weights, cols, small_master)

    near_keep, mixed_grad, far_y = together(near_keep, mixed_grad, far_y)
    near = add_into(
        "near_sum",
        (halves_of(near_keep), halves_of(near_got)),
        [(2 * depth, [(i, row(0, 0)) for i in range(2)])]
        + [(depth, [(i, row(0, 1, j)) for i in range(2)]) for j in range(2)],
        0.1,
    )
    near, mixed_grad = together(near, mixed_grad)
    near_y = swap(near[2], "y")

    columns = width // 2
    slabs = in_place((2 * ways * depth, share, columns), BF16)

    def scores_back(first_head, mixed_grad):
        return call(
            functools.partial(scores_back_kernel, first_head),
            "scores_back",
            (
                in_place((rows, columns), BF16),
                in_place((rows, columns), BF16),
                in_place((rows, columns), BF16),
                slabs,
                slabs,
            ),
            8,
            10,
            (
                pltpu.VMEM((wide, columns), F32),
                pltpu.VMEM((wide, columns), F32),
                pltpu.VMEM((4 * width, columns), BF16),
            ),
            smem=2,
        )(place, owners, query, keys, values, probs, mixed_grad, conv, out_grad)

    *grads_0, keep_0, send_0 = scores_back(0, mixed_grad)
    got_0 = swap(send_0, "core")

    arrays = (near[0], *far_x, near[1], near_y, *far[ways - 1 : 2 * (ways - 1)], *far_y)
    first_parts = list(range(ways))
    feed_two = add_into(
        "feed_two",
        arrays,
        [(depth, [(i, j * depth) for i in first_parts]) for j in range(2)]
        + [(depth, [(ways, 0), (ways + 1, 0)])]
        + [(depth, [(ways + 1 + d, 0), (2 * ways + d, 0)]) for d in pieces],
        0.1,
    )
    feed_two, mixed_grad, grads_0 = together(feed_two, mixed_grad, grads_0)
    feed_y = swap(feed_two[1], "y")
    feed_x = [shifted(feed_two[2 + d], "mlp", -d) for d in pieces]

    *grads_1, keep_1, send_1 = scores_back(HEADS // 2, mixed_grad)
    got_1 = swap(send_1, "core")
    paired_0 = add_into(
        "paired",
        (keep_0, got_0),
        [(2 * depth, [(i, 2 * depth * d) for i in range(2)]) for d in range(ways)],
        20,
    )
    feed_line = call(
        feed_line_kernel,
        "feed_line",
        tuple(in_place((2 * height, units), BF16) for _ in range(depth)),
        0.1,
        8,
    )(feed_two[0], feed_y, feed_two[2], *feed_x)
    paired_0, feed_line, keep_1, grads_1 = together(paired_0, feed_line, keep_1, grads_1)
    first_got = [shifted(paired_0[d], "mlp", -d) for d in range(1, ways)]
    feed_got = [shifted(feed_line[d], "z", d) for d in range(1, depth)]

    paired_1 = add_into(
        "paired",
        (keep_1, got_1),
        [(ways * depth, [(i, depth * j, 2 * depth) for i in range(2)]) for j in range(2)],
        0.1,
    )
    paired_1, grads_1 = together(paired_1, grads_1)
    second_got = swap(paired_1[1], "y")

    conv_grad = call(
        conv_grad_kernel, "conv_grad", (in_place((3, rows, width), F32),), 20, 8
    )(*grads_0, *grads_1, weights)[0]
    incoming, totals = call(
        conv_back_kernel,
        "conv_back",
        (in_place((local, width), F32), in_place((NSMALL_ROWS, width), F32)),
        12,
        8,
        (pltpu.VMEM((192, width), F32),),
        smem=1,
    )(
        place, grads_0[0], grads_0[2], grads_1[0], grads_1[2], conv_grad, first, frames, feed_rows,
         near_bias, far_bias, cols, small_master,
    )

    totals_got = swap(totals, "core")
    feed_keep, totals = together(feed_line[0], totals)
    feed_own = add_into(
        "feed_own",
        [part[None] for part in (feed_keep, *feed_got)],
        [(1, [(d, 0) for d in range(depth)])],
    )[0]
    feed_own, first_keep = together(feed_own, paired_0[0])
    feed_all = [shifted(feed_own[0], "z", d) for d in range(1, depth)]
    lined, line, *second = call(
        functools.partial(line_kernel, ways),
        "line",
        (
            in_place((depth, share, columns), BF16),
            in_place((depth * share + 2 * NSMALL_ROWS, columns), BF16),
        )
        + (in_place((depth, share, columns), BF16),) * ways,
        0.1,
        8,
    )(first_keep, *first_got, paired_1[0], second_got, totals, totals_got)
    lined, line, second, incoming = together(lined, line, second, incoming)
    line_got = swap(line, "y")
    second_x = [shifted(second[d], "mlp", -d) for d in range(1, ways)]
    in_grad = call(
        in_grad_kernel, "in_grad", (shape((local, width), BF16),), 20, 8, fetched=(1,)
    )(incoming, frames, middle_grad, small_master)[0]
    lined, in_grad = together(lined, in_grad)

    def slabs(count, extra):
        if extra:
            return in_place((count * share + NSMALL_ROWS, width), BF16)
        return in_place((count, share, width), BF16)

    count = depth // 2
    z_keep, z_sent = call(flat_kernel, "flat", (slabs(count, 0), slabs(count, 1)), 0.1, 8)(
        lined, line, line_got, second[0], *second_x
    )
    feed_own, z_keep, z_sent = together(feed_own, z_keep, z_sent)
    z_got = flipped(z_sent, "z", 1)
    feed_sums = [stacked(feed_own[0], *feed_all)]
    feed_sums.append(swap(feed_sums[0], "y"))
    feed_sums.append(swap(feed_sums[0], "core"))
    states = (mlp_master, mlp_first, mlp_second, mlp_average)
    mlp_new = update_feed(place, 0, 0, feed_sums[0], states)
    mlp_new, z_keep = together(mlp_new, z_keep)
    for bit in bits[::-1][1:]:
        count //= 2
        z_keep, z_sent = call(halve_kernel, "halve", (slabs(count, 0), slabs(count, 1)), 0.1, 8)(
            z_keep, z_sent, z_got
        )
        mlp_new, z_keep, z_sent = together(mlp_new, z_keep, z_sent)
        z_got = flipped(z_sent, "z", bit)
    mlp_new = update_feed(place, 1, 0, feed_sums[2], states, mlp_new)
    mlp_new, z_keep = together(mlp_new, z_keep)
    mine = call(mine_kernel, "mine", (in_place((share + NSMALL_ROWS, width), BF16),), 0.1, 8)(
        z_keep, z_sent, z_got
    )[0]
    mine, own_y, mlp_new = together(mine, feed_sums[1], mlp_new)
    shares = [mine] + [shifted(mine, "mlp", d) for d in range(1, ways)]
    other_y = swap(own_y, "core")
    mlp_new = update_feed(place, 0, 1, own_y, states, mlp_new)
    mlp_new, other_y, shares[0] = together(mlp_new, other_y, shares[0])
    mlp_new = update_feed(place, 1, 1, other_y, states, mlp_new)
    attn_shape = shape(attn_master.shape, F32)
    small_shape = shape(small_master.shape, F32)
    rest_new = call(
        update_rest_kernel,
        "update_rest",
        (attn_shape,) * 4 + (small_shape,) * 4 + (in_place((8, width), F32),),
        3,
        12,
        (pltpu.VMEM((ways, share, width), BF16),),
        smem=2,
    )(
        place, owners, *shares, attn_master, attn_first, attn_second, attn_average,
        small_master, small_first, small_second, small_average,
    )

    bias_sum = lax.dynamic_slice_in_dim(rest_new[8].reshape(-1), way * units, units, 0)
    bias_new = adamw(
        bias_master, bias_sum, bias_first, bias_second, bias_average, SMALL_RATE, 0.0
    )
    return (
        output,
        in_grad,
        *rest_new[:8],
        *mlp_new,
        *bias_new,
    )


def solution(mesh):
    seq, mlp = mesh.devices.shape
    grid = Mesh(mesh.devices.reshape(seq // 4, 2, 2, mlp), GROUPS)
    rows = P(GROUPS, None)
    tiles = P(SEATS, None, None)
    units = P(None, None, "mlp")
    bias = P("mlp")
    in_specs = (
        (rows, rows, P(), P()) + (tiles,) * 4 + (P(),) * 4 + (units,) * 4 + (bias,) * 4
    )
    out_specs = (rows, rows) + (tiles,) * 4 + (P(),) * 4 + (units,) * 4 + (bias,) * 4
    return jax.shard_map(shards, mesh=grid, in_specs=in_specs, out_specs=out_specs, check_vma=False)
```

time: 746 us -> 176 us (0.24); the launches traced: 738 us -> 175 us
  waiting for transfers between devices: 310 us -> 39.9 us
  local copies, waits for them, and re-layouts: 107 us -> 0.35 us
  matrix products: 106 us -> 0 us
  Pallas kernels: 0 us -> 93.4 us
  other arithmetic: 82.2 us -> 0.63 us
  blocking collectives: 78.6 us -> 0 us
  starting transfers between devices: 20 us -> 39.8 us
  loops' own time: 18.5 us -> 0 us
  between operations: 15.5 us -> 1.29 us
    psum x2 -> x0, waiting for transfers between devices: 150 us -> none  [the longest x1 88.4 us: shards(): matrix_sum, small_sum = lax.psum((matrix_grads, small_grad), ('seq', 'mlp'))]
    dot_general x33 -> x0, matrix products: 106 us -> none  [the longest x6 23.4 us: contract_cols(): lax.dot_general(left, right, (((1,), (1,)), ((), ())), preferred_element_...]
    reduce_scatter x2 -> x0, waiting for transfers between devices: 94.6 us -> none  [the longest x1 53.5 us: shards(): lax.psum_scatter(contract_cols(active, local_weights[1]), 'mlp', scatter_...]
    pallas_call x0 -> x37, Pallas kernels: none -> 93.4 us  [the longest x29 69.5 us: run(): pl.pallas_call(kernel, out_shape=tuple(outs), in_specs=in_smem(smem) + in...]
    psum x2 -> x0, blocking collectives: 78.6 us -> none  [the longest x1 44.7 us: shards(): matrix_sum, small_sum = lax.psum((matrix_grads, small_grad), ('seq', 'mlp'))]
    all_gather x3 -> x0, waiting for transfers between devices: 57.5 us -> none  [the longest x1 26.4 us: shards(): gathered_rows = lax.all_gather(second, 'mlp', axis=0, tiled=True)]
    ppermute x8 -> x39, waiting for transfers between devices: 7.64 us -> 39.9 us  [the longest x6 26.3 us: flipped(): lax.ppermute(array, axis, [(i, i ^ bit) for i in range(lax.axis_size(axis...]
    reduce_sum x17 -> x0, other arithmetic: 22.4 us -> none  [the longest x1 7.43 us: conv_three(): taps[:, 0, None, :] * before + taps[:, 1, None, :] * middle]
  transfers between devices with their start and end apart: 15 -> 39, of which waited for: 10 -> 17; matrix products, arithmetic and copies ran while one was open for 17% -> 0% of each run, Pallas kernels for 0% -> 37%
where the time goes in v1:
time: 176 us; the launch traced here: 175 us
  Pallas kernels  93.4 us (53%)
  waiting for transfers between devices  39.9 us (23%)
  starting transfers between devices  39.8 us (23%)
    pallas_call x29, Pallas kernels, run(): pl.pallas_call(kernel, out_shape=tuple(outs), in_specs=in_smem(smem) + in...  69.5 us
    ppermute x6, waiting for transfers between devices, flipped(): lax.ppermute(array, axis, [(i, i ^ bit) for i in range(lax.axis_size(axis...  26.3 us
    pallas_call x4, Pallas kernels, update_feed(): pl.pallas_call(functools.partial(update_kernel, core_away, y_away), out_s...  17 us
    ppermute x12, starting transfers between devices, shifted(): lax.ppermute(array, axis, [(i, (i + distance) % count) for i in range(cou...  14.3 us
    ppermute x19, starting transfers between devices, swap(): return lax.ppermute(array, axis, [(0, 1), (1, 0)])  13 us
    ppermute x6, starting transfers between devices, flipped(): lax.ppermute(array, axis, [(i, i ^ bit) for i in range(lax.axis_size(axis...  7.8 us
    ppermute x19, waiting for transfers between devices, swap(): return lax.ppermute(array, axis, [(0, 1), (1, 0)])  6.71 us
    ppermute x12, waiting for transfers between devices, shifted(): lax.ppermute(array, axis, [(i, (i + distance) % count) for i in range(cou...  3.62 us
  transfers between devices with their start and end apart: 39, of which 17 were waited for; matrix products, arithmetic and copies ran while one was open for 0% of the time, Pallas kernels for 37%

profile of v1, /device:TPU:0, one launch (start us, length us, event | category | flops | bytes accessed | tf_op | source)
XLA Modules:
  0.0 175.3 jit_solution(9163751416236275144)
XLA Ops:
  0.7 1.1 edges.1
  1.8 3.0 %collective-permute-start.1 = (bf16[128,512]{1,0:T(8,128)(2,1)S(1)}, bf16[128,512]{1,0:T(8,128)(2,1)S(1)}, u32[]{:S(2)}, u32[]{:S(2)}) collective-permute-start(bf16[128,512]{1,0:T(8,128)(2,1)S(1)} %get-tuple-element.209.refs_0_), channel_id=1, source_target_pairs={{0,4},{4,0},{1,5},{5,1},{2,6},{6,2},{3,7},{7,3},{8,12},{12,8},{9,1... | collective-permute-start | bytes 393224 | tf_op jit(solution)/shard_map/ppermute | solution.py:805
  4.8 2.6 %collective-permute-start = (bf16[1,128,512]{2,1,0:T(8,128)(2,1)S(1)}, bf16[1,128,512]{2,1,0:T(8,128)(2,1)S(1)}, u32[]{:S(2)}, u32[]{:S(2)}) collective-permute-start(bf16[1,128,512]{2,1,0:T(8,128)(2,1)S(1)} %bitcast.35), channel_id=1, source_target_pairs={{0,16},{8,24},{16,0},{24,8},{1,17},{9,25},{17,1},{25,9},{2,18},{10... | collective-permute-start | bytes 393224 | tf_op jit(solution)/shard_map/ppermute | solution.py:660
  7.4 3.4 %collective-permute-start.2 = (bf16[48,512]{1,0:T(8,128)(2,1)S(1)}, bf16[48,512]{1,0:T(8,128)(2,1)S(1)}, u32[]{:S(2)}, u32[]{:S(2)}) collective-permute-start(bf16[48,512]{1,0:T(8,128)(2,1)S(1)} %get-tuple-element.210), channel_id=1, source_target_pairs={{0,1},{1,2},{2,3},{3,4},{4,5},{5,6},{6,7},{7,8},{8,9},{9,10},{10,1... | collective-permute-start | bytes 147464 | tf_op jit(solution)/shard_map/ppermute | solution.py:973
  10.8 1.3 collective-permute-start.3
  12.2 1.3 collective-permute-done.second
  13.5 3.3 %collective-permute-done.3.after = bf16[48,512]{1,0:T(8,128)(2,1)S(1)} collective-permute-done((bf16[48,512]{1,0:T(8,128)(2,1)S(1)}, bf16[48,512]{1,0:T(8,128)(2,1)S(1)}, u32[]{:S(2)}, u32[]{:S(2)}) %collective-permute-start.3) | collective-permute-done | bytes 49184 | tf_op jit(solution)/shard_map/ppermute | solution.py:974
  16.8 2.2 %half.1 = bf16[528,1024]{1,0:T(8,128)(2,1)S(1)} custom-call(s32[5]{0:T(128)S(1)} %stack.23.place.refs_0_, f32[2,512,1024]{2,1,0:T(8,128)} %refs_0_.7, f32[1,1024]{1,0:T(1,128)S(1)} %bitcast.37), custom_call_target="tpu_custom_call" | custom-call | flops 1100000000 | bytes 3600000 | tf_op jit(solution)/shard_map/half/pallas_call | solution.py:986
  19.1 1.6 collective-permute-start.5
  20.7 0.7 collective-permute-start.4
  21.4 9.6 %collective-permute-done.5.second = bf16[2,128,512]{2,1,0:T(8,128)(2,1)S(1)} collective-permute-done((bf16[2,128,512]{2,1,0:T(8,128)(2,1)S(1)}, bf16[2,128,512]{2,1,0:T(8,128)(2,1)S(1)}, u32[]{:S(2)}, u32[]{:S(2)}) %collective-permute-start.5) | collective-permute-done | bytes 262176 | tf_op jit(solution)/shard_map/ppermute | solution.py:660
  31.1 4.7 %collective-permute-done.4.second = bf16[1,2,128,512]{3,2,1,0:T(8,128)(2,1)S(1)} collective-permute-done((bf16[1,2,128,512]{3,2,1,0:T(8,128)(2,1)S(1)}, bf16[1,2,128,512]{3,2,1,0:T(8,128)(2,1)S(1)}, u32[]{:S(2)}, u32[]{:S(2)}) %collective-permute-start.4) | collective-permute-done | bytes 262176 | tf_op jit(solution)/shard_map/ppermute | solution.py:660
  35.9 1.2 tables.1
  37.1 6.7 %norm_conv.1 = (bf16[3,1088,512]{2,1,0:T(8,128)(2,1)S(1)}, bf16[1088,512]{1,0:T(8,128)(2,1)S(1)}, bf16[1056,512]{1,0:T(8,128)(2,1)S(1)}, bf16[1056,512]{1,0:T(8,...) custom-call(bf16[48,512]{1,0:T(8,128)(2,1)S(1)} %collective-permute-done.2.before, ...), custom_call_target="tpu_custom_call" | custom-call | flops 550000000 | bytes 1800000 | tf_op jit(solution)/shard_map/norm_conv/pallas_call | solution.py:837
  43.8 2.4 %matrices.1 = bf16[2,512,1024]{2,1,0:T(8,128)(2,1)S(1)} custom-call(f32[2,512,1024]{2,1,0:T(8,128)} %refs_0_.7), custom_call_target="tpu_custom_call" | custom-call | flops 550000000 | bytes 1800000 | tf_op jit(solution)/shard_map/matrices/pallas_call | solution.py:1006
  46.2 3.0 %collective-permute-done.10.second = bf16[2,2,128,512]{3,2,1,0:T(8,128)(2,1)} collective-permute-done((bf16[2,2,128,512]{3,2,1,0:T(8,128)(2,1)S(1)}, bf16[2,2,128,512]{3,2,1,0:T(8,128)(2,1)}, u32[]{:S(2)}, u32[]{:S(2)}) %collective-permute-start.10) | collective-permute-done | bytes 524320 | tf_op jit(solution)/shard_map/ppermute | solution.py:660
  49.3 1.1 joined.7.refs_4_
  50.5 0.5 collective-permute-start.8
  51.2 2.6 %collective-permute-done.8.refs_2_ = bf16[4,128,512]{2,1,0:T(8,128)(2,1)S(1)} collective-permute-done((bf16[4,128,512]{2,1,0:T(8,128)(2,1)S(1)}, bf16[4,128,512]{2,1,0:T(8,128)(2,1)S(1)}, u32[]{:S(2)}, u32[]{:S(2)}) %collective-permute-start.8) | collective-permute-done | bytes 524320 | tf_op jit(solution)/shard_map/ppermute | solution.py:805
  53.9 0.7 collective-permute-done.9.refs_3_
  54.6 7.6 %attend.1 = (bf16[2048,512]{1,0:T(8,128)(2,1)S(1)}, bf16[1088,512]{1,0:T(8,128)(2,1)S(1)}, bf16[1088,512]{1,0:T(8,128)(2,1)S(1)}, bf16[1088,512]{1,0:T(8,128)(2,...) custom-call(s32[5]{0:T(128)S(1)} %copy-done.4, s32[16]{0:T(128)S(1)} %copy-done.6, ...), custom_call_target="tpu_custom_call" | custom-call | flops 550000000 | bytes 1800000 | tf_op jit(solution)/shard_map/attend/pallas_call | solution.py:837
  62.4 1.5 middle.1
  63.9 1.3 collective-permute-done.12.refs_2_
  65.2 9.6 %feed.2 = (bf16[1,2,8,32,1024]{4,3,2,1,0:T(8,128)(2,1)S(1)}, bf16[1,2,8,32,1024]{4,3,2,1,0:T(8,128)(2,1)S(1)}, f32[1,1,1024]{2,1,0:T(1,128)S(1)}, f32[1056,512]{1,0:T(8,128)S(1)}, f32[1056,512]{1,0:T(8,128)S(1)}) custom-call(s32[5]{0:T(128)S(1)} %copy-done.4, bf16[1,528,1024]{2,1,0:T(8,128)(2,1)} %bitcast.8.refs_1_, ...), custom_call_target="tpu_custom_call" | custom-call | flops 15399999488 | bytes 50400000 | tf_op jit(solution)/shard_map/feed/pallas_call | solution.py:837
  75.0 8.7 %feed.3 = (bf16[1,2,8,32,1024]{4,3,2,1,0:T(8,128)(2,1)S(1)}, bf16[1,2,8,32,1024]{4,3,2,1,0:T(8,128)(2,1)S(1)}, f32[1,1,1024]{2,1,0:T(1,128)S(1)}, f32[1056,512]{1,0:T(8,128)S(1)}, f32[1056,512]{1,0:T(8,128)S(1)}) custom-call(s32[5]{0:T(128)S(1)} %copy-done.4, bf16[1,512,1024]{2,1,0:T(8,128)(2,1)S(1)} %get-tuple-element.403.refs_1_, ...), custom_call_target="tpu_custom_call" | custom-call | flops 15399999488 | bytes 50400000 | tf_op jit(solution)/shard_map/feed/pallas_call | solution.py:837
  83.7 0.4 collective-permute-start.15
  84.6 1.6 collective-permute-start.14
  86.2 1.2 collective-permute-start.17
  87.4 4.5 %middle_back.1 = (bf16[1024,512]{1,0:T(8,128)(2,1)}, f32[1024,512]{1,0:T(8,128)S(1)}, bf16[1056,512]{1,0:T(8,128)(2,1)S(1)}, bf16[512,512]{1,0:T(8,128)(2,1)S(1)}, f32[32,512]{1,0:T(8,128)S(1)}) custom-call(f32[1056,512]{1,0:T(8,128)S(1)} %get-tuple-element.230.middle, bf16[1056,512]{1,0:T(8,128)(2,1)S(1)} %get-tuple-element.231.cot, ...), custom_call_target="tpu_custom_call" | custom-call | flops 550000000 | bytes 1800000 | tf_op jit(solution)/shard_map/middle_back/pallas_call | solution.py:837
  91.9 1.1 collective-permute-done.14.refs_5_
  93.0 0.4 near_sum.1
  93.4 1.6 collective-permute-start.18
  95.0 5.8 %scores_back.2 = (bf16[1056,256]{1,0:T(8,128)(2,1)S(1)}, bf16[1056,256]{1,0:T(8,128)(2,1)S(1)}, bf16[1056,256]{1,0:T(8,128)(2,1)S(1)}, bf16[16,128,256]{2,1,0:T(8,128)(2,1)S(1)}, bf16[16,128,256]{2,1,0:T(8,128)(2,1)S(1)}) custom-call(s32[5]{0:T(128)S(1)} %copy-done.4, s32[16]{0:T(128)S(1)} %copy-done.6, bf16[1088,512]{1,0:T(8,128)(2,1)S(1)} %get-tuple-element.250.query, ...), custom_call_target="tpu_custom_call" | custom-call | flops 8800000000 | bytes 28800000 | tf_op jit(solution)/shard_map/scores_back/pallas_call | solution.py:837
  101.4 1.6 collective-permute-start.19
  103.0 1.2 collective-permute-start.20
  104.2 5.6 %scores_back.3 = (bf16[1056,256]{1,0:T(8,128)(2,1)S(1)}, bf16[1056,256]{1,0:T(8,128)(2,1)S(1)}, bf16[1056,256]{1,0:T(8,128)(2,1)S(1)}, bf16[16,128,256]{2,1,0:T(8,128)(2,1)S(1)}, bf16[16,128,256]{2,1,0:T(8,128)(2,1)S(1)}) custom-call(s32[5]{0:T(128)S(1)} %copy-done.4, s32[16]{0:T(128)S(1)} %copy-done.6, bf16[1088,512]{1,0:T(8,128)(2,1)S(1)} %get-tuple-element.250.query, ...), custom_call_target="tpu_custom_call" | custom-call | flops 8800000000 | bytes 28800000 | tf_op jit(solution)/shard_map/scores_back/pallas_call | solution.py:837
  110.5 0.4 paired.2
  111.2 1.3 collective-permute-start.23
  112.6 2.2 %collective-permute-start.24 = (bf16[64,1024]{1,0:T(8,128)(2,1)S(1)}, bf16[64,1024]{1,0:T(8,128)(2,1)S(1)}, u32[]{:S(2)}, u32[]{:S(2)}) collective-permute-start(bf16[64,1024]{1,0:T(8,128)(2,1)S(1)} %get-tuple-element.317), channel_id=1, source_target_pairs={{0,24},{8,0},{16,8},{24,16},{1,25},{9,1},{17,9},{25,17},{2,26},{10... | collective-permute-start | bytes 393224 | tf_op jit(solution)/shard_map/ppermute | solution.py:810
  114.8 1.1 collective-permute-start.25
  116.3 1.7 collective-permute-start.26
  118.0 1.9 %conv_grad.1 = f32[3,1056,512]{2,1,0:T(8,128)S(1)} custom-call(bf16[1056,256]{1,0:T(8,128)(2,1)S(1)} %get-tuple-element.296.refs_0_.query_grad_0, bf16[1056,256]{1,0:T(8,128)(2,1)S(1)} %get-tuple-element.307.refs_1_, bf16[1056,256]{1,0:T(8,128)(2,1)S(1)} %get-tuple-element.297.refs_2_.value_grad_0, ...), custom_call_target="tpu_custom_call" | custom-call | flops 22000001024 | bytes 72000000 | tf_op jit(solution)/shard_map/conv_grad/pallas_call | solution.py:837
  119.9 6.6 %conv_back.1 = (f32[1024,512]{1,0:T(8,128)S(1)}, f32[32,512]{1,0:T(8,128)S(1)}) custom-call(s32[5]{0:T(128)S(1)} %copy-done.4, bf16[1056,256]{1,0:T(8,128)(2,1)S(1)} %get-tuple-element.296.refs_0_.query_grad_0, bf16[1056,256]{1,0:T(8,128)(2,1)S(1)} %get-tuple-element.297.refs_2_.value_grad_0, bf16[1056,256]{1,0:T(8,128)(2,1)S(1)} %get-tuple-element.305.refs_3_.query_grad_1, ...), custom_call_target="tpu_custom_call" | custom-call | flops 13200000000 | bytes 43200000 | tf_op jit(solution)/shard_map/conv_back/pallas_call | solution.py:837
  126.7 0.6 collective-permute-start.30
  127.3 1.5 collective-permute-start.31
  128.9 2.8 %collective-permute-start.32 = (bf16[64,1024]{1,0:T(8,128)(2,1)S(1)}, bf16[64,1024]{1,0:T(8,128)(2,1)S(1)}, u32[]{:S(2)}, u32[]{:S(2)}) collective-permute-start(bf16[64,1024]{1,0:T(8,128)(2,1)S(1)} %bitcast.29), channel_id=1, source_target_pairs={{0,24},{8,0},{16,8},{24,16},{1,25},{9,1},{17,9},{25,17},{2,26},{10... | collective-permute-start | bytes 393224 | tf_op jit(solution)/shard_map/ppermute | solution.py:810
  132.0 0.4 collective-permute-start.28
  132.4 0.9 collective-permute-start.29
  133.3 4.6 %in_grad.1 = bf16[1024,512]{1,0:T(8,128)(2,1)} custom-call(f32[1024,512]{1,0:T(8,128)S(1)} %get-tuple-element.330.incoming, bf16[1024,512]{1,0:T(8,128)(2,1)} %frames.5, f32[1024,512]{1,0:T(8,128)S(1)} %get-tuple-element.331.middle_grad, f32[17,512]{1,0:T(8,128)S(1)} %copy-done.2), custom_call_target="tpu_custom_call" | custom-call | flops 22000001024 | bytes 72000000 | tf_op jit(solution)/shard_map/in_grad/pallas_call | solution.py:837
  137.9 2.0 %collective-permute-done.29.refs_1_ = bf16[4,128,256]{2,1,0:T(8,128)(2,1)S(1)} collective-permute-done((bf16[4,128,256]{2,1,0:T(8,128)(2,1)S(1)}, bf16[4,128,256]{2,1,0:T(8,128)(2,1)S(1)}, u32[]{:S(2)}, u32[]{:S(2)}) %collective-permute-start.29) | collective-permute-done | bytes 262176 | tf_op jit(solution)/shard_map/ppermute | solution.py:810
  140.0 0.6 collective-permute-done.28.line_got
  140.9 1.1 collective-permute-start.36
  142.0 1.4 collective-permute-start.34
  143.4 4.2 %update_feed.4 = (f32[2,512,1024]{2,1,0:T(8,128)}, f32[2,512,1024]{2,1,0:T(8,128)}, f32[2,512,1024]{2,1,0:T(8,128)}, f32[2,512,1024]{2,1,0:T(8,128)}) custom-call(s32[5]{0:T(128)S(1)} %copy-done.4, bf16[4,64,1024]{2,1,0:T(8,128)(2,1)S(1)} %stacked.3.column, f32[2,512,1024]{2,1,0:T(8,128)} %refs_0_.7, f32[2,512,1024]{2,1,0:T(8,128)} %refs_1_.7, ...), custom_call_target="tpu_custom_call" | custom-call | flops 330000000 | bytes 1080000 | tf_op jit(solution)/shard_map/update_feed/pallas_call | solution.py:889
  147.6 3.4 %collective-permute-done.34.got = bf16[288,512]{1,0:T(8,128)(2,1)S(1)} collective-permute-done((bf16[288,512]{1,0:T(8,128)(2,1)S(1)}, bf16[288,512]{1,0:T(8,128)(2,1)S(1)}, u32[]{:S(2)}, u32[]{:S(2)}) %collective-permute-start.34) | collective-permute-done | bytes 294944 | tf_op jit(solution)/shard_map/ppermute | solution.py:660
  151.1 1.4 collective-permute-start.35
  152.6 4.2 %update_feed.5 = (f32[2,512,1024]{2,1,0:T(8,128)}, f32[2,512,1024]{2,1,0:T(8,128)}, f32[2,512,1024]{2,1,0:T(8,128)}, f32[2,512,1024]{2,1,0:T(8,128)}) custom-call(s32[5]{0:T(128)S(1)} %copy-done.4, bf16[4,64,1024]{2,1,0:T(8,128)(2,1)S(1)} %collective-permute-done.33.column, ...), custom_call_target="tpu_custom_call", output_to_operand_aliasing={{0}: (6, {}), {1}: (7, {}), {2}: (8, {}), {3}: (9, {})} | custom-call | flops 330000000 | bytes 1080000 | tf_op jit(solution)/shard_map/update_feed/pallas_call | solution.py:889
  156.8 4.3 %collective-permute-done.35.got = bf16[160,512]{1,0:T(8,128)(2,1)S(1)} collective-permute-done((bf16[160,512]{1,0:T(8,128)(2,1)S(1)}, bf16[160,512]{1,0:T(8,128)(2,1)S(1)}, u32[]{:S(2)}, u32[]{:S(2)}) %collective-permute-start.35) | collective-permute-done | bytes 163872 | tf_op jit(solution)/shard_map/ppermute | solution.py:660
  161.2 0.9 collective-permute-start.38
  162.1 4.3 %update_feed.6 = (f32[2,512,1024]{2,1,0:T(8,128)}, f32[2,512,1024]{2,1,0:T(8,128)}, f32[2,512,1024]{2,1,0:T(8,128)}, f32[2,512,1024]{2,1,0:T(8,128)}) custom-call(s32[5]{0:T(128)S(1)} %copy-done.4, bf16[4,64,1024]{2,1,0:T(8,128)(2,1)S(1)} %collective-permute-done.36.column, ...), custom_call_target="tpu_custom_call", output_to_operand_aliasing={{0}: (6, {}), {1}: (7, {}), {2}: (8, {}), {3}: (9, {})} | custom-call | flops 330000000 | bytes 1080000 | tf_op jit(solution)/shard_map/update_feed/pallas_call | solution.py:889
  166.5 1.4 collective-permute-done.38.refs_1_
  167.9 2.5 %update_rest.1 = (f32[2,128,512]{2,1,0:T(8,128)}, f32[2,128,512]{2,1,0:T(8,128)}, f32[2,128,512]{2,1,0:T(8,128)}, f32[2,128,512]{2,1,0:T(8,128)}, f32[17,512]{1,...) custom-call(s32[5]{0:T(128)S(1)} %copy-done.4, ...), custom_call_target="tpu_custom_call" | custom-call | flops 3300000000 | bytes 10800000 | tf_op jit(solution)/shard_map/update_rest/pallas_call | solution.py:837
  170.4 4.2 %update_feed.7 = (f32[2,512,1024]{2,1,0:T(8,128)}, f32[2,512,1024]{2,1,0:T(8,128)}, f32[2,512,1024]{2,1,0:T(8,128)}, f32[2,512,1024]{2,1,0:T(8,128)}) custom-call(s32[5]{0:T(128)S(1)} %copy-done.4, bf16[4,64,1024]{2,1,0:T(8,128)(2,1)S(1)} %collective-permute-done.37.column, ...), custom_call_target="tpu_custom_call", output_to_operand_aliasing={{0}: (6, {}), {1}: (7, {}), {2}: (8, {}), {3}: (9, {})} | custom-call | flops 330000000 | bytes 1080000 | tf_op jit(solution)/shard_map/update_feed/pallas_call | solution.py:889
  174.7 0.6 multiply_add_fusion
  (87 shorter events, 4.4 us)
Async XLA Ops:
  0.7 16.1 %copy-start.5 = (f32[1024]{0:T(1024)S(1)}, f32[1024]{0:T(1024)}, u32[]{:S(2)}) copy-start(f32[1024]{0:T(1024)} %param.36) | copy-start | bytes 12292
  1.8 10.4 %collective-permute-start.1 = (bf16[128,512]{1,0:T(8,128)(2,1)S(1)}, bf16[128,512]{1,0:T(8,128)(2,1)S(1)}, u32[]{:S(2)}, u32[]{:S(2)}) collective-permute-start(bf16[128,512]{1,0:T(8,128)(2,1)S(1)} %get-tuple-element.209.refs_0_), channel_id=1, source_target_pairs={{0,4},{4,0},{1,5},{5,1},{2,6},{6,2},{3,7},{7,3},{8,12},{12,8},{9,1... | collective-permute-start | bytes 393224 | tf_op jit(solution)/shard_map/ppermute | solution.py:805
  4.8 8.7 %collective-permute-start = (bf16[1,128,512]{2,1,0:T(8,128)(2,1)S(1)}, bf16[1,128,512]{2,1,0:T(8,128)(2,1)S(1)}, u32[]{:S(2)}, u32[]{:S(2)}) collective-permute-start(bf16[1,128,512]{2,1,0:T(8,128)(2,1)S(1)} %bitcast.35), channel_id=1, source_target_pairs={{0,16},{8,24},{16,0},{24,8},{1,17},{9,25},{17,1},{25,9},{2,18},{10... | collective-permute-start | bytes 393224 | tf_op jit(solution)/shard_map/ppermute | solution.py:660
  7.4 6.1 %collective-permute-start.2 = (bf16[48,512]{1,0:T(8,128)(2,1)S(1)}, bf16[48,512]{1,0:T(8,128)(2,1)S(1)}, u32[]{:S(2)}, u32[]{:S(2)}) collective-permute-start(bf16[48,512]{1,0:T(8,128)(2,1)S(1)} %get-tuple-element.210), channel_id=1, source_target_pairs={{0,1},{1,2},{2,3},{3,4},{4,5},{5,6},{6,7},{7,8},{8,9},{9,10},{10,1... | collective-permute-start | bytes 147464 | tf_op jit(solution)/shard_map/ppermute | solution.py:973
  10.8 6.0 %collective-permute-start.3 = (bf16[48,512]{1,0:T(8,128)(2,1)S(1)}, bf16[48,512]{1,0:T(8,128)(2,1)S(1)}, u32[]{:S(2)}, u32[]{:S(2)}) collective-permute-start(bf16[48,512]{1,0:T(8,128)(2,1)S(1)} %get-tuple-element.211), channel_id=1, source_target_pairs={{1,0},{2,1},{3,2},{4,3},{5,4},{6,5},{7,6},{8,7},{9,8},{10,9},{11,1... | collective-permute-start | bytes 147464 | tf_op jit(solution)/shard_map/ppermute | solution.py:974
  12.2 6.8 %copy-start.3 = (s32[5]{0:T(128)}, s32[5]{0:T(128)S(1)}, u32[]{:S(2)}) copy-start(s32[5]{0:T(128)S(1)} %stack.23.place.refs_0_) | copy-start | bytes 64
  19.0 27.2 %collective-permute-start.7 = (bf16[528,1024]{1,0:T(8,128)(2,1)S(1)}, bf16[528,1024]{1,0:T(8,128)(2,1)}, u32[]{:S(2)}, u32[]{:S(2)}) collective-permute-start(bf16[528,1024]{1,0:T(8,128)(2,1)S(1)} %half.1), channel_id=1, source_target_pairs={{0,1},{1,0},{2,3},{3,2},{4,5},{5,4},{6,7},{7,6},{8,9},{9,8},{10,11... | collective-permute-start | bytes 3244040 | tf_op jit(solution)/shard_map/ppermute | solution.py:810
  19.1 11.9 %collective-permute-start.5 = (bf16[2,128,512]{2,1,0:T(8,128)(2,1)S(1)}, bf16[2,128,512]{2,1,0:T(8,128)(2,1)S(1)}, u32[]{:S(2)}, u32[]{:S(2)}) collective-permute-start(bf16[2,128,512]{2,1,0:T(8,128)(2,1)S(1)} %joined.4.first), channel_id=1, source_target_pairs={{0,8},{8,0},{16,24},{24,16},{1,9},{9,1},{17,25},{25,17},{2,10},{10... | collective-permute-start | bytes 786440 | tf_op jit(solution)/shard_map/ppermute | solution.py:660
  20.7 15.1 %collective-permute-start.4 = (bf16[1,2,128,512]{3,2,1,0:T(8,128)(2,1)S(1)}, bf16[1,2,128,512]{3,2,1,0:T(8,128)(2,1)S(1)}, u32[]{:S(2)}, u32[]{:S(2)}) collective-permute-start(bf16[1,2,128,512]{3,2,1,0:T(8,128)(2,1)S(1)} %bitcast.25), channel_id=1, source_target_pairs={{0,16},{8,24},{16,0},{24,8},{1,17},{9,25},{17,1},{25,9},{2,18},{10... | collective-permute-start | bytes 786440 | tf_op jit(solution)/shard_map/ppermute | solution.py:660
  31.0 15.2 %collective-permute-start.6 = (bf16[4,128,512]{2,1,0:T(8,128)(2,1)S(1)}, bf16[4,128,512]{2,1,0:T(8,128)(2,1)S(1)}, u32[]{:S(2)}, u32[]{:S(2)}) collective-permute-start(bf16[4,128,512]{2,1,0:T(8,128)(2,1)S(1)} %joined.6.refs_0_), channel_id=1, source_target_pairs={{0,4},{4,0},{1,5},{5,1},{2,6},{6,2},{3,7},{7,3},{8,12},{12,8},{9,1... | collective-permute-start | bytes 1572872 | tf_op jit(solution)/shard_map/ppermute | solution.py:805
  35.8 1.3 copy-start.2
  35.8 13.5 %collective-permute-start.10 = (bf16[2,2,128,512]{3,2,1,0:T(8,128)(2,1)S(1)}, bf16[2,2,128,512]{3,2,1,0:T(8,128)(2,1)}, u32[]{:S(2)}, u32[]{:S(2)}) collective-permute-start(bf16[2,2,128,512]{3,2,1,0:T(8,128)(2,1)S(1)} %joined.5.first), channel_id=1, source_target_pairs={{0,8},{8,0},{16,24},{24,16},{1,9},{9,1},{17,25},{25,17},{2,10},{10... | collective-permute-start | bytes 1572872 | tf_op jit(solution)/shard_map/ppermute | solution.py:660
  50.4 4.3 %copy-start.4 = (s32[5]{0:T(128)S(1)}, s32[5]{0:T(128)}, u32[]{:S(2)}) copy-start(s32[5]{0:T(128)} %copy-done.3) | copy-start | bytes 64
  50.4 4.2 %copy-start.6 = (s32[16]{0:T(128)S(1)}, s32[16]{0:T(128)}, u32[]{:S(2)}) copy-start(s32[16]{0:T(128)} %owners.7) | copy-start | bytes 196
  50.4 4.2 %collective-permute-start.11 = (bf16[4,2,128,512]{3,2,1,0:T(8,128)(2,1)S(1)}, bf16[4,2,128,512]{3,2,1,0:T(8,128)(2,1)S(1)}, u32[]{:S(2)}, u32[]{:S(2)}) collective-permute-start(bf16[4,2,128,512]{3,2,1,0:T(8,128)(2,1)S(1)} %joined.7.refs_4_), channel_id=1, source_target_pairs={{0,2},{2,0},{1,3},{3,1},{4,6},{6,4},{5,7},{7,5},{8,10},{10,8},{9,1... | collective-permute-start | bytes 3145736 | tf_op jit(solution)/shard_map/ppermute | solution.py:805
  50.5 3.4 %collective-permute-start.8 = (bf16[4,128,512]{2,1,0:T(8,128)(2,1)S(1)}, bf16[4,128,512]{2,1,0:T(8,128)(2,1)S(1)}, u32[]{:S(2)}, u32[]{:S(2)}) collective-permute-start(bf16[4,128,512]{2,1,0:T(8,128)(2,1)S(1)} %joined.6.refs_0_), channel_id=1, source_target_pairs={{0,2},{2,0},{1,3},{3,1},{4,6},{6,4},{5,7},{7,5},{8,10},{10,8},{9,1... | collective-permute-start | bytes 1572872 | tf_op jit(solution)/shard_map/ppermute | solution.py:805
  51.0 3.6 %collective-permute-start.9 = (bf16[4,128,512]{2,1,0:T(8,128)(2,1)S(1)}, bf16[4,128,512]{2,1,0:T(8,128)(2,1)S(1)}, u32[]{:S(2)}, u32[]{:S(2)}) collective-permute-start(bf16[4,128,512]{2,1,0:T(8,128)(2,1)S(1)} %collective-permute-done.6.refs_1_), channel_id=1, source_target_pairs={{0,2},{2,0},{1,3},{3,1},{4,6},{6,4},{5,7},{7,5},{8,10},{10,8},{9,1... | collective-permute-start | bytes 1572872 | tf_op jit(solution)/shard_map/ppermute | solution.py:805
  62.2 3.0 %collective-permute-start.12 = (bf16[1,528,1024]{2,1,0:T(8,128)(2,1)}, bf16[1,528,1024]{2,1,0:T(8,128)(2,1)S(1)}, u32[]{:S(2)}, u32[]{:S(2)}) collective-permute-start(bf16[1,528,1024]{2,1,0:T(8,128)(2,1)} %bitcast.8.refs_1_), channel_id=1, source_target_pairs={{0,2},{2,0},{1,3},{3,1},{4,6},{6,4},{5,7},{7,5},{8,10},{10,8},{9,1... | collective-permute-start | bytes 3244040 | tf_op jit(solution)/shard_map/ppermute | solution.py:805
  74.8 9.3 %collective-permute-start.13 = (bf16[1,2,8,32,1024]{4,3,2,1,0:T(8,128)(2,1)S(1)}, bf16[1,2,8,32,1024]{4,3,2,1,0:T(8,128)(2,1)S(1)}, u32[]{:S(2)}, u32[]{:S(2)}) collective-permute-start(bf16[1,2,8,32,1024]{4,3,2,1,0:T(8,128)(2,1)S(1)} %get-tuple-element.238), channel_id=1, source_target_pairs={{0,2},{2,0},{1,3},{3,1},{4,6},{6,4},{5,7},{7,5},{8,10},{10,8},{9,1... | collective-permute-start | bytes 3145736 | tf_op jit(solution)/shard_map/ppermute | solution.py:805
  83.7 9.3 %collective-permute-start.15 = (bf16[1,2,8,32,1024]{4,3,2,1,0:T(8,128)(2,1)S(1)}, bf16[1,2,8,32,1024]{4,3,2,1,0:T(8,128)(2,1)S(1)}, u32[]{:S(2)}, u32[]{:S(2)}) collective-permute-start(bf16[1,2,8,32,1024]{4,3,2,1,0:T(8,128)(2,1)S(1)} %get-tuple-element.258), channel_id=1, source_target_pairs={{0,2},{2,0},{1,3},{3,1},{4,6},{6,4},{5,7},{7,5},{8,10},{10,8},{9,1... | collective-permute-start | bytes 3145736 | tf_op jit(solution)/shard_map/ppermute | solution.py:805
  84.6 8.4 %collective-permute-start.14 = (bf16[4,32,1024]{2,1,0:T(8,128)(2,1)S(1)}, bf16[4,32,1024]{2,1,0:T(8,128)(2,1)S(1)}, u32[]{:S(2)}, u32[]{:S(2)}) collective-permute-start(bf16[4,32,1024]{2,1,0:T(8,128)(2,1)S(1)} %get-tuple-element.256), channel_id=1, source_target_pairs={{0,4},{4,0},{1,5},{5,1},{2,6},{6,2},{3,7},{7,3},{8,12},{12,8},{9,1... | collective-permute-start | bytes 786440 | tf_op jit(solution)/shard_map/ppermute | solution.py:805
  86.2 14.7 %collective-permute-start.17 = (bf16[8,32,1024]{2,1,0:T(8,128)(2,1)S(1)}, bf16[8,32,1024]{2,1,0:T(8,128)(2,1)S(1)}, u32[]{:S(2)}, u32[]{:S(2)}) collective-permute-start(bf16[8,32,1024]{2,1,0:T(8,128)(2,1)S(1)} %get-tuple-element.270), channel_id=1, source_target_pairs={{0,1},{1,0},{2,3},{3,2},{4,5},{5,4},{6,7},{7,6},{8,9},{9,8},{10,11... | collective-permute-start | bytes 1572872 | tf_op jit(solution)/shard_map/ppermute | solution.py:810
  93.4 7.6 %collective-permute-start.18 = (bf16[4,32,1024]{2,1,0:T(8,128)(2,1)S(1)}, bf16[4,32,1024]{2,1,0:T(8,128)(2,1)S(1)}, u32[]{:S(2)}, u32[]{:S(2)}) collective-permute-start(bf16[4,32,1024]{2,1,0:T(8,128)(2,1)S(1)} %get-tuple-element.272), channel_id=1, source_target_pairs={{0,4},{4,0},{1,5},{5,1},{2,6},{6,2},{3,7},{7,3},{8,12},{12,8},{9,1... | collective-permute-start | bytes 786440 | tf_op jit(solution)/shard_map/ppermute | solution.py:805
  100.8 9.6 %collective-permute-start.16 = (bf16[16,128,256]{2,1,0:T(8,128)(2,1)S(1)}, bf16[16,128,256]{2,1,0:T(8,128)(2,1)S(1)}, u32[]{:S(2)}, u32[]{:S(2)}) collective-permute-start(bf16[16,128,256]{2,1,0:T(8,128)(2,1)S(1)} %get-tuple-element.266), channel_id=1, source_target_pairs={{0,2},{2,0},{1,3},{3,1},{4,6},{6,4},{5,7},{7,5},{8,10},{10,8},{9,1... | collective-permute-start | bytes 3145736 | tf_op jit(solution)/shard_map/ppermute | solution.py:805
  101.4 8.7 %collective-permute-start.19 = (bf16[4,32,1024]{2,1,0:T(8,128)(2,1)S(1)}, bf16[4,32,1024]{2,1,0:T(8,128)(2,1)S(1)}, u32[]{:S(2)}, u32[]{:S(2)}) collective-permute-start(bf16[4,32,1024]{2,1,0:T(8,128)(2,1)S(1)} %get-tuple-element.283), channel_id=1, source_target_pairs={{0,4},{4,0},{1,5},{5,1},{2,6},{6,2},{3,7},{7,3},{8,12},{12,8},{9,1... | collective-permute-start | bytes 786440 | tf_op jit(solution)/shard_map/ppermute | solution.py:805
  103.0 7.3 %collective-permute-start.20 = (bf16[4,32,1024]{2,1,0:T(8,128)(2,1)S(1)}, bf16[4,32,1024]{2,1,0:T(8,128)(2,1)S(1)}, u32[]{:S(2)}, u32[]{:S(2)}) collective-permute-start(bf16[4,32,1024]{2,1,0:T(8,128)(2,1)S(1)} %get-tuple-element.285), channel_id=1, source_target_pairs={{0,1},{1,0},{2,3},{3,2},{4,5},{5,4},{6,7},{7,6},{8,9},{9,8},{10,11... | collective-permute-start | bytes 786440 | tf_op jit(solution)/shard_map/ppermute | solution.py:810
  109.8 6.1 %collective-permute-start.21 = (bf16[16,128,256]{2,1,0:T(8,128)(2,1)S(1)}, bf16[16,128,256]{2,1,0:T(8,128)(2,1)S(1)}, u32[]{:S(2)}, u32[]{:S(2)}) collective-permute-start(bf16[16,128,256]{2,1,0:T(8,128)(2,1)S(1)} %get-tuple-element.299), channel_id=1, source_target_pairs={{0,2},{2,0},{1,3},{3,1},{4,6},{6,4},{5,7},{7,5},{8,10},{10,8},{9,1... | collective-permute-start | bytes 3145736 | tf_op jit(solution)/shard_map/ppermute | solution.py:805
  110.9 15.6 %collective-permute-start.22 = (bf16[64,1024]{1,0:T(8,128)(2,1)S(1)}, bf16[64,1024]{1,0:T(8,128)(2,1)S(1)}, u32[]{:S(2)}, u32[]{:S(2)}) collective-permute-start(bf16[64,1024]{1,0:T(8,128)(2,1)S(1)} %get-tuple-element.315), channel_id=1, source_target_pairs={{0,8},{8,16},{16,24},{24,0},{1,9},{9,17},{17,25},{25,1},{2,10},{10... | collective-permute-start | bytes 393224 | tf_op jit(solution)/shard_map/ppermute | solution.py:810
  111.2 15.4 %collective-permute-start.23 = (bf16[64,1024]{1,0:T(8,128)(2,1)S(1)}, bf16[64,1024]{1,0:T(8,128)(2,1)S(1)}, u32[]{:S(2)}, u32[]{:S(2)}) collective-permute-start(bf16[64,1024]{1,0:T(8,128)(2,1)S(1)} %get-tuple-element.316), channel_id=1, source_target_pairs={{0,16},{8,24},{16,0},{24,8},{1,17},{9,25},{17,1},{25,9},{2,18},{10... | collective-permute-start | bytes 393224 | tf_op jit(solution)/shard_map/ppermute | solution.py:810
  112.6 14.0 %collective-permute-start.24 = (bf16[64,1024]{1,0:T(8,128)(2,1)S(1)}, bf16[64,1024]{1,0:T(8,128)(2,1)S(1)}, u32[]{:S(2)}, u32[]{:S(2)}) collective-permute-start(bf16[64,1024]{1,0:T(8,128)(2,1)S(1)} %get-tuple-element.317), channel_id=1, source_target_pairs={{0,24},{8,0},{16,8},{24,16},{1,25},{9,1},{17,9},{25,17},{2,26},{10... | collective-permute-start | bytes 393224 | tf_op jit(solution)/shard_map/ppermute | solution.py:810
  114.8 16.9 %collective-permute-start.25 = (bf16[8,128,256]{2,1,0:T(8,128)(2,1)S(1)}, bf16[8,128,256]{2,1,0:T(8,128)(2,1)S(1)}, u32[]{:S(2)}, u32[]{:S(2)}) collective-permute-start(bf16[8,128,256]{2,1,0:T(8,128)(2,1)S(1)} %get-tuple-element.320), channel_id=1, source_target_pairs={{0,1},{1,0},{2,3},{3,2},{4,5},{5,4},{6,7},{7,6},{8,9},{9,8},{10,11... | collective-permute-start | bytes 1572872 | tf_op jit(solution)/shard_map/ppermute | solution.py:810
  116.3 3.6 %copy-start = (bf16[1024,512]{1,0:T(8,128)(2,1)S(1)}, bf16[1024,512]{1,0:T(8,128)(2,1)}, u32[]{:S(2)}) copy-start(bf16[1024,512]{1,0:T(8,128)(2,1)} %frames.5) | copy-start | bytes 3145732
  116.3 15.4 %collective-permute-start.26 = (bf16[8,128,256]{2,1,0:T(8,128)(2,1)S(1)}, bf16[8,128,256]{2,1,0:T(8,128)(2,1)S(1)}, u32[]{:S(2)}, u32[]{:S(2)}) collective-permute-start(bf16[8,128,256]{2,1,0:T(8,128)(2,1)S(1)} %get-tuple-element.322), channel_id=1, source_target_pairs={{0,4},{4,0},{1,5},{5,1},{2,6},{6,2},{3,7},{7,3},{8,12},{12,8},{9,1... | collective-permute-start | bytes 1572872 | tf_op jit(solution)/shard_map/ppermute | solution.py:805
  126.5 2.3 %collective-permute-start.27 = (f32[32,512]{1,0:T(8,128)S(1)}, f32[32,512]{1,0:T(8,128)S(1)}, u32[]{:S(2)}, u32[]{:S(2)}) collective-permute-start(f32[32,512]{1,0:T(8,128)S(1)} %get-tuple-element.323.refs_4_), channel_id=1, source_target_pairs={{0,2},{2,0},{1,3},{3,1},{4,6},{6,4},{5,7},{7,5},{8,10},{10,8},{9,1... | collective-permute-start | bytes 196616 | tf_op jit(solution)/shard_map/ppermute | solution.py:805
  126.7 14.0 %collective-permute-start.30 = (bf16[64,1024]{1,0:T(8,128)(2,1)S(1)}, bf16[64,1024]{1,0:T(8,128)(2,1)S(1)}, u32[]{:S(2)}, u32[]{:S(2)}) collective-permute-start(bf16[64,1024]{1,0:T(8,128)(2,1)S(1)} %bitcast.27), channel_id=1, source_target_pairs={{0,8},{8,16},{16,24},{24,0},{1,9},{9,17},{17,25},{25,1},{2,10},{10... | collective-permute-start | bytes 393224 | tf_op jit(solution)/shard_map/ppermute | solution.py:810
  127.3 13.4 %collective-permute-start.31 = (bf16[64,1024]{1,0:T(8,128)(2,1)S(1)}, bf16[64,1024]{1,0:T(8,128)(2,1)S(1)}, u32[]{:S(2)}, u32[]{:S(2)}) collective-permute-start(bf16[64,1024]{1,0:T(8,128)(2,1)S(1)} %bitcast.28), channel_id=1, source_target_pairs={{0,16},{8,24},{16,0},{24,8},{1,17},{9,25},{17,1},{25,9},{2,18},{10... | collective-permute-start | bytes 393224 | tf_op jit(solution)/shard_map/ppermute | solution.py:810
  128.9 11.9 %collective-permute-start.32 = (bf16[64,1024]{1,0:T(8,128)(2,1)S(1)}, bf16[64,1024]{1,0:T(8,128)(2,1)S(1)}, u32[]{:S(2)}, u32[]{:S(2)}) collective-permute-start(bf16[64,1024]{1,0:T(8,128)(2,1)S(1)} %bitcast.29), channel_id=1, source_target_pairs={{0,24},{8,0},{16,8},{24,16},{1,25},{9,1},{17,9},{25,17},{2,26},{10... | collective-permute-start | bytes 393224 | tf_op jit(solution)/shard_map/ppermute | solution.py:810
  132.0 8.6 %collective-permute-start.28 = (bf16[576,256]{1,0:T(8,128)(2,1)S(1)}, bf16[576,256]{1,0:T(8,128)(2,1)S(1)}, u32[]{:S(2)}, u32[]{:S(2)}) collective-permute-start(bf16[576,256]{1,0:T(8,128)(2,1)S(1)} %get-tuple-element.335.line), channel_id=1, source_target_pairs={{0,4},{4,0},{1,5},{5,1},{2,6},{6,2},{3,7},{7,3},{8,12},{12,8},{9,1... | collective-permute-start | bytes 884744 | tf_op jit(solution)/shard_map/ppermute | solution.py:805
  132.4 7.6 %collective-permute-start.29 = (bf16[4,128,256]{2,1,0:T(8,128)(2,1)S(1)}, bf16[4,128,256]{2,1,0:T(8,128)(2,1)S(1)}, u32[]{:S(2)}, u32[]{:S(2)}) collective-permute-start(bf16[4,128,256]{2,1,0:T(8,128)(2,1)S(1)} %get-tuple-element.337), channel_id=1, source_target_pairs={{0,1},{1,0},{2,3},{3,2},{4,5},{5,4},{6,7},{7,6},{8,9},{9,8},{10,11... | collective-permute-start | bytes 786440 | tf_op jit(solution)/shard_map/ppermute | solution.py:810
  140.8 11.8 %collective-permute-start.33 = (bf16[4,64,1024]{2,1,0:T(8,128)(2,1)S(1)}, bf16[4,64,1024]{2,1,0:T(8,128)(2,1)S(1)}, u32[]{:S(2)}, u32[]{:S(2)}) collective-permute-start(bf16[4,64,1024]{2,1,0:T(8,128)(2,1)S(1)} %stacked.3.column), channel_id=1, source_target_pairs={{0,2},{2,0},{1,3},{3,1},{4,6},{6,4},{5,7},{7,5},{8,10},{10,8},{9,1... | collective-permute-start | bytes 1572872 | tf_op jit(solution)/shard_map/ppermute | solution.py:805
  140.9 20.2 %collective-permute-start.36 = (bf16[4,64,1024]{2,1,0:T(8,128)(2,1)S(1)}, bf16[4,64,1024]{2,1,0:T(8,128)(2,1)S(1)}, u32[]{:S(2)}, u32[]{:S(2)}) collective-permute-start(bf16[4,64,1024]{2,1,0:T(8,128)(2,1)S(1)} %stacked.3.column), channel_id=1, source_target_pairs={{0,4},{4,0},{1,5},{5,1},{2,6},{6,2},{3,7},{7,3},{8,12},{12,8},{9,1... | collective-permute-start | bytes 1572872 | tf_op jit(solution)/shard_map/ppermute | solution.py:805
  142.0 9.1 %collective-permute-start.34 = (bf16[288,512]{1,0:T(8,128)(2,1)S(1)}, bf16[288,512]{1,0:T(8,128)(2,1)S(1)}, u32[]{:S(2)}, u32[]{:S(2)}) collective-permute-start(bf16[288,512]{1,0:T(8,128)(2,1)S(1)} %get-tuple-element.351.sent), channel_id=1, source_target_pairs={{0,8},{8,0},{16,24},{24,16},{1,9},{9,1},{17,25},{25,17},{2,10},{10... | collective-permute-start | bytes 884744 | tf_op jit(solution)/shard_map/ppermute | solution.py:660
  151.1 9.9 %collective-permute-start.35 = (bf16[160,512]{1,0:T(8,128)(2,1)S(1)}, bf16[160,512]{1,0:T(8,128)(2,1)S(1)}, u32[]{:S(2)}, u32[]{:S(2)}) collective-permute-start(bf16[160,512]{1,0:T(8,128)(2,1)S(1)} %get-tuple-element.364.sent), channel_id=1, source_target_pairs={{0,16},{8,24},{16,0},{24,8},{1,17},{9,25},{17,1},{25,9},{2,18},{10... | collective-permute-start | bytes 491528 | tf_op jit(solution)/shard_map/ppermute | solution.py:660
  161.1 5.3 %collective-permute-start.37 = (bf16[4,64,1024]{2,1,0:T(8,128)(2,1)S(1)}, bf16[4,64,1024]{2,1,0:T(8,128)(2,1)S(1)}, u32[]{:S(2)}, u32[]{:S(2)}) collective-permute-start(bf16[4,64,1024]{2,1,0:T(8,128)(2,1)S(1)} %collective-permute-done.36.column), channel_id=1, source_target_pairs={{0,2},{2,0},{1,3},{3,1},{4,6},{6,4},{5,7},{7,5},{8,10},{10,8},{9,1... | collective-permute-start | bytes 1572872 | tf_op jit(solution)/shard_map/ppermute | solution.py:805
  161.2 6.6 %collective-permute-start.38 = (bf16[160,512]{1,0:T(8,128)(2,1)S(1)}, bf16[160,512]{1,0:T(8,128)(2,1)S(1)}, u32[]{:S(2)}, u32[]{:S(2)}) collective-permute-start(bf16[160,512]{1,0:T(8,128)(2,1)S(1)} %mine.1.refs_0_), channel_id=1, source_target_pairs={{0,1},{1,0},{2,3},{3,2},{4,5},{5,4},{6,7},{7,6},{8,9},{9,8},{10,11... | collective-permute-start | bytes 491528 | tf_op jit(solution)/shard_map/ppermute | solution.py:810
  162.1 5.7 %copy-start.1 = (f32[2,128,512]{2,1,0:T(8,128)S(1)}, f32[2,128,512]{2,1,0:T(8,128)}, u32[]{:S(2)}) copy-start(f32[2,128,512]{2,1,0:T(8,128)} %refs_2_.8) | copy-start | bytes 1572868
  162.1 5.7 %copy-start.7 = (f32[2,128,512]{2,1,0:T(8,128)S(1)}, f32[2,128,512]{2,1,0:T(8,128)}, u32[]{:S(2)}) copy-start(f32[2,128,512]{2,1,0:T(8,128)} %refs_3_.8) | copy-start | bytes 1572868
  162.1 5.7 %copy-start.8 = (f32[2,128,512]{2,1,0:T(8,128)S(1)}, f32[2,128,512]{2,1,0:T(8,128)}, u32[]{:S(2)}) copy-start(f32[2,128,512]{2,1,0:T(8,128)} %refs_4_.1) | copy-start | bytes 1572868
  162.1 5.7 %copy-start.9 = (f32[2,128,512]{2,1,0:T(8,128)S(1)}, f32[2,128,512]{2,1,0:T(8,128)}, u32[]{:S(2)}) copy-start(f32[2,128,512]{2,1,0:T(8,128)} %refs_5_.1) | copy-start | bytes 1572868
  162.1 5.7 %copy-start.10 = (f32[17,512]{1,0:T(8,128)S(1)}, f32[17,512]{1,0:T(8,128)}, u32[]{:S(2)}) copy-start(f32[17,512]{1,0:T(8,128)} %refs_7_.1) | copy-start | bytes 104452
  162.1 5.7 %copy-start.11 = (f32[17,512]{1,0:T(8,128)S(1)}, f32[17,512]{1,0:T(8,128)}, u32[]{:S(2)}) copy-start(f32[17,512]{1,0:T(8,128)} %refs_8_.1) | copy-start | bytes 104452
  162.1 5.7 %copy-start.12 = (f32[17,512]{1,0:T(8,128)S(1)}, f32[17,512]{1,0:T(8,128)}, u32[]{:S(2)}) copy-start(f32[17,512]{1,0:T(8,128)} %refs_9_.3) | copy-start | bytes 104452
  170.4 4.3 %copy-start.13 = (f32[1024]{0:T(1024)S(1)}, f32[1024]{0:T(1024)}, u32[]{:S(2)}) copy-start(f32[1024]{0:T(1024)} %param.39) | copy-start | bytes 12292
  170.4 4.3 %copy-start.14 = (f32[1024]{0:T(1024)S(1)}, f32[1024]{0:T(1024)}, u32[]{:S(2)}) copy-start(f32[1024]{0:T(1024)} %param.37) | copy-start | bytes 12292
  170.4 4.3 %copy-start.15 = (f32[1024]{0:T(1024)S(1)}, f32[1024]{0:T(1024)}, u32[]{:S(2)}) copy-start(f32[1024]{0:T(1024)} %param.38) | copy-start | bytes 12292

commit v2 on v1

--- a/solution.py
+++ b/solution.py
@@ -750,10 +750,11 @@
 
 
 def update_rest_kernel(place, owners, *refs):
-    ways = len(refs) - 18
+    ways = len(refs) - 26
     shares = refs[:ways]
-    attn, small = refs[ways : ways + 4], refs[ways + 4 : ways + 8]
-    attn_out, small_out, bias_out, grads = refs[ways + 8 : ways + 12], refs[ways + 12 : ways + 16], refs[-2], refs[-1]
+    attn, small, hidden = (refs[ways + k : ways + k + 4] for k in (0, 4, 8))
+    attn_out, small_out, hidden_out = (refs[ways + k : ways + k + 4] for k in (12, 16, 20))
+    grads, rows_held = refs[-2:]
     share = shares[0].shape[0] - NSMALL_ROWS
     width = shares[0].shape[1]
     for d in range(ways):
@@ -762,7 +763,18 @@
     new = adamw(*[small[0][...], totals[0:NSMALL]], *[ref[...] for ref in small[1:]], SMALL_RATE, 0.0)
     for out, value in zip(small_out, new):
         out[...] = value
-    bias_out[...] = totals[24:]
+    rows_held[...] = totals[24:]
+    units = hidden[0].shape[1]
+    chunk = min(units, width)
+    for j in range(units // chunk):
+        offset = place[3] * units + j * chunk
+        lanes = pl.ds(pl.multiple_of(offset % width, chunk), chunk)
+        grad = rows_held[pl.ds(offset // width, 1), lanes]
+        here = slice(j * chunk, (j + 1) * chunk)
+        old = [ref[:, here] for ref in hidden]
+        new = adamw(old[0], grad, *old[1:], SMALL_RATE, 0.0)
+        for out, value in zip(hidden_out, new):
+            out[:, here] = value
     seat = (place[0] * 2 + place[1]) * 2 + place[2]
     parts = TILE // share
     held = sum(jnp.where(owners[i] == seat, 1, 0) for i in range(TILES))
@@ -1050,6 +1062,9 @@
     away = [swap(column, "core") for column in columns]
     tiles = columns[:2] + away[:2] + columns[2:] + away[2:]
 
+    halves = half_got[0][None] if ways == 2 else stacked(*half_got)
+    halves, tiles = together(halves, tiles)
+    others = swap(halves, "core")
     weights, query, keys, values, probs, mixed = call(
         attend_kernel,
         "attend",
@@ -1065,9 +1080,7 @@
         8,
         smem=2,
     )(place, owners, *tiles, conv, cols, codes, small_master)
-    half_got, mixed = together(half_got, mixed)
-    halves = half_got[0][None] if ways == 2 else stacked(*half_got)
-    others = swap(halves, "core")
+    others, mixed = together(others, mixed)
     middle, second, second_t = call(
         middle_kernel,
         "middle",
@@ -1289,20 +1302,18 @@
     rest_new = call(
         update_rest_kernel,
         "update_rest",
-        (attn_shape,) * 4 + (small_shape,) * 4 + (in_place((8, width), F32),),
+        (attn_shape,) * 4 + (small_shape,) * 4 + (shape((1, units), F32),) * 4,
         3,
         12,
-        (pltpu.VMEM((ways, share, width), BF16),),
+        (pltpu.VMEM((ways, share, width), BF16), pltpu.VMEM((8, width), F32)),
         smem=2,
     )(
         place, owners, *shares, attn_master, attn_first, attn_second, attn_average,
         small_master, small_first, small_second, small_average,
-    )
-
-    bias_sum = lax.dynamic_slice_in_dim(rest_new[8].reshape(-1), way * units, units, 0)
-    bias_new = adamw(
-        bias_master, bias_sum, bias_first, bias_second, bias_average, SMALL_RATE, 0.0
-    )
+        *[state.reshape(1, units) for state in (bias_master, bias_first, bias_second, bias_average)],
+    )
+
+    bias_new = [part.reshape(units) for part in rest_new[8:]]
     return (
         output,
         in_grad,

time: 176 us -> 173 us (0.983)
  waiting for transfers between devices: 39.9 us -> 37.5 us
  transfers between devices with their start and end apart: 39 -> 39, of which waited for: 17 -> 14; matrix products, arithmetic and copies ran while one was open for 0% -> 0% of each run, Pallas kernels for 37% -> 44%
where the time goes in v2:
time: 173 us
  Pallas kernels  93.4 us (54%)
  starting transfers between devices  39.8 us (23%)
  waiting for transfers between devices  37.5 us (22%)
    pallas_call x29, Pallas kernels, run(): pl.pallas_call(kernel, out_shape=tuple(outs), in_specs=in_smem(smem) + in...  69.6 us
    ppermute x6, waiting for transfers between devices, flipped(): lax.ppermute(array, axis, [(i, i ^ bit) for i in range(lax.axis_size(axis...  26.3 us
    pallas_call x4, Pallas kernels, update_feed(): pl.pallas_call(functools.partial(update_kernel, core_away, y_away), out_s...  16.9 us
    ppermute x12, starting transfers between devices, shifted(): lax.ppermute(array, axis, [(i, (i + distance) % count) for i in range(cou...  14.3 us
    ppermute x19, starting transfers between devices, swap(): return lax.ppermute(array, axis, [(0, 1), (1, 0)])  13 us
    ppermute x6, starting transfers between devices, flipped(): lax.ppermute(array, axis, [(i, i ^ bit) for i in range(lax.axis_size(axis...  7.79 us
    ppermute x19, waiting for transfers between devices, swap(): return lax.ppermute(array, axis, [(0, 1), (1, 0)])  5.82 us
  transfers between devices with their start and end apart: 39, of which 14 were waited for; matrix products, arithmetic and copies ran while one was open for 0% of the time, Pallas kernels for 44%

profile of v2, /device:TPU:0, one launch (start us, length us, event | category | flops | bytes accessed | tf_op | source)
XLA Modules:
  0.0 172.6 jit_solution(12494545112996835180)
XLA Ops:
  0.7 1.1 edges.1
  1.8 3.0 %collective-permute-start.1 = (bf16[128,512]{1,0:T(8,128)(2,1)S(1)}, bf16[128,512]{1,0:T(8,128)(2,1)S(1)}, u32[]{:S(2)}, u32[]{:S(2)}) collective-permute-start(bf16[128,512]{1,0:T(8,128)(2,1)S(1)} %get-tuple-element.219.refs_0_), channel_id=1, source_target_pairs={{0,4},{4,0},{1,5},{5,1},{2,6},{6,2},{3,7},{7,3},{8,12},{12,8},{9,1... | collective-permute-start | bytes 393224 | tf_op jit(solution)/shard_map/ppermute | solution.py:817
  4.8 2.6 %collective-permute-start = (bf16[1,128,512]{2,1,0:T(8,128)(2,1)S(1)}, bf16[1,128,512]{2,1,0:T(8,128)(2,1)S(1)}, u32[]{:S(2)}, u32[]{:S(2)}) collective-permute-start(bf16[1,128,512]{2,1,0:T(8,128)(2,1)S(1)} %bitcast.40), channel_id=1, source_target_pairs={{0,16},{8,24},{16,0},{24,8},{1,17},{9,25},{17,1},{25,9},{2,18},{10... | collective-permute-start | bytes 393224 | tf_op jit(solution)/shard_map/ppermute | solution.py:660
  7.4 3.4 %collective-permute-start.2 = (bf16[48,512]{1,0:T(8,128)(2,1)S(1)}, bf16[48,512]{1,0:T(8,128)(2,1)S(1)}, u32[]{:S(2)}, u32[]{:S(2)}) collective-permute-start(bf16[48,512]{1,0:T(8,128)(2,1)S(1)} %get-tuple-element.220), channel_id=1, source_target_pairs={{0,1},{1,2},{2,3},{3,4},{4,5},{5,6},{6,7},{7,8},{8,9},{9,10},{10,1... | collective-permute-start | bytes 147464 | tf_op jit(solution)/shard_map/ppermute | solution.py:985
  10.8 1.3 collective-permute-start.3
  12.2 1.3 collective-permute-done.second
  13.5 3.3 %collective-permute-done.3.after = bf16[48,512]{1,0:T(8,128)(2,1)S(1)} collective-permute-done((bf16[48,512]{1,0:T(8,128)(2,1)S(1)}, bf16[48,512]{1,0:T(8,128)(2,1)S(1)}, u32[]{:S(2)}, u32[]{:S(2)}) %collective-permute-start.3) | collective-permute-done | bytes 49184 | tf_op jit(solution)/shard_map/ppermute | solution.py:986
  16.8 2.2 %half.1 = bf16[528,1024]{1,0:T(8,128)(2,1)S(1)} custom-call(s32[5]{0:T(128)S(1)} %stack.23.place.refs_0_, f32[2,512,1024]{2,1,0:T(8,128)} %refs_0_.7, f32[1,1024]{1,0:T(1,128)S(1)} %bitcast.42), custom_call_target="tpu_custom_call" | custom-call | flops 1100000000 | bytes 3600000 | tf_op jit(solution)/shard_map/half/pallas_call | solution.py:998
  19.1 1.6 collective-permute-start.5
  20.7 0.7 collective-permute-start.4
  21.4 9.6 %collective-permute-done.5.second = bf16[2,128,512]{2,1,0:T(8,128)(2,1)S(1)} collective-permute-done((bf16[2,128,512]{2,1,0:T(8,128)(2,1)S(1)}, bf16[2,128,512]{2,1,0:T(8,128)(2,1)S(1)}, u32[]{:S(2)}, u32[]{:S(2)}) %collective-permute-start.5) | collective-permute-done | bytes 262176 | tf_op jit(solution)/shard_map/ppermute | solution.py:660
  31.1 4.7 %collective-permute-done.4.second = bf16[1,2,128,512]{3,2,1,0:T(8,128)(2,1)S(1)} collective-permute-done((bf16[1,2,128,512]{3,2,1,0:T(8,128)(2,1)S(1)}, bf16[1,2,128,512]{3,2,1,0:T(8,128)(2,1)S(1)}, u32[]{:S(2)}, u32[]{:S(2)}) %collective-permute-start.4) | collective-permute-done | bytes 262176 | tf_op jit(solution)/shard_map/ppermute | solution.py:660
  35.9 1.2 tables.1
  37.1 6.7 %norm_conv.1 = (bf16[3,1088,512]{2,1,0:T(8,128)(2,1)S(1)}, bf16[1088,512]{1,0:T(8,128)(2,1)S(1)}, bf16[1056,512]{1,0:T(8,128)(2,1)S(1)}, bf16[1056,512]{1,0:T(8,...) custom-call(bf16[48,512]{1,0:T(8,128)(2,1)S(1)} %collective-permute-done.2.before, ...), custom_call_target="tpu_custom_call" | custom-call | flops 550000000 | bytes 1800000 | tf_op jit(solution)/shard_map/norm_conv/pallas_call | solution.py:849
  43.8 2.4 %matrices.1 = bf16[2,512,1024]{2,1,0:T(8,128)(2,1)S(1)} custom-call(f32[2,512,1024]{2,1,0:T(8,128)} %refs_0_.7), custom_call_target="tpu_custom_call" | custom-call | flops 550000000 | bytes 1800000 | tf_op jit(solution)/shard_map/matrices/pallas_call | solution.py:1018
  46.2 3.0 %collective-permute-done.10.second = bf16[2,2,128,512]{3,2,1,0:T(8,128)(2,1)} collective-permute-done((bf16[2,2,128,512]{3,2,1,0:T(8,128)(2,1)S(1)}, bf16[2,2,128,512]{3,2,1,0:T(8,128)(2,1)}, u32[]{:S(2)}, u32[]{:S(2)}) %collective-permute-start.10) | collective-permute-done | bytes 524320 | tf_op jit(solution)/shard_map/ppermute | solution.py:660
  49.3 1.1 joined.7.refs_4_
  50.5 0.5 collective-permute-start.8
  51.1 2.8 %collective-permute-done.8.refs_2_ = bf16[4,128,512]{2,1,0:T(8,128)(2,1)S(1)} collective-permute-done((bf16[4,128,512]{2,1,0:T(8,128)(2,1)S(1)}, bf16[4,128,512]{2,1,0:T(8,128)(2,1)S(1)}, u32[]{:S(2)}, u32[]{:S(2)}) %collective-permute-start.8) | collective-permute-done | bytes 524320 | tf_op jit(solution)/shard_map/ppermute | solution.py:817
  53.9 0.7 collective-permute-done.9.refs_3_
  55.0 7.6 %attend.1 = (bf16[2048,512]{1,0:T(8,128)(2,1)S(1)}, bf16[1088,512]{1,0:T(8,128)(2,1)S(1)}, bf16[1088,512]{1,0:T(8,128)(2,1)S(1)}, bf16[1088,512]{1,0:T(8,128)(2,...) custom-call(s32[5]{0:T(128)S(1)} %copy-done.4, s32[16]{0:T(128)S(1)} %copy-done.6, ...), custom_call_target="tpu_custom_call" | custom-call | flops 550000000 | bytes 1800000 | tf_op jit(solution)/shard_map/attend/pallas_call | solution.py:849
  62.5 1.5 middle.1
  64.0 9.6 %feed.2 = (bf16[1,2,8,32,1024]{4,3,2,1,0:T(8,128)(2,1)S(1)}, bf16[1,2,8,32,1024]{4,3,2,1,0:T(8,128)(2,1)S(1)}, f32[1,1,1024]{2,1,0:T(1,128)S(1)}, f32[1056,512]{1,0:T(8,128)S(1)}, f32[1056,512]{1,0:T(8,128)S(1)}) custom-call(s32[5]{0:T(128)S(1)} %copy-done.4, bf16[1,528,1024]{2,1,0:T(8,128)(2,1)} %bitcast.8.refs_1_, ...), custom_call_target="tpu_custom_call" | custom-call | flops 15399999488 | bytes 50400000 | tf_op jit(solution)/shard_map/feed/pallas_call | solution.py:849
  73.7 0.4 collective-permute-start.13
  74.1 8.7 %feed.3 = (bf16[1,2,8,32,1024]{4,3,2,1,0:T(8,128)(2,1)S(1)}, bf16[1,2,8,32,1024]{4,3,2,1,0:T(8,128)(2,1)S(1)}, f32[1,1,1024]{2,1,0:T(1,128)S(1)}, f32[1056,512]{1,0:T(8,128)S(1)}, f32[1056,512]{1,0:T(8,128)S(1)}) custom-call(s32[5]{0:T(128)S(1)} %copy-done.4, bf16[1,512,1024]{2,1,0:T(8,128)(2,1)S(1)} %get-tuple-element.419.refs_1_, ...), custom_call_target="tpu_custom_call" | custom-call | flops 15399999488 | bytes 50400000 | tf_op jit(solution)/shard_map/feed/pallas_call | solution.py:849
  83.0 0.4 far_sum.1
  83.4 1.6 collective-permute-start.14
  85.1 1.2 collective-permute-start.17
  86.3 4.5 %middle_back.1 = (bf16[1024,512]{1,0:T(8,128)(2,1)}, f32[1024,512]{1,0:T(8,128)S(1)}, bf16[1056,512]{1,0:T(8,128)(2,1)S(1)}, bf16[512,512]{1,0:T(8,128)(2,1)S(1)}, f32[32,512]{1,0:T(8,128)S(1)}) custom-call(f32[1056,512]{1,0:T(8,128)S(1)} %get-tuple-element.247.middle, bf16[1056,512]{1,0:T(8,128)(2,1)S(1)} %get-tuple-element.248.cot, ...), custom_call_target="tpu_custom_call" | custom-call | flops 550000000 | bytes 1800000 | tf_op jit(solution)/shard_map/middle_back/pallas_call | solution.py:849
  90.8 1.3 collective-permute-done.14.refs_5_
  92.1 0.4 near_sum.1
  92.5 1.6 collective-permute-start.18
  94.1 5.8 %scores_back.2 = (bf16[1056,256]{1,0:T(8,128)(2,1)S(1)}, bf16[1056,256]{1,0:T(8,128)(2,1)S(1)}, bf16[1056,256]{1,0:T(8,128)(2,1)S(1)}, bf16[16,128,256]{2,1,0:T(8,128)(2,1)S(1)}, bf16[16,128,256]{2,1,0:T(8,128)(2,1)S(1)}) custom-call(s32[5]{0:T(128)S(1)} %copy-done.4, s32[16]{0:T(128)S(1)} %copy-done.6, bf16[1088,512]{1,0:T(8,128)(2,1)S(1)} %get-tuple-element.267.query, ...), custom_call_target="tpu_custom_call" | custom-call | flops 8800000000 | bytes 28800000 | tf_op jit(solution)/shard_map/scores_back/pallas_call | solution.py:849
  100.3 0.4 feed_two.1
  100.8 1.6 collective-permute-start.19
  102.4 1.2 collective-permute-start.20
  103.6 5.6 %scores_back.3 = (bf16[1056,256]{1,0:T(8,128)(2,1)S(1)}, bf16[1056,256]{1,0:T(8,128)(2,1)S(1)}, bf16[1056,256]{1,0:T(8,128)(2,1)S(1)}, bf16[16,128,256]{2,1,0:T(8,128)(2,1)S(1)}, bf16[16,128,256]{2,1,0:T(8,128)(2,1)S(1)}) custom-call(s32[5]{0:T(128)S(1)} %copy-done.4, s32[16]{0:T(128)S(1)} %copy-done.6, bf16[1088,512]{1,0:T(8,128)(2,1)S(1)} %get-tuple-element.267.query, ...), custom_call_target="tpu_custom_call" | custom-call | flops 8800000000 | bytes 28800000 | tf_op jit(solution)/shard_map/scores_back/pallas_call | solution.py:849
  109.6 0.4 paired.2
  110.4 1.3 collective-permute-start.23
  111.7 2.2 %collective-permute-start.24 = (bf16[64,1024]{1,0:T(8,128)(2,1)S(1)}, bf16[64,1024]{1,0:T(8,128)(2,1)S(1)}, u32[]{:S(2)}, u32[]{:S(2)}) collective-permute-start(bf16[64,1024]{1,0:T(8,128)(2,1)S(1)} %get-tuple-element.334), channel_id=1, source_target_pairs={{0,24},{8,0},{16,8},{24,16},{1,25},{9,1},{17,9},{25,17},{2,26},{10... | collective-permute-start | bytes 393224 | tf_op jit(solution)/shard_map/ppermute | solution.py:822
  113.9 1.1 collective-permute-start.25
  115.0 0.4 paired.3
  115.4 1.7 %collective-permute-start.26 = (bf16[8,128,256]{2,1,0:T(8,128)(2,1)S(1)}, bf16[8,128,256]{2,1,0:T(8,128)(2,1)S(1)}, u32[]{:S(2)}, u32[]{:S(2)}) collective-permute-start(bf16[8,128,256]{2,1,0:T(8,128)(2,1)S(1)} %get-tuple-element.339), channel_id=1, source_target_pairs={{0,4},{4,0},{1,5},{5,1},{2,6},{6,2},{3,7},{7,3},{8,12},{12,8},{9,1... | collective-permute-start | bytes 1572872 | tf_op jit(solution)/shard_map/ppermute | solution.py:817
  117.2 1.9 %conv_grad.1 = f32[3,1056,512]{2,1,0:T(8,128)S(1)} custom-call(bf16[1056,256]{1,0:T(8,128)(2,1)S(1)} %get-tuple-element.313.refs_0_.query_grad_0, bf16[1056,256]{1,0:T(8,128)(2,1)S(1)} %get-tuple-element.324.refs_1_, bf16[1056,256]{1,0:T(8,128)(2,1)S(1)} %get-tuple-element.314.refs_2_.value_grad_0, ...), custom_call_target="tpu_custom_call" | custom-call | flops 22000001024 | bytes 72000000 | tf_op jit(solution)/shard_map/conv_grad/pallas_call | solution.py:849
  119.1 6.6 %conv_back.1 = (f32[1024,512]{1,0:T(8,128)S(1)}, f32[32,512]{1,0:T(8,128)S(1)}) custom-call(s32[5]{0:T(128)S(1)} %copy-done.4, bf16[1056,256]{1,0:T(8,128)(2,1)S(1)} %get-tuple-element.313.refs_0_.query_grad_0, bf16[1056,256]{1,0:T(8,128)(2,1)S(1)} %get-tuple-element.314.refs_2_.value_grad_0, bf16[1056,256]{1,0:T(8,128)(2,1)S(1)} %get-tuple-element.322.refs_3_.query_grad_1, ...), custom_call_target="tpu_custom_call" | custom-call | flops 13200000000 | bytes 43200000 | tf_op jit(solution)/shard_map/conv_back/pallas_call | solution.py:849
  125.8 0.6 collective-permute-start.30
  126.4 1.5 collective-permute-start.31
  128.0 2.8 %collective-permute-start.32 = (bf16[64,1024]{1,0:T(8,128)(2,1)S(1)}, bf16[64,1024]{1,0:T(8,128)(2,1)S(1)}, u32[]{:S(2)}, u32[]{:S(2)}) collective-permute-start(bf16[64,1024]{1,0:T(8,128)(2,1)S(1)} %bitcast.34), channel_id=1, source_target_pairs={{0,24},{8,0},{16,8},{24,16},{1,25},{9,1},{17,9},{25,17},{2,26},{10... | collective-permute-start | bytes 393224 | tf_op jit(solution)/shard_map/ppermute | solution.py:822
  131.1 0.4 collective-permute-start.28
  131.5 0.9 collective-permute-start.29
  132.4 4.6 %in_grad.1 = bf16[1024,512]{1,0:T(8,128)(2,1)} custom-call(f32[1024,512]{1,0:T(8,128)S(1)} %get-tuple-element.347.incoming, bf16[1024,512]{1,0:T(8,128)(2,1)} %frames.5, f32[1024,512]{1,0:T(8,128)S(1)} %get-tuple-element.348.middle_grad, f32[17,512]{1,0:T(8,128)S(1)} %copy-done.2), custom_call_target="tpu_custom_call" | custom-call | flops 22000001024 | bytes 72000000 | tf_op jit(solution)/shard_map/in_grad/pallas_call | solution.py:849
  137.0 2.0 %collective-permute-done.29.refs_1_ = bf16[4,128,256]{2,1,0:T(8,128)(2,1)S(1)} collective-permute-done((bf16[4,128,256]{2,1,0:T(8,128)(2,1)S(1)}, bf16[4,128,256]{2,1,0:T(8,128)(2,1)S(1)}, u32[]{:S(2)}, u32[]{:S(2)}) %collective-permute-start.29) | collective-permute-done | bytes 262176 | tf_op jit(solution)/shard_map/ppermute | solution.py:822
  139.1 0.6 collective-permute-done.28.line_got
  140.0 1.1 collective-permute-start.36
  141.1 1.4 collective-permute-start.34
  142.5 4.2 %update_feed.4 = (f32[2,512,1024]{2,1,0:T(8,128)}, f32[2,512,1024]{2,1,0:T(8,128)}, f32[2,512,1024]{2,1,0:T(8,128)}, f32[2,512,1024]{2,1,0:T(8,128)}) custom-call(s32[5]{0:T(128)S(1)} %copy-done.4, bf16[4,64,1024]{2,1,0:T(8,128)(2,1)S(1)} %stacked.3.column, f32[2,512,1024]{2,1,0:T(8,128)} %refs_0_.7, f32[2,512,1024]{2,1,0:T(8,128)} %refs_1_.7, ...), custom_call_target="tpu_custom_call" | custom-call | flops 330000000 | bytes 1080000 | tf_op jit(solution)/shard_map/update_feed/pallas_call | solution.py:901
  146.7 3.4 %collective-permute-done.34.got = bf16[288,512]{1,0:T(8,128)(2,1)S(1)} collective-permute-done((bf16[288,512]{1,0:T(8,128)(2,1)S(1)}, bf16[288,512]{1,0:T(8,128)(2,1)S(1)}, u32[]{:S(2)}, u32[]{:S(2)}) %collective-permute-start.34) | collective-permute-done | bytes 294944 | tf_op jit(solution)/shard_map/ppermute | solution.py:660
  150.3 1.4 collective-permute-start.35
  151.7 4.2 %update_feed.5 = (f32[2,512,1024]{2,1,0:T(8,128)}, f32[2,512,1024]{2,1,0:T(8,128)}, f32[2,512,1024]{2,1,0:T(8,128)}, f32[2,512,1024]{2,1,0:T(8,128)}) custom-call(s32[5]{0:T(128)S(1)} %copy-done.4, bf16[4,64,1024]{2,1,0:T(8,128)(2,1)S(1)} %collective-permute-done.33.column, ...), custom_call_target="tpu_custom_call", output_to_operand_aliasing={{0}: (6, {}), {1}: (7, {}), {2}: (8, {}), {3}: (9, {})} | custom-call | flops 330000000 | bytes 1080000 | tf_op jit(solution)/shard_map/update_feed/pallas_call | solution.py:901
  155.9 4.3 %collective-permute-done.35.got = bf16[160,512]{1,0:T(8,128)(2,1)S(1)} collective-permute-done((bf16[160,512]{1,0:T(8,128)(2,1)S(1)}, bf16[160,512]{1,0:T(8,128)(2,1)S(1)}, u32[]{:S(2)}, u32[]{:S(2)}) %collective-permute-start.35) | collective-permute-done | bytes 163872 | tf_op jit(solution)/shard_map/ppermute | solution.py:660
  160.3 0.9 collective-permute-start.38
  161.2 4.2 %update_feed.6 = (f32[2,512,1024]{2,1,0:T(8,128)}, f32[2,512,1024]{2,1,0:T(8,128)}, f32[2,512,1024]{2,1,0:T(8,128)}, f32[2,512,1024]{2,1,0:T(8,128)}) custom-call(s32[5]{0:T(128)S(1)} %copy-done.4, bf16[4,64,1024]{2,1,0:T(8,128)(2,1)S(1)} %collective-permute-done.36.column, ...), custom_call_target="tpu_custom_call", output_to_operand_aliasing={{0}: (6, {}), {1}: (7, {}), {2}: (8, {}), {3}: (9, {})} | custom-call | flops 330000000 | bytes 1080000 | tf_op jit(solution)/shard_map/update_feed/pallas_call | solution.py:901
  165.5 4.3 %update_feed.7 = (f32[2,512,1024]{2,1,0:T(8,128)}, f32[2,512,1024]{2,1,0:T(8,128)}, f32[2,512,1024]{2,1,0:T(8,128)}, f32[2,512,1024]{2,1,0:T(8,128)}) custom-call(s32[5]{0:T(128)S(1)} %copy-done.4, bf16[4,64,1024]{2,1,0:T(8,128)(2,1)S(1)} %collective-permute-done.37.column, ...), custom_call_target="tpu_custom_call", output_to_operand_aliasing={{0}: (6, {}), {1}: (7, {}), {2}: (8, {}), {3}: (9, {})} | custom-call | flops 330000000 | bytes 1080000 | tf_op jit(solution)/shard_map/update_feed/pallas_call | solution.py:901
  169.9 2.5 %update_rest.1 = (f32[2,128,512]{2,1,0:T(8,128)}, f32[2,128,512]{2,1,0:T(8,128)}, f32[2,128,512]{2,1,0:T(8,128)}, f32[2,128,512]{2,1,0:T(8,128)}, f32[17,512]{1,...) custom-call(s32[5]{0:T(128)S(1)} %copy-done.4, ...), custom_call_target="tpu_custom_call" | custom-call | flops 3300000000 | bytes 10800000 | tf_op jit(solution)/shard_map/update_rest/pallas_call | solution.py:849
  (85 shorter events, 3.1 us)
Async XLA Ops:
  0.7 16.1 %copy-start.5 = (f32[1024]{0:T(1024)S(1)}, f32[1024]{0:T(1024)}, u32[]{:S(2)}) copy-start(f32[1024]{0:T(1024)} %param.36) | copy-start | bytes 12292
  1.8 10.4 %collective-permute-start.1 = (bf16[128,512]{1,0:T(8,128)(2,1)S(1)}, bf16[128,512]{1,0:T(8,128)(2,1)S(1)}, u32[]{:S(2)}, u32[]{:S(2)}) collective-permute-start(bf16[128,512]{1,0:T(8,128)(2,1)S(1)} %get-tuple-element.219.refs_0_), channel_id=1, source_target_pairs={{0,4},{4,0},{1,5},{5,1},{2,6},{6,2},{3,7},{7,3},{8,12},{12,8},{9,1... | collective-permute-start | bytes 393224 | tf_op jit(solution)/shard_map/ppermute | solution.py:817
  4.8 8.7 %collective-permute-start = (bf16[1,128,512]{2,1,0:T(8,128)(2,1)S(1)}, bf16[1,128,512]{2,1,0:T(8,128)(2,1)S(1)}, u32[]{:S(2)}, u32[]{:S(2)}) collective-permute-start(bf16[1,128,512]{2,1,0:T(8,128)(2,1)S(1)} %bitcast.40), channel_id=1, source_target_pairs={{0,16},{8,24},{16,0},{24,8},{1,17},{9,25},{17,1},{25,9},{2,18},{10... | collective-permute-start | bytes 393224 | tf_op jit(solution)/shard_map/ppermute | solution.py:660
  7.4 6.1 %collective-permute-start.2 = (bf16[48,512]{1,0:T(8,128)(2,1)S(1)}, bf16[48,512]{1,0:T(8,128)(2,1)S(1)}, u32[]{:S(2)}, u32[]{:S(2)}) collective-permute-start(bf16[48,512]{1,0:T(8,128)(2,1)S(1)} %get-tuple-element.220), channel_id=1, source_target_pairs={{0,1},{1,2},{2,3},{3,4},{4,5},{5,6},{6,7},{7,8},{8,9},{9,10},{10,1... | collective-permute-start | bytes 147464 | tf_op jit(solution)/shard_map/ppermute | solution.py:985
  10.8 6.0 %collective-permute-start.3 = (bf16[48,512]{1,0:T(8,128)(2,1)S(1)}, bf16[48,512]{1,0:T(8,128)(2,1)S(1)}, u32[]{:S(2)}, u32[]{:S(2)}) collective-permute-start(bf16[48,512]{1,0:T(8,128)(2,1)S(1)} %get-tuple-element.221), channel_id=1, source_target_pairs={{1,0},{2,1},{3,2},{4,3},{5,4},{6,5},{7,6},{8,7},{9,8},{10,9},{11,1... | collective-permute-start | bytes 147464 | tf_op jit(solution)/shard_map/ppermute | solution.py:986
  12.2 6.8 %copy-start.3 = (s32[5]{0:T(128)}, s32[5]{0:T(128)S(1)}, u32[]{:S(2)}) copy-start(s32[5]{0:T(128)S(1)} %stack.23.place.refs_0_) | copy-start | bytes 64
  19.0 27.2 %collective-permute-start.7 = (bf16[528,1024]{1,0:T(8,128)(2,1)S(1)}, bf16[528,1024]{1,0:T(8,128)(2,1)}, u32[]{:S(2)}, u32[]{:S(2)}) collective-permute-start(bf16[528,1024]{1,0:T(8,128)(2,1)S(1)} %half.1), channel_id=1, source_target_pairs={{0,1},{1,0},{2,3},{3,2},{4,5},{5,4},{6,7},{7,6},{8,9},{9,8},{10,11... | collective-permute-start | bytes 3244040 | tf_op jit(solution)/shard_map/ppermute | solution.py:822
  19.1 11.9 %collective-permute-start.5 = (bf16[2,128,512]{2,1,0:T(8,128)(2,1)S(1)}, bf16[2,128,512]{2,1,0:T(8,128)(2,1)S(1)}, u32[]{:S(2)}, u32[]{:S(2)}) collective-permute-start(bf16[2,128,512]{2,1,0:T(8,128)(2,1)S(1)} %joined.4.first), channel_id=1, source_target_pairs={{0,8},{8,0},{16,24},{24,16},{1,9},{9,1},{17,25},{25,17},{2,10},{10... | collective-permute-start | bytes 786440 | tf_op jit(solution)/shard_map/ppermute | solution.py:660
  20.7 15.1 %collective-permute-start.4 = (bf16[1,2,128,512]{3,2,1,0:T(8,128)(2,1)S(1)}, bf16[1,2,128,512]{3,2,1,0:T(8,128)(2,1)S(1)}, u32[]{:S(2)}, u32[]{:S(2)}) collective-permute-start(bf16[1,2,128,512]{3,2,1,0:T(8,128)(2,1)S(1)} %bitcast.30), channel_id=1, source_target_pairs={{0,16},{8,24},{16,0},{24,8},{1,17},{9,25},{17,1},{25,9},{2,18},{10... | collective-permute-start | bytes 786440 | tf_op jit(solution)/shard_map/ppermute | solution.py:660
  31.0 15.2 %collective-permute-start.6 = (bf16[4,128,512]{2,1,0:T(8,128)(2,1)S(1)}, bf16[4,128,512]{2,1,0:T(8,128)(2,1)S(1)}, u32[]{:S(2)}, u32[]{:S(2)}) collective-permute-start(bf16[4,128,512]{2,1,0:T(8,128)(2,1)S(1)} %joined.6.refs_0_), channel_id=1, source_target_pairs={{0,4},{4,0},{1,5},{5,1},{2,6},{6,2},{3,7},{7,3},{8,12},{12,8},{9,1... | collective-permute-start | bytes 1572872 | tf_op jit(solution)/shard_map/ppermute | solution.py:817
  35.8 1.3 copy-start.2
  35.8 13.5 %collective-permute-start.10 = (bf16[2,2,128,512]{3,2,1,0:T(8,128)(2,1)S(1)}, bf16[2,2,128,512]{3,2,1,0:T(8,128)(2,1)}, u32[]{:S(2)}, u32[]{:S(2)}) collective-permute-start(bf16[2,2,128,512]{3,2,1,0:T(8,128)(2,1)S(1)} %joined.5.first), channel_id=1, source_target_pairs={{0,8},{8,0},{16,24},{24,16},{1,9},{9,1},{17,25},{25,17},{2,10},{10... | collective-permute-start | bytes 1572872 | tf_op jit(solution)/shard_map/ppermute | solution.py:660
  50.4 4.6 %copy-start.4 = (s32[5]{0:T(128)S(1)}, s32[5]{0:T(128)}, u32[]{:S(2)}) copy-start(s32[5]{0:T(128)} %copy-done.3) | copy-start | bytes 64
  50.4 4.6 %copy-start.6 = (s32[16]{0:T(128)S(1)}, s32[16]{0:T(128)}, u32[]{:S(2)}) copy-start(s32[16]{0:T(128)} %owners.7) | copy-start | bytes 196
  50.4 4.2 %collective-permute-start.11 = (bf16[4,2,128,512]{3,2,1,0:T(8,128)(2,1)S(1)}, bf16[4,2,128,512]{3,2,1,0:T(8,128)(2,1)S(1)}, u32[]{:S(2)}, u32[]{:S(2)}) collective-permute-start(bf16[4,2,128,512]{3,2,1,0:T(8,128)(2,1)S(1)} %joined.7.refs_4_), channel_id=1, source_target_pairs={{0,2},{2,0},{1,3},{3,1},{4,6},{6,4},{5,7},{7,5},{8,10},{10,8},{9,1... | collective-permute-start | bytes 3145736 | tf_op jit(solution)/shard_map/ppermute | solution.py:817
  50.5 3.4 %collective-permute-start.8 = (bf16[4,128,512]{2,1,0:T(8,128)(2,1)S(1)}, bf16[4,128,512]{2,1,0:T(8,128)(2,1)S(1)}, u32[]{:S(2)}, u32[]{:S(2)}) collective-permute-start(bf16[4,128,512]{2,1,0:T(8,128)(2,1)S(1)} %joined.6.refs_0_), channel_id=1, source_target_pairs={{0,2},{2,0},{1,3},{3,1},{4,6},{6,4},{5,7},{7,5},{8,10},{10,8},{9,1... | collective-permute-start | bytes 1572872 | tf_op jit(solution)/shard_map/ppermute | solution.py:817
  51.0 3.6 %collective-permute-start.9 = (bf16[4,128,512]{2,1,0:T(8,128)(2,1)S(1)}, bf16[4,128,512]{2,1,0:T(8,128)(2,1)S(1)}, u32[]{:S(2)}, u32[]{:S(2)}) collective-permute-start(bf16[4,128,512]{2,1,0:T(8,128)(2,1)S(1)} %collective-permute-done.6.refs_1_), channel_id=1, source_target_pairs={{0,2},{2,0},{1,3},{3,1},{4,6},{6,4},{5,7},{7,5},{8,10},{10,8},{9,1... | collective-permute-start | bytes 1572872 | tf_op jit(solution)/shard_map/ppermute | solution.py:817
  54.6 7.9 %collective-permute-start.12 = (bf16[1,528,1024]{2,1,0:T(8,128)(2,1)}, bf16[1,528,1024]{2,1,0:T(8,128)(2,1)S(1)}, u32[]{:S(2)}, u32[]{:S(2)}) collective-permute-start(bf16[1,528,1024]{2,1,0:T(8,128)(2,1)} %bitcast.8.refs_1_), channel_id=1, source_target_pairs={{0,2},{2,0},{1,3},{3,1},{4,6},{6,4},{5,7},{7,5},{8,10},{10,8},{9,1... | collective-permute-start | bytes 3244040 | tf_op jit(solution)/shard_map/ppermute | solution.py:817
  73.7 9.3 %collective-permute-start.13 = (bf16[1,2,8,32,1024]{4,3,2,1,0:T(8,128)(2,1)S(1)}, bf16[1,2,8,32,1024]{4,3,2,1,0:T(8,128)(2,1)S(1)}, u32[]{:S(2)}, u32[]{:S(2)}) collective-permute-start(bf16[1,2,8,32,1024]{4,3,2,1,0:T(8,128)(2,1)S(1)} %get-tuple-element.255), channel_id=1, source_target_pairs={{0,2},{2,0},{1,3},{3,1},{4,6},{6,4},{5,7},{7,5},{8,10},{10,8},{9,1... | collective-permute-start | bytes 3145736 | tf_op jit(solution)/shard_map/ppermute | solution.py:817
  82.8 9.3 %collective-permute-start.15 = (bf16[1,2,8,32,1024]{4,3,2,1,0:T(8,128)(2,1)S(1)}, bf16[1,2,8,32,1024]{4,3,2,1,0:T(8,128)(2,1)S(1)}, u32[]{:S(2)}, u32[]{:S(2)}) collective-permute-start(bf16[1,2,8,32,1024]{4,3,2,1,0:T(8,128)(2,1)S(1)} %get-tuple-element.275), channel_id=1, source_target_pairs={{0,2},{2,0},{1,3},{3,1},{4,6},{6,4},{5,7},{7,5},{8,10},{10,8},{9,1... | collective-permute-start | bytes 3145736 | tf_op jit(solution)/shard_map/ppermute | solution.py:817
  83.4 8.6 %collective-permute-start.14 = (bf16[4,32,1024]{2,1,0:T(8,128)(2,1)S(1)}, bf16[4,32,1024]{2,1,0:T(8,128)(2,1)S(1)}, u32[]{:S(2)}, u32[]{:S(2)}) collective-permute-start(bf16[4,32,1024]{2,1,0:T(8,128)(2,1)S(1)} %get-tuple-element.273), channel_id=1, source_target_pairs={{0,4},{4,0},{1,5},{5,1},{2,6},{6,2},{3,7},{7,3},{8,12},{12,8},{9,1... | collective-permute-start | bytes 786440 | tf_op jit(solution)/shard_map/ppermute | solution.py:817
  85.1 15.0 %collective-permute-start.17 = (bf16[8,32,1024]{2,1,0:T(8,128)(2,1)S(1)}, bf16[8,32,1024]{2,1,0:T(8,128)(2,1)S(1)}, u32[]{:S(2)}, u32[]{:S(2)}) collective-permute-start(bf16[8,32,1024]{2,1,0:T(8,128)(2,1)S(1)} %get-tuple-element.287), channel_id=1, source_target_pairs={{0,1},{1,0},{2,3},{3,2},{4,5},{5,4},{6,7},{7,6},{8,9},{9,8},{10,11... | collective-permute-start | bytes 1572872 | tf_op jit(solution)/shard_map/ppermute | solution.py:822
  92.5 7.8 %collective-permute-start.18 = (bf16[4,32,1024]{2,1,0:T(8,128)(2,1)S(1)}, bf16[4,32,1024]{2,1,0:T(8,128)(2,1)S(1)}, u32[]{:S(2)}, u32[]{:S(2)}) collective-permute-start(bf16[4,32,1024]{2,1,0:T(8,128)(2,1)S(1)} %get-tuple-element.289), channel_id=1, source_target_pairs={{0,4},{4,0},{1,5},{5,1},{2,6},{6,2},{3,7},{7,3},{8,12},{12,8},{9,1... | collective-permute-start | bytes 786440 | tf_op jit(solution)/shard_map/ppermute | solution.py:817
  99.9 9.6 %collective-permute-start.16 = (bf16[16,128,256]{2,1,0:T(8,128)(2,1)S(1)}, bf16[16,128,256]{2,1,0:T(8,128)(2,1)S(1)}, u32[]{:S(2)}, u32[]{:S(2)}) collective-permute-start(bf16[16,128,256]{2,1,0:T(8,128)(2,1)S(1)} %get-tuple-element.283), channel_id=1, source_target_pairs={{0,2},{2,0},{1,3},{3,1},{4,6},{6,4},{5,7},{7,5},{8,10},{10,8},{9,1... | collective-permute-start | bytes 3145736 | tf_op jit(solution)/shard_map/ppermute | solution.py:817
  100.8 8.5 %collective-permute-start.19 = (bf16[4,32,1024]{2,1,0:T(8,128)(2,1)S(1)}, bf16[4,32,1024]{2,1,0:T(8,128)(2,1)S(1)}, u32[]{:S(2)}, u32[]{:S(2)}) collective-permute-start(bf16[4,32,1024]{2,1,0:T(8,128)(2,1)S(1)} %get-tuple-element.300), channel_id=1, source_target_pairs={{0,4},{4,0},{1,5},{5,1},{2,6},{6,2},{3,7},{7,3},{8,12},{12,8},{9,1... | collective-permute-start | bytes 786440 | tf_op jit(solution)/shard_map/ppermute | solution.py:817
  102.4 7.0 %collective-permute-start.20 = (bf16[4,32,1024]{2,1,0:T(8,128)(2,1)S(1)}, bf16[4,32,1024]{2,1,0:T(8,128)(2,1)S(1)}, u32[]{:S(2)}, u32[]{:S(2)}) collective-permute-start(bf16[4,32,1024]{2,1,0:T(8,128)(2,1)S(1)} %get-tuple-element.302), channel_id=1, source_target_pairs={{0,1},{1,0},{2,3},{3,2},{4,5},{5,4},{6,7},{7,6},{8,9},{9,8},{10,11... | collective-permute-start | bytes 786440 | tf_op jit(solution)/shard_map/ppermute | solution.py:822
  109.2 5.8 %collective-permute-start.21 = (bf16[16,128,256]{2,1,0:T(8,128)(2,1)S(1)}, bf16[16,128,256]{2,1,0:T(8,128)(2,1)S(1)}, u32[]{:S(2)}, u32[]{:S(2)}) collective-permute-start(bf16[16,128,256]{2,1,0:T(8,128)(2,1)S(1)} %get-tuple-element.316), channel_id=1, source_target_pairs={{0,2},{2,0},{1,3},{3,1},{4,6},{6,4},{5,7},{7,5},{8,10},{10,8},{9,1... | collective-permute-start | bytes 3145736 | tf_op jit(solution)/shard_map/ppermute | solution.py:817
  110.0 15.6 %collective-permute-start.22 = (bf16[64,1024]{1,0:T(8,128)(2,1)S(1)}, bf16[64,1024]{1,0:T(8,128)(2,1)S(1)}, u32[]{:S(2)}, u32[]{:S(2)}) collective-permute-start(bf16[64,1024]{1,0:T(8,128)(2,1)S(1)} %get-tuple-element.332), channel_id=1, source_target_pairs={{0,8},{8,16},{16,24},{24,0},{1,9},{9,17},{17,25},{25,1},{2,10},{10... | collective-permute-start | bytes 393224 | tf_op jit(solution)/shard_map/ppermute | solution.py:822
  110.4 15.4 %collective-permute-start.23 = (bf16[64,1024]{1,0:T(8,128)(2,1)S(1)}, bf16[64,1024]{1,0:T(8,128)(2,1)S(1)}, u32[]{:S(2)}, u32[]{:S(2)}) collective-permute-start(bf16[64,1024]{1,0:T(8,128)(2,1)S(1)} %get-tuple-element.333), channel_id=1, source_target_pairs={{0,16},{8,24},{16,0},{24,8},{1,17},{9,25},{17,1},{25,9},{2,18},{10... | collective-permute-start | bytes 393224 | tf_op jit(solution)/shard_map/ppermute | solution.py:822
  111.7 14.0 %collective-permute-start.24 = (bf16[64,1024]{1,0:T(8,128)(2,1)S(1)}, bf16[64,1024]{1,0:T(8,128)(2,1)S(1)}, u32[]{:S(2)}, u32[]{:S(2)}) collective-permute-start(bf16[64,1024]{1,0:T(8,128)(2,1)S(1)} %get-tuple-element.334), channel_id=1, source_target_pairs={{0,24},{8,0},{16,8},{24,16},{1,25},{9,1},{17,9},{25,17},{2,26},{10... | collective-permute-start | bytes 393224 | tf_op jit(solution)/shard_map/ppermute | solution.py:822
  113.9 16.9 %collective-permute-start.25 = (bf16[8,128,256]{2,1,0:T(8,128)(2,1)S(1)}, bf16[8,128,256]{2,1,0:T(8,128)(2,1)S(1)}, u32[]{:S(2)}, u32[]{:S(2)}) collective-permute-start(bf16[8,128,256]{2,1,0:T(8,128)(2,1)S(1)} %get-tuple-element.337), channel_id=1, source_target_pairs={{0,1},{1,0},{2,3},{3,2},{4,5},{5,4},{6,7},{7,6},{8,9},{9,8},{10,11... | collective-permute-start | bytes 1572872 | tf_op jit(solution)/shard_map/ppermute | solution.py:822
  115.4 3.6 %copy-start = (bf16[1024,512]{1,0:T(8,128)(2,1)S(1)}, bf16[1024,512]{1,0:T(8,128)(2,1)}, u32[]{:S(2)}) copy-start(bf16[1024,512]{1,0:T(8,128)(2,1)} %frames.5) | copy-start | bytes 3145732
  115.4 15.4 %collective-permute-start.26 = (bf16[8,128,256]{2,1,0:T(8,128)(2,1)S(1)}, bf16[8,128,256]{2,1,0:T(8,128)(2,1)S(1)}, u32[]{:S(2)}, u32[]{:S(2)}) collective-permute-start(bf16[8,128,256]{2,1,0:T(8,128)(2,1)S(1)} %get-tuple-element.339), channel_id=1, source_target_pairs={{0,4},{4,0},{1,5},{5,1},{2,6},{6,2},{3,7},{7,3},{8,12},{12,8},{9,1... | collective-permute-start | bytes 1572872 | tf_op jit(solution)/shard_map/ppermute | solution.py:817
  125.6 2.3 %collective-permute-start.27 = (f32[32,512]{1,0:T(8,128)S(1)}, f32[32,512]{1,0:T(8,128)S(1)}, u32[]{:S(2)}, u32[]{:S(2)}) collective-permute-start(f32[32,512]{1,0:T(8,128)S(1)} %get-tuple-element.340.refs_4_), channel_id=1, source_target_pairs={{0,2},{2,0},{1,3},{3,1},{4,6},{6,4},{5,7},{7,5},{8,10},{10,8},{9,1... | collective-permute-start | bytes 196616 | tf_op jit(solution)/shard_map/ppermute | solution.py:817
  125.8 14.0 %collective-permute-start.30 = (bf16[64,1024]{1,0:T(8,128)(2,1)S(1)}, bf16[64,1024]{1,0:T(8,128)(2,1)S(1)}, u32[]{:S(2)}, u32[]{:S(2)}) collective-permute-start(bf16[64,1024]{1,0:T(8,128)(2,1)S(1)} %bitcast.32), channel_id=1, source_target_pairs={{0,8},{8,16},{16,24},{24,0},{1,9},{9,17},{17,25},{25,1},{2,10},{10... | collective-permute-start | bytes 393224 | tf_op jit(solution)/shard_map/ppermute | solution.py:822
  126.4 13.4 %collective-permute-start.31 = (bf16[64,1024]{1,0:T(8,128)(2,1)S(1)}, bf16[64,1024]{1,0:T(8,128)(2,1)S(1)}, u32[]{:S(2)}, u32[]{:S(2)}) collective-permute-start(bf16[64,1024]{1,0:T(8,128)(2,1)S(1)} %bitcast.33), channel_id=1, source_target_pairs={{0,16},{8,24},{16,0},{24,8},{1,17},{9,25},{17,1},{25,9},{2,18},{10... | collective-permute-start | bytes 393224 | tf_op jit(solution)/shard_map/ppermute | solution.py:822
  128.0 11.9 %collective-permute-start.32 = (bf16[64,1024]{1,0:T(8,128)(2,1)S(1)}, bf16[64,1024]{1,0:T(8,128)(2,1)S(1)}, u32[]{:S(2)}, u32[]{:S(2)}) collective-permute-start(bf16[64,1024]{1,0:T(8,128)(2,1)S(1)} %bitcast.34), channel_id=1, source_target_pairs={{0,24},{8,0},{16,8},{24,16},{1,25},{9,1},{17,9},{25,17},{2,26},{10... | collective-permute-start | bytes 393224 | tf_op jit(solution)/shard_map/ppermute | solution.py:822
  131.1 8.6 %collective-permute-start.28 = (bf16[576,256]{1,0:T(8,128)(2,1)S(1)}, bf16[576,256]{1,0:T(8,128)(2,1)S(1)}, u32[]{:S(2)}, u32[]{:S(2)}) collective-permute-start(bf16[576,256]{1,0:T(8,128)(2,1)S(1)} %get-tuple-element.352.line), channel_id=1, source_target_pairs={{0,4},{4,0},{1,5},{5,1},{2,6},{6,2},{3,7},{7,3},{8,12},{12,8},{9,1... | collective-permute-start | bytes 884744 | tf_op jit(solution)/shard_map/ppermute | solution.py:817
  131.5 7.6 %collective-permute-start.29 = (bf16[4,128,256]{2,1,0:T(8,128)(2,1)S(1)}, bf16[4,128,256]{2,1,0:T(8,128)(2,1)S(1)}, u32[]{:S(2)}, u32[]{:S(2)}) collective-permute-start(bf16[4,128,256]{2,1,0:T(8,128)(2,1)S(1)} %get-tuple-element.354), channel_id=1, source_target_pairs={{0,1},{1,0},{2,3},{3,2},{4,5},{5,4},{6,7},{7,6},{8,9},{9,8},{10,11... | collective-permute-start | bytes 786440 | tf_op jit(solution)/shard_map/ppermute | solution.py:822
  139.9 11.8 %collective-permute-start.33 = (bf16[4,64,1024]{2,1,0:T(8,128)(2,1)S(1)}, bf16[4,64,1024]{2,1,0:T(8,128)(2,1)S(1)}, u32[]{:S(2)}, u32[]{:S(2)}) collective-permute-start(bf16[4,64,1024]{2,1,0:T(8,128)(2,1)S(1)} %stacked.3.column), channel_id=1, source_target_pairs={{0,2},{2,0},{1,3},{3,1},{4,6},{6,4},{5,7},{7,5},{8,10},{10,8},{9,1... | collective-permute-start | bytes 1572872 | tf_op jit(solution)/shard_map/ppermute | solution.py:817
  140.0 20.2 %collective-permute-start.36 = (bf16[4,64,1024]{2,1,0:T(8,128)(2,1)S(1)}, bf16[4,64,1024]{2,1,0:T(8,128)(2,1)S(1)}, u32[]{:S(2)}, u32[]{:S(2)}) collective-permute-start(bf16[4,64,1024]{2,1,0:T(8,128)(2,1)S(1)} %stacked.3.column), channel_id=1, source_target_pairs={{0,4},{4,0},{1,5},{5,1},{2,6},{6,2},{3,7},{7,3},{8,12},{12,8},{9,1... | collective-permute-start | bytes 1572872 | tf_op jit(solution)/shard_map/ppermute | solution.py:817
  141.1 9.1 %collective-permute-start.34 = (bf16[288,512]{1,0:T(8,128)(2,1)S(1)}, bf16[288,512]{1,0:T(8,128)(2,1)S(1)}, u32[]{:S(2)}, u32[]{:S(2)}) collective-permute-start(bf16[288,512]{1,0:T(8,128)(2,1)S(1)} %get-tuple-element.368.sent), channel_id=1, source_target_pairs={{0,8},{8,0},{16,24},{24,16},{1,9},{9,1},{17,25},{25,17},{2,10},{10... | collective-permute-start | bytes 884744 | tf_op jit(solution)/shard_map/ppermute | solution.py:660
  150.3 9.9 %collective-permute-start.35 = (bf16[160,512]{1,0:T(8,128)(2,1)S(1)}, bf16[160,512]{1,0:T(8,128)(2,1)S(1)}, u32[]{:S(2)}, u32[]{:S(2)}) collective-permute-start(bf16[160,512]{1,0:T(8,128)(2,1)S(1)} %get-tuple-element.381.sent), channel_id=1, source_target_pairs={{0,16},{8,24},{16,0},{24,8},{1,17},{9,25},{17,1},{25,9},{2,18},{10... | collective-permute-start | bytes 491528 | tf_op jit(solution)/shard_map/ppermute | solution.py:660
  160.2 5.2 %collective-permute-start.37 = (bf16[4,64,1024]{2,1,0:T(8,128)(2,1)S(1)}, bf16[4,64,1024]{2,1,0:T(8,128)(2,1)S(1)}, u32[]{:S(2)}, u32[]{:S(2)}) collective-permute-start(bf16[4,64,1024]{2,1,0:T(8,128)(2,1)S(1)} %collective-permute-done.36.column), channel_id=1, source_target_pairs={{0,2},{2,0},{1,3},{3,1},{4,6},{6,4},{5,7},{7,5},{8,10},{10,8},{9,1... | collective-permute-start | bytes 1572872 | tf_op jit(solution)/shard_map/ppermute | solution.py:817
  160.3 9.5 %collective-permute-start.38 = (bf16[160,512]{1,0:T(8,128)(2,1)S(1)}, bf16[160,512]{1,0:T(8,128)(2,1)S(1)}, u32[]{:S(2)}, u32[]{:S(2)}) collective-permute-start(bf16[160,512]{1,0:T(8,128)(2,1)S(1)} %mine.1.refs_0_), channel_id=1, source_target_pairs={{0,1},{1,0},{2,3},{3,2},{4,5},{5,4},{6,7},{7,6},{8,9},{9,8},{10,11... | collective-permute-start | bytes 491528 | tf_op jit(solution)/shard_map/ppermute | solution.py:822
  165.4 4.4 %copy-start.1 = (f32[2,128,512]{2,1,0:T(8,128)S(1)}, f32[2,128,512]{2,1,0:T(8,128)}, u32[]{:S(2)}) copy-start(f32[2,128,512]{2,1,0:T(8,128)} %refs_2_.8) | copy-start | bytes 1572868
  165.4 4.4 %copy-start.7 = (f32[2,128,512]{2,1,0:T(8,128)S(1)}, f32[2,128,512]{2,1,0:T(8,128)}, u32[]{:S(2)}) copy-start(f32[2,128,512]{2,1,0:T(8,128)} %refs_3_.8) | copy-start | bytes 1572868
  165.4 4.4 %copy-start.8 = (f32[2,128,512]{2,1,0:T(8,128)S(1)}, f32[2,128,512]{2,1,0:T(8,128)}, u32[]{:S(2)}) copy-start(f32[2,128,512]{2,1,0:T(8,128)} %refs_4_.1) | copy-start | bytes 1572868
  165.5 4.4 %copy-start.9 = (f32[2,128,512]{2,1,0:T(8,128)S(1)}, f32[2,128,512]{2,1,0:T(8,128)}, u32[]{:S(2)}) copy-start(f32[2,128,512]{2,1,0:T(8,128)} %refs_5_.1) | copy-start | bytes 1572868
  165.5 4.4 %copy-start.10 = (f32[17,512]{1,0:T(8,128)S(1)}, f32[17,512]{1,0:T(8,128)}, u32[]{:S(2)}) copy-start(f32[17,512]{1,0:T(8,128)} %refs_7_.1) | copy-start | bytes 104452
  165.5 4.4 %copy-start.11 = (f32[17,512]{1,0:T(8,128)S(1)}, f32[17,512]{1,0:T(8,128)}, u32[]{:S(2)}) copy-start(f32[17,512]{1,0:T(8,128)} %refs_8_.1) | copy-start | bytes 104452
  165.5 4.4 %copy-start.12 = (f32[17,512]{1,0:T(8,128)S(1)}, f32[17,512]{1,0:T(8,128)}, u32[]{:S(2)}) copy-start(f32[17,512]{1,0:T(8,128)} %refs_9_.3) | copy-start | bytes 104452
  165.5 4.4 %copy-start.13 = (f32[1024]{0:T(1024)S(1)}, f32[1024]{0:T(1024)}, u32[]{:S(2)}) copy-start(f32[1024]{0:T(1024)} %param.37) | copy-start | bytes 12292
  165.5 4.4 %copy-start.14 = (f32[1024]{0:T(1024)S(1)}, f32[1024]{0:T(1024)}, u32[]{:S(2)}) copy-start(f32[1024]{0:T(1024)} %param.38) | copy-start | bytes 12292
  165.5 4.4 %copy-start.15 = (f32[1024]{0:T(1024)S(1)}, f32[1024]{0:T(1024)}, u32[]{:S(2)}) copy-start(f32[1024]{0:T(1024)} %param.39) | copy-start | bytes 12292

commit v3 on v2

--- a/solution.py
+++ b/solution.py
@@ -218,6 +218,11 @@
         cols_out[c * 128 : c * 128 + size, :] = columns[0:size]
 
 
+def slot_of(owners, i):
+    owner = owners[i]
+    return owner, sum(jnp.where((owners[j] == owner) & (j < i), 1, 0) for j in range(TILES))
+
+
 def slots_of(owners):
     found = [owners[i] for i in range(TILES)]
     return [
@@ -237,17 +242,19 @@
 def attend_kernel(
     place, owners, *refs
 ):
-    tiles, refs = (refs[:6], refs[6:])
+    tiles, refs = (refs[:8], refs[8:])
     conv, cols, codes, small, *refs = refs
     weights_out, query_out, key_out, value_out, probs_out, mixed_out = refs
     rows, width = mixed_out.shape
     wide = conv.shape[1]
     depth = tiles[0].shape[0]
-    for i, (owner, slot) in enumerate(slots_of(owners)):
-        spot = pl.ds(i * TILE, TILE)
+    def tile_step(i, carry):
+        owner, slot = slot_of(owners, i)
+        spot = pl.ds(pl.multiple_of(i * TILE, TILE), TILE)
         core_away = (owner + place[2]) % 2
         y_away = (owner // 2 + place[1]) % 2
         z_away = place_of(place[0] ^ (owner // 4), depth)
+        late = z_away // (depth // 2)
         for r, source in enumerate(tiles[:4]):
 
             @pl.when((slot == 0) & (core_away * 2 + y_away == r))
@@ -256,9 +263,13 @@
 
         for r, source in enumerate(tiles[4:]):
 
-            @pl.when((slot == 1) & (core_away == r))
+            @pl.when((slot == 1) & (core_away * 2 + late == r))
             def _(source=source):
-                weights_out[spot, :] = source[z_away, y_away]
+                weights_out[spot, :] = source[z_away % (depth // 2), y_away]
+
+        return carry
+
+    lax.fori_loop(0, TILES, tile_step, 0)
 
     def matrix(c):
         return weights_out[c * width : (c + 1) * width, :]
@@ -1054,13 +1065,11 @@
         fetched=(1, 3),
     )(before, frames, after, cotangent, cols, small_master)
 
-    column_b, column_a_y, conv, half_got, low_mlp = together(
-        column_b, column_a_y, conv, half_got, low_mlp
-    )
-    column_b = joined(column_b, column_b_z)
-    columns = [column_a, column_a_y, column_b]
-    away = [swap(column, "core") for column in columns]
-    tiles = columns[:2] + away[:2] + columns[2:] + away[2:]
+    column_b_z, column_a_y, conv, half_got, low_mlp = together(
+        column_b_z, column_a_y, conv, half_got, low_mlp
+    )
+    away = [swap(column, "core") for column in (column_a, column_a_y, column_b, column_b_z)]
+    tiles = [column_a, column_a_y] + away[:2] + [column_b, column_b_z] + away[2:]
 
     halves = half_got[0][None] if ways == 2 else stacked(*half_got)
     halves, tiles = together(halves, tiles)

time: 173 us -> 172 us (level)
  waiting for transfers between devices: 37.5 us -> 35.7 us
    ppermute x19 -> x20, waiting for transfers between devices: 5.82 us -> 4.74 us  [swap(): return lax.ppermute(array, axis, [(0, 1), (1, 0)])]
    ppermute x19 -> x20, starting transfers between devices: 13 us -> 13.4 us  [swap(): return lax.ppermute(array, axis, [(0, 1), (1, 0)])]
    pallas_call x29 -> x28, Pallas kernels: 69.6 us -> 69.5 us  [run(): pl.pallas_call(kernel, out_shape=tuple(outs), in_specs=in_smem(smem) + in...]
  transfers between devices with their start and end apart: 39 -> 40, of which waited for: 14 -> 13; matrix products, arithmetic and copies ran while one was open for 0% -> 0% of each run, Pallas kernels for 44% -> 45%
where the time goes in v3:
time: 172 us; the launch traced here: 171 us
  Pallas kernels  93.3 us (54%)
  starting transfers between devices  40.1 us (23%)
  waiting for transfers between devices  35.7 us (21%)
    pallas_call x28, Pallas kernels, run(): pl.pallas_call(kernel, out_shape=tuple(outs), in_specs=in_smem(smem) + in...  69.5 us
    ppermute x6, waiting for transfers between devices, flipped(): lax.ppermute(array, axis, [(i, i ^ bit) for i in range(lax.axis_size(axis...  25.7 us
    pallas_call x4, Pallas kernels, update_feed(): pl.pallas_call(functools.partial(update_kernel, core_away, y_away), out_s...  16.9 us
    ppermute x12, starting transfers between devices, shifted(): lax.ppermute(array, axis, [(i, (i + distance) % count) for i in range(cou...  14.3 us
    ppermute x20, starting transfers between devices, swap(): return lax.ppermute(array, axis, [(0, 1), (1, 0)])  13.4 us
    ppermute x6, starting transfers between devices, flipped(): lax.ppermute(array, axis, [(i, i ^ bit) for i in range(lax.axis_size(axis...  7.79 us
    ppermute x20, waiting for transfers between devices, swap(): return lax.ppermute(array, axis, [(0, 1), (1, 0)])  4.74 us
  transfers between devices with their start and end apart: 40, of which 13 were waited for; matrix products, arithmetic and copies ran while one was open for 0% of the time, Pallas kernels for 45%

profile of v3, /device:TPU:0, one launch (start us, length us, event | category | flops | bytes accessed | tf_op | source)
XLA Modules:
  0.0 171.1 jit_solution(1086670168375023359)
XLA Ops:
  0.7 1.1 edges.1
  1.8 3.0 %collective-permute-start.1 = (bf16[128,512]{1,0:T(8,128)(2,1)S(1)}, bf16[128,512]{1,0:T(8,128)(2,1)S(1)}, u32[]{:S(2)}, u32[]{:S(2)}) collective-permute-start(bf16[128,512]{1,0:T(8,128)(2,1)S(1)} %get-tuple-element.221.refs_0_), channel_id=1, source_target_pairs={{0,4},{4,0},{1,5},{5,1},{2,6},{6,2},{3,7},{7,3},{8,12},{12,8},{9,1... | collective-permute-start | bytes 393224 | tf_op jit(solution)/shard_map/ppermute | solution.py:828
  4.8 2.6 %collective-permute-start = (bf16[1,128,512]{2,1,0:T(8,128)(2,1)S(1)}, bf16[1,128,512]{2,1,0:T(8,128)(2,1)S(1)}, u32[]{:S(2)}, u32[]{:S(2)}) collective-permute-start(bf16[1,128,512]{2,1,0:T(8,128)(2,1)S(1)} %bitcast.40), channel_id=1, source_target_pairs={{0,16},{8,24},{16,0},{24,8},{1,17},{9,25},{17,1},{25,9},{2,18},{10... | collective-permute-start | bytes 393224 | tf_op jit(solution)/shard_map/ppermute | solution.py:671
  7.4 3.4 %collective-permute-start.2 = (bf16[48,512]{1,0:T(8,128)(2,1)S(1)}, bf16[48,512]{1,0:T(8,128)(2,1)S(1)}, u32[]{:S(2)}, u32[]{:S(2)}) collective-permute-start(bf16[48,512]{1,0:T(8,128)(2,1)S(1)} %get-tuple-element.222), channel_id=1, source_target_pairs={{0,1},{1,2},{2,3},{3,4},{4,5},{5,6},{6,7},{7,8},{8,9},{9,10},{10,1... | collective-permute-start | bytes 147464 | tf_op jit(solution)/shard_map/ppermute | solution.py:996
  10.8 1.3 collective-permute-start.3
  12.2 1.3 collective-permute-done.second
  13.5 3.3 %collective-permute-done.3.after = bf16[48,512]{1,0:T(8,128)(2,1)S(1)} collective-permute-done((bf16[48,512]{1,0:T(8,128)(2,1)S(1)}, bf16[48,512]{1,0:T(8,128)(2,1)S(1)}, u32[]{:S(2)}, u32[]{:S(2)}) %collective-permute-start.3) | collective-permute-done | bytes 49184 | tf_op jit(solution)/shard_map/ppermute | solution.py:997
  16.8 2.2 %half.1 = bf16[528,1024]{1,0:T(8,128)(2,1)S(1)} custom-call(s32[5]{0:T(128)S(1)} %stack.23.place.refs_0_, f32[2,512,1024]{2,1,0:T(8,128)} %refs_0_.7, f32[1,1024]{1,0:T(1,128)S(1)} %bitcast.42), custom_call_target="tpu_custom_call" | custom-call | flops 1100000000 | bytes 3600000 | tf_op jit(solution)/shard_map/half/pallas_call | solution.py:1009
  19.1 1.6 collective-permute-start.6
  20.7 0.7 collective-permute-start.4
  21.4 9.6 %collective-permute-done.6.second = bf16[2,128,512]{2,1,0:T(8,128)(2,1)S(1)} collective-permute-done((bf16[2,128,512]{2,1,0:T(8,128)(2,1)S(1)}, bf16[2,128,512]{2,1,0:T(8,128)(2,1)S(1)}, u32[]{:S(2)}, u32[]{:S(2)}) %collective-permute-start.6) | collective-permute-done | bytes 262176 | tf_op jit(solution)/shard_map/ppermute | solution.py:671
  31.1 4.7 %collective-permute-done.4.second = bf16[1,2,128,512]{3,2,1,0:T(8,128)(2,1)S(1)} collective-permute-done((bf16[1,2,128,512]{3,2,1,0:T(8,128)(2,1)S(1)}, bf16[1,2,128,512]{3,2,1,0:T(8,128)(2,1)S(1)}, u32[]{:S(2)}, u32[]{:S(2)}) %collective-permute-start.4) | collective-permute-done | bytes 262176 | tf_op jit(solution)/shard_map/ppermute | solution.py:671
  35.9 1.2 tables.1
  37.1 6.7 %norm_conv.1 = (bf16[3,1088,512]{2,1,0:T(8,128)(2,1)S(1)}, bf16[1088,512]{1,0:T(8,128)(2,1)S(1)}, bf16[1056,512]{1,0:T(8,128)(2,1)S(1)}, bf16[1056,512]{1,0:T(8,...) custom-call(bf16[48,512]{1,0:T(8,128)(2,1)S(1)} %collective-permute-done.2.before, ...), custom_call_target="tpu_custom_call" | custom-call | flops 550000000 | bytes 1800000 | tf_op jit(solution)/shard_map/norm_conv/pallas_call | solution.py:860
  43.9 0.5 collective-permute-start.11
  44.4 2.3 %matrices.1 = bf16[2,512,1024]{2,1,0:T(8,128)(2,1)S(1)} custom-call(f32[2,512,1024]{2,1,0:T(8,128)} %refs_0_.7), custom_call_target="tpu_custom_call" | custom-call | flops 550000000 | bytes 1800000 | tf_op jit(solution)/shard_map/matrices/pallas_call | solution.py:1029
  46.8 2.5 %collective-permute-done.5.refs_5_ = bf16[2,2,128,512]{3,2,1,0:T(8,128)(2,1)} collective-permute-done((bf16[2,2,128,512]{3,2,1,0:T(8,128)(2,1)S(1)}, bf16[2,2,128,512]{3,2,1,0:T(8,128)(2,1)}, u32[]{:S(2)}, u32[]{:S(2)}) %collective-permute-start.5) | collective-permute-done | bytes 524320 | tf_op jit(solution)/shard_map/ppermute | solution.py:671
  49.3 0.5 collective-permute-start.12
  49.8 2.1 %collective-permute-done.10.refs_3_ = bf16[4,128,512]{2,1,0:T(8,128)(2,1)S(1)} collective-permute-done((bf16[4,128,512]{2,1,0:T(8,128)(2,1)S(1)}, bf16[4,128,512]{2,1,0:T(8,128)(2,1)S(1)}, u32[]{:S(2)}, u32[]{:S(2)}) %collective-permute-start.10) | collective-permute-done | bytes 524320 | tf_op jit(solution)/shard_map/ppermute | solution.py:828
  52.5 8.6 %attend.1 = (bf16[2048,512]{1,0:T(8,128)(2,1)S(1)}, bf16[1088,512]{1,0:T(8,128)(2,1)S(1)}, bf16[1088,512]{1,0:T(8,128)(2,1)S(1)}, bf16[1088,512]{1,0:T(8,128)(2,...) custom-call(s32[5]{0:T(128)S(1)} %copy-done.4, s32[16]{0:T(128)S(1)} %copy-done.6, ...), custom_call_target="tpu_custom_call" | custom-call | flops 550000000 | bytes 1800000 | tf_op jit(solution)/shard_map/attend/pallas_call | solution.py:860
  61.1 1.6 middle.1
  62.7 9.7 %feed.2 = (bf16[1,2,8,32,1024]{4,3,2,1,0:T(8,128)(2,1)S(1)}, bf16[1,2,8,32,1024]{4,3,2,1,0:T(8,128)(2,1)S(1)}, f32[1,1,1024]{2,1,0:T(1,128)S(1)}, f32[1056,512]{1,0:T(8,128)S(1)}, f32[1056,512]{1,0:T(8,128)S(1)}) custom-call(s32[5]{0:T(128)S(1)} %copy-done.4, bf16[1,528,1024]{2,1,0:T(8,128)(2,1)} %bitcast.8.refs_1_, ...), custom_call_target="tpu_custom_call" | custom-call | flops 15399999488 | bytes 50400000 | tf_op jit(solution)/shard_map/feed/pallas_call | solution.py:860
  72.4 0.4 collective-permute-start.14
  72.8 8.8 %feed.3 = (bf16[1,2,8,32,1024]{4,3,2,1,0:T(8,128)(2,1)S(1)}, bf16[1,2,8,32,1024]{4,3,2,1,0:T(8,128)(2,1)S(1)}, f32[1,1,1024]{2,1,0:T(1,128)S(1)}, f32[1056,512]{1,0:T(8,128)S(1)}, f32[1056,512]{1,0:T(8,128)S(1)}) custom-call(s32[5]{0:T(128)S(1)} %copy-done.4, bf16[1,512,1024]{2,1,0:T(8,128)(2,1)S(1)} %get-tuple-element.423.refs_1_, ...), custom_call_target="tpu_custom_call" | custom-call | flops 15399999488 | bytes 50400000 | tf_op jit(solution)/shard_map/feed/pallas_call | solution.py:860
  81.9 0.4 far_sum.1
  82.3 1.6 collective-permute-start.15
  83.9 1.2 collective-permute-start.18
  85.1 4.6 %middle_back.1 = (bf16[1024,512]{1,0:T(8,128)(2,1)}, f32[1024,512]{1,0:T(8,128)S(1)}, bf16[1056,512]{1,0:T(8,128)(2,1)S(1)}, bf16[512,512]{1,0:T(8,128)(2,1)S(1)}, f32[32,512]{1,0:T(8,128)S(1)}) custom-call(f32[1056,512]{1,0:T(8,128)S(1)} %get-tuple-element.251.middle, bf16[1056,512]{1,0:T(8,128)(2,1)S(1)} %get-tuple-element.252.cot, ...), custom_call_target="tpu_custom_call" | custom-call | flops 550000000 | bytes 1800000 | tf_op jit(solution)/shard_map/middle_back/pallas_call | solution.py:860
  89.7 1.2 collective-permute-done.15.refs_5_
  90.9 0.4 near_sum.1
  91.4 1.6 collective-permute-start.19
  93.0 5.6 %scores_back.2 = (bf16[1056,256]{1,0:T(8,128)(2,1)S(1)}, bf16[1056,256]{1,0:T(8,128)(2,1)S(1)}, bf16[1056,256]{1,0:T(8,128)(2,1)S(1)}, bf16[16,128,256]{2,1,0:T(8,128)(2,1)S(1)}, bf16[16,128,256]{2,1,0:T(8,128)(2,1)S(1)}) custom-call(s32[5]{0:T(128)S(1)} %copy-done.4, s32[16]{0:T(128)S(1)} %copy-done.6, bf16[1088,512]{1,0:T(8,128)(2,1)S(1)} %get-tuple-element.271.query, ...), custom_call_target="tpu_custom_call" | custom-call | flops 8800000000 | bytes 28800000 | tf_op jit(solution)/shard_map/scores_back/pallas_call | solution.py:860
  98.7 0.5 collective-permute-done.19.refs_3_
  99.2 0.4 feed_two.1
  99.6 1.6 collective-permute-start.20
  101.2 1.2 collective-permute-start.21
  102.4 5.6 %scores_back.3 = (bf16[1056,256]{1,0:T(8,128)(2,1)S(1)}, bf16[1056,256]{1,0:T(8,128)(2,1)S(1)}, bf16[1056,256]{1,0:T(8,128)(2,1)S(1)}, bf16[16,128,256]{2,1,0:T(8,128)(2,1)S(1)}, bf16[16,128,256]{2,1,0:T(8,128)(2,1)S(1)}) custom-call(s32[5]{0:T(128)S(1)} %copy-done.4, s32[16]{0:T(128)S(1)} %copy-done.6, bf16[1088,512]{1,0:T(8,128)(2,1)S(1)} %get-tuple-element.271.query, ...), custom_call_target="tpu_custom_call" | custom-call | flops 8800000000 | bytes 28800000 | tf_op jit(solution)/shard_map/scores_back/pallas_call | solution.py:860
  108.3 0.4 paired.2
  109.1 1.2 collective-permute-start.24
  110.3 2.3 %collective-permute-start.25 = (bf16[64,1024]{1,0:T(8,128)(2,1)S(1)}, bf16[64,1024]{1,0:T(8,128)(2,1)S(1)}, u32[]{:S(2)}, u32[]{:S(2)}) collective-permute-start(bf16[64,1024]{1,0:T(8,128)(2,1)S(1)} %get-tuple-element.338), channel_id=1, source_target_pairs={{0,24},{8,0},{16,8},{24,16},{1,25},{9,1},{17,9},{25,17},{2,26},{10... | collective-permute-start | bytes 393224 | tf_op jit(solution)/shard_map/ppermute | solution.py:833
  112.6 1.0 collective-permute-start.26
  113.6 0.4 paired.3
  114.0 1.7 %collective-permute-start.27 = (bf16[8,128,256]{2,1,0:T(8,128)(2,1)S(1)}, bf16[8,128,256]{2,1,0:T(8,128)(2,1)S(1)}, u32[]{:S(2)}, u32[]{:S(2)}) collective-permute-start(bf16[8,128,256]{2,1,0:T(8,128)(2,1)S(1)} %get-tuple-element.343), channel_id=1, source_target_pairs={{0,4},{4,0},{1,5},{5,1},{2,6},{6,2},{3,7},{7,3},{8,12},{12,8},{9,1... | collective-permute-start | bytes 1572872 | tf_op jit(solution)/shard_map/ppermute | solution.py:828
  115.8 1.9 %conv_grad.1 = f32[3,1056,512]{2,1,0:T(8,128)S(1)} custom-call(bf16[1056,256]{1,0:T(8,128)(2,1)S(1)} %get-tuple-element.317.refs_0_.query_grad_0, bf16[1056,256]{1,0:T(8,128)(2,1)S(1)} %get-tuple-element.328.refs_1_, bf16[1056,256]{1,0:T(8,128)(2,1)S(1)} %get-tuple-element.318.refs_2_.value_grad_0, ...), custom_call_target="tpu_custom_call" | custom-call | flops 22000001024 | bytes 72000000 | tf_op jit(solution)/shard_map/conv_grad/pallas_call | solution.py:860
  117.7 6.4 %conv_back.1 = (f32[1024,512]{1,0:T(8,128)S(1)}, f32[32,512]{1,0:T(8,128)S(1)}) custom-call(s32[5]{0:T(128)S(1)} %copy-done.4, bf16[1056,256]{1,0:T(8,128)(2,1)S(1)} %get-tuple-element.317.refs_0_.query_grad_0, bf16[1056,256]{1,0:T(8,128)(2,1)S(1)} %get-tuple-element.318.refs_2_.value_grad_0, bf16[1056,256]{1,0:T(8,128)(2,1)S(1)} %get-tuple-element.326.refs_3_.query_grad_1, ...), custom_call_target="tpu_custom_call" | custom-call | flops 13200000000 | bytes 43200000 | tf_op jit(solution)/shard_map/conv_back/pallas_call | solution.py:860
  124.2 0.6 collective-permute-start.31
  124.8 1.5 collective-permute-start.32
  126.4 2.8 %collective-permute-start.33 = (bf16[64,1024]{1,0:T(8,128)(2,1)S(1)}, bf16[64,1024]{1,0:T(8,128)(2,1)S(1)}, u32[]{:S(2)}, u32[]{:S(2)}) collective-permute-start(bf16[64,1024]{1,0:T(8,128)(2,1)S(1)} %bitcast.34), channel_id=1, source_target_pairs={{0,24},{8,0},{16,8},{24,16},{1,25},{9,1},{17,9},{25,17},{2,26},{10... | collective-permute-start | bytes 393224 | tf_op jit(solution)/shard_map/ppermute | solution.py:833
  129.5 0.4 collective-permute-start.29
  129.9 1.0 collective-permute-start.30
  130.9 4.6 %in_grad.1 = bf16[1024,512]{1,0:T(8,128)(2,1)} custom-call(f32[1024,512]{1,0:T(8,128)S(1)} %get-tuple-element.351.incoming, bf16[1024,512]{1,0:T(8,128)(2,1)} %frames.5, f32[1024,512]{1,0:T(8,128)S(1)} %get-tuple-element.352.middle_grad, f32[17,512]{1,0:T(8,128)S(1)} %copy-done.2), custom_call_target="tpu_custom_call" | custom-call | flops 22000001024 | bytes 72000000 | tf_op jit(solution)/shard_map/in_grad/pallas_call | solution.py:860
  135.5 2.0 %collective-permute-done.30.refs_1_ = bf16[4,128,256]{2,1,0:T(8,128)(2,1)S(1)} collective-permute-done((bf16[4,128,256]{2,1,0:T(8,128)(2,1)S(1)}, bf16[4,128,256]{2,1,0:T(8,128)(2,1)S(1)}, u32[]{:S(2)}, u32[]{:S(2)}) %collective-permute-start.30) | collective-permute-done | bytes 262176 | tf_op jit(solution)/shard_map/ppermute | solution.py:833
  137.5 0.6 collective-permute-done.29.line_got
  138.4 1.1 collective-permute-start.37
  139.5 1.4 collective-permute-start.35
  140.9 4.2 %update_feed.4 = (f32[2,512,1024]{2,1,0:T(8,128)}, f32[2,512,1024]{2,1,0:T(8,128)}, f32[2,512,1024]{2,1,0:T(8,128)}, f32[2,512,1024]{2,1,0:T(8,128)}) custom-call(s32[5]{0:T(128)S(1)} %copy-done.4, bf16[4,64,1024]{2,1,0:T(8,128)(2,1)S(1)} %stacked.3.column, f32[2,512,1024]{2,1,0:T(8,128)} %refs_0_.7, f32[2,512,1024]{2,1,0:T(8,128)} %refs_1_.7, ...), custom_call_target="tpu_custom_call" | custom-call | flops 330000000 | bytes 1080000 | tf_op jit(solution)/shard_map/update_feed/pallas_call | solution.py:912
  145.1 3.4 %collective-permute-done.35.got = bf16[288,512]{1,0:T(8,128)(2,1)S(1)} collective-permute-done((bf16[288,512]{1,0:T(8,128)(2,1)S(1)}, bf16[288,512]{1,0:T(8,128)(2,1)S(1)}, u32[]{:S(2)}, u32[]{:S(2)}) %collective-permute-start.35) | collective-permute-done | bytes 294944 | tf_op jit(solution)/shard_map/ppermute | solution.py:671
  148.7 1.4 collective-permute-start.36
  150.1 4.2 %update_feed.5 = (f32[2,512,1024]{2,1,0:T(8,128)}, f32[2,512,1024]{2,1,0:T(8,128)}, f32[2,512,1024]{2,1,0:T(8,128)}, f32[2,512,1024]{2,1,0:T(8,128)}) custom-call(s32[5]{0:T(128)S(1)} %copy-done.4, bf16[4,64,1024]{2,1,0:T(8,128)(2,1)S(1)} %collective-permute-done.34.column, ...), custom_call_target="tpu_custom_call", output_to_operand_aliasing={{0}: (6, {}), {1}: (7, {}), {2}: (8, {}), {3}: (9, {})} | custom-call | flops 330000000 | bytes 1080000 | tf_op jit(solution)/shard_map/update_feed/pallas_call | solution.py:912
  154.3 4.3 %collective-permute-done.36.got = bf16[160,512]{1,0:T(8,128)(2,1)S(1)} collective-permute-done((bf16[160,512]{1,0:T(8,128)(2,1)S(1)}, bf16[160,512]{1,0:T(8,128)(2,1)S(1)}, u32[]{:S(2)}, u32[]{:S(2)}) %collective-permute-start.36) | collective-permute-done | bytes 163872 | tf_op jit(solution)/shard_map/ppermute | solution.py:671
  158.7 0.9 collective-permute-start.39
  159.6 4.2 %update_feed.6 = (f32[2,512,1024]{2,1,0:T(8,128)}, f32[2,512,1024]{2,1,0:T(8,128)}, f32[2,512,1024]{2,1,0:T(8,128)}, f32[2,512,1024]{2,1,0:T(8,128)}) custom-call(s32[5]{0:T(128)S(1)} %copy-done.4, bf16[4,64,1024]{2,1,0:T(8,128)(2,1)S(1)} %collective-permute-done.37.column, ...), custom_call_target="tpu_custom_call", output_to_operand_aliasing={{0}: (6, {}), {1}: (7, {}), {2}: (8, {}), {3}: (9, {})} | custom-call | flops 330000000 | bytes 1080000 | tf_op jit(solution)/shard_map/update_feed/pallas_call | solution.py:912
  164.0 4.3 %update_feed.7 = (f32[2,512,1024]{2,1,0:T(8,128)}, f32[2,512,1024]{2,1,0:T(8,128)}, f32[2,512,1024]{2,1,0:T(8,128)}, f32[2,512,1024]{2,1,0:T(8,128)}) custom-call(s32[5]{0:T(128)S(1)} %copy-done.4, bf16[4,64,1024]{2,1,0:T(8,128)(2,1)S(1)} %collective-permute-done.38.column, ...), custom_call_target="tpu_custom_call", output_to_operand_aliasing={{0}: (6, {}), {1}: (7, {}), {2}: (8, {}), {3}: (9, {})} | custom-call | flops 330000000 | bytes 1080000 | tf_op jit(solution)/shard_map/update_feed/pallas_call | solution.py:912
  168.3 2.5 %update_rest.1 = (f32[2,128,512]{2,1,0:T(8,128)}, f32[2,128,512]{2,1,0:T(8,128)}, f32[2,128,512]{2,1,0:T(8,128)}, f32[2,128,512]{2,1,0:T(8,128)}, f32[17,512]{1,...) custom-call(s32[5]{0:T(128)S(1)} %copy-done.4, ...), custom_call_target="tpu_custom_call" | custom-call | flops 3300000000 | bytes 10800000 | tf_op jit(solution)/shard_map/update_rest/pallas_call | solution.py:860
  (86 shorter events, 2.9 us)
Async XLA Ops:
  0.7 16.1 %copy-start.5 = (f32[1024]{0:T(1024)S(1)}, f32[1024]{0:T(1024)}, u32[]{:S(2)}) copy-start(f32[1024]{0:T(1024)} %param.36) | copy-start | bytes 12292
  1.8 10.4 %collective-permute-start.1 = (bf16[128,512]{1,0:T(8,128)(2,1)S(1)}, bf16[128,512]{1,0:T(8,128)(2,1)S(1)}, u32[]{:S(2)}, u32[]{:S(2)}) collective-permute-start(bf16[128,512]{1,0:T(8,128)(2,1)S(1)} %get-tuple-element.221.refs_0_), channel_id=1, source_target_pairs={{0,4},{4,0},{1,5},{5,1},{2,6},{6,2},{3,7},{7,3},{8,12},{12,8},{9,1... | collective-permute-start | bytes 393224 | tf_op jit(solution)/shard_map/ppermute | solution.py:828
  4.8 8.7 %collective-permute-start = (bf16[1,128,512]{2,1,0:T(8,128)(2,1)S(1)}, bf16[1,128,512]{2,1,0:T(8,128)(2,1)S(1)}, u32[]{:S(2)}, u32[]{:S(2)}) collective-permute-start(bf16[1,128,512]{2,1,0:T(8,128)(2,1)S(1)} %bitcast.40), channel_id=1, source_target_pairs={{0,16},{8,24},{16,0},{24,8},{1,17},{9,25},{17,1},{25,9},{2,18},{10... | collective-permute-start | bytes 393224 | tf_op jit(solution)/shard_map/ppermute | solution.py:671
  7.4 6.1 %collective-permute-start.2 = (bf16[48,512]{1,0:T(8,128)(2,1)S(1)}, bf16[48,512]{1,0:T(8,128)(2,1)S(1)}, u32[]{:S(2)}, u32[]{:S(2)}) collective-permute-start(bf16[48,512]{1,0:T(8,128)(2,1)S(1)} %get-tuple-element.222), channel_id=1, source_target_pairs={{0,1},{1,2},{2,3},{3,4},{4,5},{5,6},{6,7},{7,8},{8,9},{9,10},{10,1... | collective-permute-start | bytes 147464 | tf_op jit(solution)/shard_map/ppermute | solution.py:996
  10.8 6.0 %collective-permute-start.3 = (bf16[48,512]{1,0:T(8,128)(2,1)S(1)}, bf16[48,512]{1,0:T(8,128)(2,1)S(1)}, u32[]{:S(2)}, u32[]{:S(2)}) collective-permute-start(bf16[48,512]{1,0:T(8,128)(2,1)S(1)} %get-tuple-element.223), channel_id=1, source_target_pairs={{1,0},{2,1},{3,2},{4,3},{5,4},{6,5},{7,6},{8,7},{9,8},{10,9},{11,1... | collective-permute-start | bytes 147464 | tf_op jit(solution)/shard_map/ppermute | solution.py:997
  12.2 6.8 %copy-start.3 = (s32[5]{0:T(128)}, s32[5]{0:T(128)S(1)}, u32[]{:S(2)}) copy-start(s32[5]{0:T(128)S(1)} %stack.23.place.refs_0_) | copy-start | bytes 64
  19.0 30.3 %collective-permute-start.8 = (bf16[528,1024]{1,0:T(8,128)(2,1)S(1)}, bf16[528,1024]{1,0:T(8,128)(2,1)}, u32[]{:S(2)}, u32[]{:S(2)}) collective-permute-start(bf16[528,1024]{1,0:T(8,128)(2,1)S(1)} %half.1), channel_id=1, source_target_pairs={{0,1},{1,0},{2,3},{3,2},{4,5},{5,4},{6,7},{7,6},{8,9},{9,8},{10,11... | collective-permute-start | bytes 3244040 | tf_op jit(solution)/shard_map/ppermute | solution.py:833
  19.1 11.9 %collective-permute-start.6 = (bf16[2,128,512]{2,1,0:T(8,128)(2,1)S(1)}, bf16[2,128,512]{2,1,0:T(8,128)(2,1)S(1)}, u32[]{:S(2)}, u32[]{:S(2)}) collective-permute-start(bf16[2,128,512]{2,1,0:T(8,128)(2,1)S(1)} %joined.3.first), channel_id=1, source_target_pairs={{0,8},{8,0},{16,24},{24,16},{1,9},{9,1},{17,25},{25,17},{2,10},{10... | collective-permute-start | bytes 786440 | tf_op jit(solution)/shard_map/ppermute | solution.py:671
  20.7 15.1 %collective-permute-start.4 = (bf16[1,2,128,512]{3,2,1,0:T(8,128)(2,1)S(1)}, bf16[1,2,128,512]{3,2,1,0:T(8,128)(2,1)S(1)}, u32[]{:S(2)}, u32[]{:S(2)}) collective-permute-start(bf16[1,2,128,512]{3,2,1,0:T(8,128)(2,1)S(1)} %bitcast.30), channel_id=1, source_target_pairs={{0,16},{8,24},{16,0},{24,8},{1,17},{9,25},{17,1},{25,9},{2,18},{10... | collective-permute-start | bytes 786440 | tf_op jit(solution)/shard_map/ppermute | solution.py:671
  31.0 15.8 %collective-permute-start.7 = (bf16[4,128,512]{2,1,0:T(8,128)(2,1)S(1)}, bf16[4,128,512]{2,1,0:T(8,128)(2,1)S(1)}, u32[]{:S(2)}, u32[]{:S(2)}) collective-permute-start(bf16[4,128,512]{2,1,0:T(8,128)(2,1)S(1)} %joined.5.refs_0_), channel_id=1, source_target_pairs={{0,4},{4,0},{1,5},{5,1},{2,6},{6,2},{3,7},{7,3},{8,12},{12,8},{9,1... | collective-permute-start | bytes 1572872 | tf_op jit(solution)/shard_map/ppermute | solution.py:828
  35.8 1.3 copy-start.2
  35.8 13.5 %collective-permute-start.5 = (bf16[2,2,128,512]{3,2,1,0:T(8,128)(2,1)S(1)}, bf16[2,2,128,512]{3,2,1,0:T(8,128)(2,1)}, u32[]{:S(2)}, u32[]{:S(2)}) collective-permute-start(bf16[2,2,128,512]{3,2,1,0:T(8,128)(2,1)S(1)} %joined.4.refs_4_), channel_id=1, source_target_pairs={{0,8},{8,0},{16,24},{24,16},{1,9},{9,1},{17,25},{25,17},{2,10},{10... | collective-permute-start | bytes 1572872 | tf_op jit(solution)/shard_map/ppermute | solution.py:671
  43.8 6.0 %collective-permute-start.9 = (bf16[4,128,512]{2,1,0:T(8,128)(2,1)S(1)}, bf16[4,128,512]{2,1,0:T(8,128)(2,1)S(1)}, u32[]{:S(2)}, u32[]{:S(2)}) collective-permute-start(bf16[4,128,512]{2,1,0:T(8,128)(2,1)S(1)} %joined.5.refs_0_), channel_id=1, source_target_pairs={{0,2},{2,0},{1,3},{3,1},{4,6},{6,4},{5,7},{7,5},{8,10},{10,8},{9,1... | collective-permute-start | bytes 1572872 | tf_op jit(solution)/shard_map/ppermute | solution.py:828
  43.9 5.9 %collective-permute-start.11 = (bf16[2,2,128,512]{3,2,1,0:T(8,128)(2,1)S(1)}, bf16[2,2,128,512]{3,2,1,0:T(8,128)(2,1)S(1)}, u32[]{:S(2)}, u32[]{:S(2)}) collective-permute-start(bf16[2,2,128,512]{3,2,1,0:T(8,128)(2,1)S(1)} %joined.4.refs_4_), channel_id=1, source_target_pairs={{0,2},{2,0},{1,3},{3,1},{4,6},{6,4},{5,7},{7,5},{8,10},{10,8},{9,1... | collective-permute-start | bytes 1572872 | tf_op jit(solution)/shard_map/ppermute | solution.py:828
  46.8 5.7 %copy-start.4 = (s32[5]{0:T(128)S(1)}, s32[5]{0:T(128)}, u32[]{:S(2)}) copy-start(s32[5]{0:T(128)} %copy-done.3) | copy-start | bytes 64
  46.8 5.7 %copy-start.6 = (s32[16]{0:T(128)S(1)}, s32[16]{0:T(128)}, u32[]{:S(2)}) copy-start(s32[16]{0:T(128)} %owners.7) | copy-start | bytes 196
  49.3 2.6 %collective-permute-start.10 = (bf16[4,128,512]{2,1,0:T(8,128)(2,1)S(1)}, bf16[4,128,512]{2,1,0:T(8,128)(2,1)S(1)}, u32[]{:S(2)}, u32[]{:S(2)}) collective-permute-start(bf16[4,128,512]{2,1,0:T(8,128)(2,1)S(1)} %collective-permute-done.7.refs_1_), channel_id=1, source_target_pairs={{0,2},{2,0},{1,3},{3,1},{4,6},{6,4},{5,7},{7,5},{8,10},{10,8},{9,1... | collective-permute-start | bytes 1572872 | tf_op jit(solution)/shard_map/ppermute | solution.py:828
  49.3 2.9 %collective-permute-start.12 = (bf16[2,2,128,512]{3,2,1,0:T(8,128)(2,1)}, bf16[2,2,128,512]{3,2,1,0:T(8,128)(2,1)S(1)}, u32[]{:S(2)}, u32[]{:S(2)}) collective-permute-start(bf16[2,2,128,512]{3,2,1,0:T(8,128)(2,1)} %collective-permute-done.5.refs_5_), channel_id=1, source_target_pairs={{0,2},{2,0},{1,3},{3,1},{4,6},{6,4},{5,7},{7,5},{8,10},{10,8},{9,1... | collective-permute-start | bytes 1572872 | tf_op jit(solution)/shard_map/ppermute | solution.py:828
  52.1 9.0 %collective-permute-start.13 = (bf16[1,528,1024]{2,1,0:T(8,128)(2,1)}, bf16[1,528,1024]{2,1,0:T(8,128)(2,1)S(1)}, u32[]{:S(2)}, u32[]{:S(2)}) collective-permute-start(bf16[1,528,1024]{2,1,0:T(8,128)(2,1)} %bitcast.8.refs_1_), channel_id=1, source_target_pairs={{0,2},{2,0},{1,3},{3,1},{4,6},{6,4},{5,7},{7,5},{8,10},{10,8},{9,1... | collective-permute-start | bytes 3244040 | tf_op jit(solution)/shard_map/ppermute | solution.py:828
  72.4 9.5 %collective-permute-start.14 = (bf16[1,2,8,32,1024]{4,3,2,1,0:T(8,128)(2,1)S(1)}, bf16[1,2,8,32,1024]{4,3,2,1,0:T(8,128)(2,1)S(1)}, u32[]{:S(2)}, u32[]{:S(2)}) collective-permute-start(bf16[1,2,8,32,1024]{4,3,2,1,0:T(8,128)(2,1)S(1)} %get-tuple-element.259), channel_id=1, source_target_pairs={{0,2},{2,0},{1,3},{3,1},{4,6},{6,4},{5,7},{7,5},{8,10},{10,8},{9,1... | collective-permute-start | bytes 3145736 | tf_op jit(solution)/shard_map/ppermute | solution.py:828
  81.7 9.3 %collective-permute-start.16 = (bf16[1,2,8,32,1024]{4,3,2,1,0:T(8,128)(2,1)S(1)}, bf16[1,2,8,32,1024]{4,3,2,1,0:T(8,128)(2,1)S(1)}, u32[]{:S(2)}, u32[]{:S(2)}) collective-permute-start(bf16[1,2,8,32,1024]{4,3,2,1,0:T(8,128)(2,1)S(1)} %get-tuple-element.279), channel_id=1, source_target_pairs={{0,2},{2,0},{1,3},{3,1},{4,6},{6,4},{5,7},{7,5},{8,10},{10,8},{9,1... | collective-permute-start | bytes 3145736 | tf_op jit(solution)/shard_map/ppermute | solution.py:828
  82.3 8.6 %collective-permute-start.15 = (bf16[4,32,1024]{2,1,0:T(8,128)(2,1)S(1)}, bf16[4,32,1024]{2,1,0:T(8,128)(2,1)S(1)}, u32[]{:S(2)}, u32[]{:S(2)}) collective-permute-start(bf16[4,32,1024]{2,1,0:T(8,128)(2,1)S(1)} %get-tuple-element.277), channel_id=1, source_target_pairs={{0,4},{4,0},{1,5},{5,1},{2,6},{6,2},{3,7},{7,3},{8,12},{12,8},{9,1... | collective-permute-start | bytes 786440 | tf_op jit(solution)/shard_map/ppermute | solution.py:828
  83.9 14.7 %collective-permute-start.18 = (bf16[8,32,1024]{2,1,0:T(8,128)(2,1)S(1)}, bf16[8,32,1024]{2,1,0:T(8,128)(2,1)S(1)}, u32[]{:S(2)}, u32[]{:S(2)}) collective-permute-start(bf16[8,32,1024]{2,1,0:T(8,128)(2,1)S(1)} %get-tuple-element.291), channel_id=1, source_target_pairs={{0,1},{1,0},{2,3},{3,2},{4,5},{5,4},{6,7},{7,6},{8,9},{9,8},{10,11... | collective-permute-start | bytes 1572872 | tf_op jit(solution)/shard_map/ppermute | solution.py:833
  91.4 7.8 %collective-permute-start.19 = (bf16[4,32,1024]{2,1,0:T(8,128)(2,1)S(1)}, bf16[4,32,1024]{2,1,0:T(8,128)(2,1)S(1)}, u32[]{:S(2)}, u32[]{:S(2)}) collective-permute-start(bf16[4,32,1024]{2,1,0:T(8,128)(2,1)S(1)} %get-tuple-element.293), channel_id=1, source_target_pairs={{0,4},{4,0},{1,5},{5,1},{2,6},{6,2},{3,7},{7,3},{8,12},{12,8},{9,1... | collective-permute-start | bytes 786440 | tf_op jit(solution)/shard_map/ppermute | solution.py:828
  98.6 9.7 %collective-permute-start.17 = (bf16[16,128,256]{2,1,0:T(8,128)(2,1)S(1)}, bf16[16,128,256]{2,1,0:T(8,128)(2,1)S(1)}, u32[]{:S(2)}, u32[]{:S(2)}) collective-permute-start(bf16[16,128,256]{2,1,0:T(8,128)(2,1)S(1)} %get-tuple-element.287), channel_id=1, source_target_pairs={{0,2},{2,0},{1,3},{3,1},{4,6},{6,4},{5,7},{7,5},{8,10},{10,8},{9,1... | collective-permute-start | bytes 3145736 | tf_op jit(solution)/shard_map/ppermute | solution.py:828
  99.6 8.5 %collective-permute-start.20 = (bf16[4,32,1024]{2,1,0:T(8,128)(2,1)S(1)}, bf16[4,32,1024]{2,1,0:T(8,128)(2,1)S(1)}, u32[]{:S(2)}, u32[]{:S(2)}) collective-permute-start(bf16[4,32,1024]{2,1,0:T(8,128)(2,1)S(1)} %get-tuple-element.304), channel_id=1, source_target_pairs={{0,4},{4,0},{1,5},{5,1},{2,6},{6,2},{3,7},{7,3},{8,12},{12,8},{9,1... | collective-permute-start | bytes 786440 | tf_op jit(solution)/shard_map/ppermute | solution.py:828
  101.2 6.9 %collective-permute-start.21 = (bf16[4,32,1024]{2,1,0:T(8,128)(2,1)S(1)}, bf16[4,32,1024]{2,1,0:T(8,128)(2,1)S(1)}, u32[]{:S(2)}, u32[]{:S(2)}) collective-permute-start(bf16[4,32,1024]{2,1,0:T(8,128)(2,1)S(1)} %get-tuple-element.306), channel_id=1, source_target_pairs={{0,1},{1,0},{2,3},{3,2},{4,5},{5,4},{6,7},{7,6},{8,9},{9,8},{10,11... | collective-permute-start | bytes 786440 | tf_op jit(solution)/shard_map/ppermute | solution.py:833
  108.0 5.6 %collective-permute-start.22 = (bf16[16,128,256]{2,1,0:T(8,128)(2,1)S(1)}, bf16[16,128,256]{2,1,0:T(8,128)(2,1)S(1)}, u32[]{:S(2)}, u32[]{:S(2)}) collective-permute-start(bf16[16,128,256]{2,1,0:T(8,128)(2,1)S(1)} %get-tuple-element.320), channel_id=1, source_target_pairs={{0,2},{2,0},{1,3},{3,1},{4,6},{6,4},{5,7},{7,5},{8,10},{10,8},{9,1... | collective-permute-start | bytes 3145736 | tf_op jit(solution)/shard_map/ppermute | solution.py:828
  108.7 15.3 %collective-permute-start.23 = (bf16[64,1024]{1,0:T(8,128)(2,1)S(1)}, bf16[64,1024]{1,0:T(8,128)(2,1)S(1)}, u32[]{:S(2)}, u32[]{:S(2)}) collective-permute-start(bf16[64,1024]{1,0:T(8,128)(2,1)S(1)} %get-tuple-element.336), channel_id=1, source_target_pairs={{0,8},{8,16},{16,24},{24,0},{1,9},{9,17},{17,25},{25,1},{2,10},{10... | collective-permute-start | bytes 393224 | tf_op jit(solution)/shard_map/ppermute | solution.py:833
  109.1 15.1 %collective-permute-start.24 = (bf16[64,1024]{1,0:T(8,128)(2,1)S(1)}, bf16[64,1024]{1,0:T(8,128)(2,1)S(1)}, u32[]{:S(2)}, u32[]{:S(2)}) collective-permute-start(bf16[64,1024]{1,0:T(8,128)(2,1)S(1)} %get-tuple-element.337), channel_id=1, source_target_pairs={{0,16},{8,24},{16,0},{24,8},{1,17},{9,25},{17,1},{25,9},{2,18},{10... | collective-permute-start | bytes 393224 | tf_op jit(solution)/shard_map/ppermute | solution.py:833
  110.3 13.8 %collective-permute-start.25 = (bf16[64,1024]{1,0:T(8,128)(2,1)S(1)}, bf16[64,1024]{1,0:T(8,128)(2,1)S(1)}, u32[]{:S(2)}, u32[]{:S(2)}) collective-permute-start(bf16[64,1024]{1,0:T(8,128)(2,1)S(1)} %get-tuple-element.338), channel_id=1, source_target_pairs={{0,24},{8,0},{16,8},{24,16},{1,25},{9,1},{17,9},{25,17},{2,26},{10... | collective-permute-start | bytes 393224 | tf_op jit(solution)/shard_map/ppermute | solution.py:833
  112.6 16.7 %collective-permute-start.26 = (bf16[8,128,256]{2,1,0:T(8,128)(2,1)S(1)}, bf16[8,128,256]{2,1,0:T(8,128)(2,1)S(1)}, u32[]{:S(2)}, u32[]{:S(2)}) collective-permute-start(bf16[8,128,256]{2,1,0:T(8,128)(2,1)S(1)} %get-tuple-element.341), channel_id=1, source_target_pairs={{0,1},{1,0},{2,3},{3,2},{4,5},{5,4},{6,7},{7,6},{8,9},{9,8},{10,11... | collective-permute-start | bytes 1572872 | tf_op jit(solution)/shard_map/ppermute | solution.py:833
  114.0 3.6 %copy-start = (bf16[1024,512]{1,0:T(8,128)(2,1)S(1)}, bf16[1024,512]{1,0:T(8,128)(2,1)}, u32[]{:S(2)}) copy-start(bf16[1024,512]{1,0:T(8,128)(2,1)} %frames.5) | copy-start | bytes 3145732
  114.0 15.2 %collective-permute-start.27 = (bf16[8,128,256]{2,1,0:T(8,128)(2,1)S(1)}, bf16[8,128,256]{2,1,0:T(8,128)(2,1)S(1)}, u32[]{:S(2)}, u32[]{:S(2)}) collective-permute-start(bf16[8,128,256]{2,1,0:T(8,128)(2,1)S(1)} %get-tuple-element.343), channel_id=1, source_target_pairs={{0,4},{4,0},{1,5},{5,1},{2,6},{6,2},{3,7},{7,3},{8,12},{12,8},{9,1... | collective-permute-start | bytes 1572872 | tf_op jit(solution)/shard_map/ppermute | solution.py:828
  124.0 2.3 %collective-permute-start.28 = (f32[32,512]{1,0:T(8,128)S(1)}, f32[32,512]{1,0:T(8,128)S(1)}, u32[]{:S(2)}, u32[]{:S(2)}) collective-permute-start(f32[32,512]{1,0:T(8,128)S(1)} %get-tuple-element.344.refs_4_), channel_id=1, source_target_pairs={{0,2},{2,0},{1,3},{3,1},{4,6},{6,4},{5,7},{7,5},{8,10},{10,8},{9,1... | collective-permute-start | bytes 196616 | tf_op jit(solution)/shard_map/ppermute | solution.py:828
  124.2 14.0 %collective-permute-start.31 = (bf16[64,1024]{1,0:T(8,128)(2,1)S(1)}, bf16[64,1024]{1,0:T(8,128)(2,1)S(1)}, u32[]{:S(2)}, u32[]{:S(2)}) collective-permute-start(bf16[64,1024]{1,0:T(8,128)(2,1)S(1)} %bitcast.32), channel_id=1, source_target_pairs={{0,8},{8,16},{16,24},{24,0},{1,9},{9,17},{17,25},{25,1},{2,10},{10... | collective-permute-start | bytes 393224 | tf_op jit(solution)/shard_map/ppermute | solution.py:833
  124.8 13.4 %collective-permute-start.32 = (bf16[64,1024]{1,0:T(8,128)(2,1)S(1)}, bf16[64,1024]{1,0:T(8,128)(2,1)S(1)}, u32[]{:S(2)}, u32[]{:S(2)}) collective-permute-start(bf16[64,1024]{1,0:T(8,128)(2,1)S(1)} %bitcast.33), channel_id=1, source_target_pairs={{0,16},{8,24},{16,0},{24,8},{1,17},{9,25},{17,1},{25,9},{2,18},{10... | collective-permute-start | bytes 393224 | tf_op jit(solution)/shard_map/ppermute | solution.py:833
  126.4 11.9 %collective-permute-start.33 = (bf16[64,1024]{1,0:T(8,128)(2,1)S(1)}, bf16[64,1024]{1,0:T(8,128)(2,1)S(1)}, u32[]{:S(2)}, u32[]{:S(2)}) collective-permute-start(bf16[64,1024]{1,0:T(8,128)(2,1)S(1)} %bitcast.34), channel_id=1, source_target_pairs={{0,24},{8,0},{16,8},{24,16},{1,25},{9,1},{17,9},{25,17},{2,26},{10... | collective-permute-start | bytes 393224 | tf_op jit(solution)/shard_map/ppermute | solution.py:833
  129.5 8.6 %collective-permute-start.29 = (bf16[576,256]{1,0:T(8,128)(2,1)S(1)}, bf16[576,256]{1,0:T(8,128)(2,1)S(1)}, u32[]{:S(2)}, u32[]{:S(2)}) collective-permute-start(bf16[576,256]{1,0:T(8,128)(2,1)S(1)} %get-tuple-element.356.line), channel_id=1, source_target_pairs={{0,4},{4,0},{1,5},{5,1},{2,6},{6,2},{3,7},{7,3},{8,12},{12,8},{9,1... | collective-permute-start | bytes 884744 | tf_op jit(solution)/shard_map/ppermute | solution.py:828
  129.9 7.6 %collective-permute-start.30 = (bf16[4,128,256]{2,1,0:T(8,128)(2,1)S(1)}, bf16[4,128,256]{2,1,0:T(8,128)(2,1)S(1)}, u32[]{:S(2)}, u32[]{:S(2)}) collective-permute-start(bf16[4,128,256]{2,1,0:T(8,128)(2,1)S(1)} %get-tuple-element.358), channel_id=1, source_target_pairs={{0,1},{1,0},{2,3},{3,2},{4,5},{5,4},{6,7},{7,6},{8,9},{9,8},{10,11... | collective-permute-start | bytes 786440 | tf_op jit(solution)/shard_map/ppermute | solution.py:833
  138.3 11.8 %collective-permute-start.34 = (bf16[4,64,1024]{2,1,0:T(8,128)(2,1)S(1)}, bf16[4,64,1024]{2,1,0:T(8,128)(2,1)S(1)}, u32[]{:S(2)}, u32[]{:S(2)}) collective-permute-start(bf16[4,64,1024]{2,1,0:T(8,128)(2,1)S(1)} %stacked.3.column), channel_id=1, source_target_pairs={{0,2},{2,0},{1,3},{3,1},{4,6},{6,4},{5,7},{7,5},{8,10},{10,8},{9,1... | collective-permute-start | bytes 1572872 | tf_op jit(solution)/shard_map/ppermute | solution.py:828
  138.4 20.2 %collective-permute-start.37 = (bf16[4,64,1024]{2,1,0:T(8,128)(2,1)S(1)}, bf16[4,64,1024]{2,1,0:T(8,128)(2,1)S(1)}, u32[]{:S(2)}, u32[]{:S(2)}) collective-permute-start(bf16[4,64,1024]{2,1,0:T(8,128)(2,1)S(1)} %stacked.3.column), channel_id=1, source_target_pairs={{0,4},{4,0},{1,5},{5,1},{2,6},{6,2},{3,7},{7,3},{8,12},{12,8},{9,1... | collective-permute-start | bytes 1572872 | tf_op jit(solution)/shard_map/ppermute | solution.py:828
  139.5 9.1 %collective-permute-start.35 = (bf16[288,512]{1,0:T(8,128)(2,1)S(1)}, bf16[288,512]{1,0:T(8,128)(2,1)S(1)}, u32[]{:S(2)}, u32[]{:S(2)}) collective-permute-start(bf16[288,512]{1,0:T(8,128)(2,1)S(1)} %get-tuple-element.372.sent), channel_id=1, source_target_pairs={{0,8},{8,0},{16,24},{24,16},{1,9},{9,1},{17,25},{25,17},{2,10},{10... | collective-permute-start | bytes 884744 | tf_op jit(solution)/shard_map/ppermute | solution.py:671
  148.7 9.9 %collective-permute-start.36 = (bf16[160,512]{1,0:T(8,128)(2,1)S(1)}, bf16[160,512]{1,0:T(8,128)(2,1)S(1)}, u32[]{:S(2)}, u32[]{:S(2)}) collective-permute-start(bf16[160,512]{1,0:T(8,128)(2,1)S(1)} %get-tuple-element.385.sent), channel_id=1, source_target_pairs={{0,16},{8,24},{16,0},{24,8},{1,17},{9,25},{17,1},{25,9},{2,18},{10... | collective-permute-start | bytes 491528 | tf_op jit(solution)/shard_map/ppermute | solution.py:671
  158.6 5.2 %collective-permute-start.38 = (bf16[4,64,1024]{2,1,0:T(8,128)(2,1)S(1)}, bf16[4,64,1024]{2,1,0:T(8,128)(2,1)S(1)}, u32[]{:S(2)}, u32[]{:S(2)}) collective-permute-start(bf16[4,64,1024]{2,1,0:T(8,128)(2,1)S(1)} %collective-permute-done.37.column), channel_id=1, source_target_pairs={{0,2},{2,0},{1,3},{3,1},{4,6},{6,4},{5,7},{7,5},{8,10},{10,8},{9,1... | collective-permute-start | bytes 1572872 | tf_op jit(solution)/shard_map/ppermute | solution.py:828
  158.7 9.5 %collective-permute-start.39 = (bf16[160,512]{1,0:T(8,128)(2,1)S(1)}, bf16[160,512]{1,0:T(8,128)(2,1)S(1)}, u32[]{:S(2)}, u32[]{:S(2)}) collective-permute-start(bf16[160,512]{1,0:T(8,128)(2,1)S(1)} %mine.1.refs_0_), channel_id=1, source_target_pairs={{0,1},{1,0},{2,3},{3,2},{4,5},{5,4},{6,7},{7,6},{8,9},{9,8},{10,11... | collective-permute-start | bytes 491528 | tf_op jit(solution)/shard_map/ppermute | solution.py:833
  163.8 4.4 %copy-start.1 = (f32[2,128,512]{2,1,0:T(8,128)S(1)}, f32[2,128,512]{2,1,0:T(8,128)}, u32[]{:S(2)}) copy-start(f32[2,128,512]{2,1,0:T(8,128)} %refs_2_.8) | copy-start | bytes 1572868
  163.9 4.4 %copy-start.7 = (f32[2,128,512]{2,1,0:T(8,128)S(1)}, f32[2,128,512]{2,1,0:T(8,128)}, u32[]{:S(2)}) copy-start(f32[2,128,512]{2,1,0:T(8,128)} %refs_3_.8) | copy-start | bytes 1572868
  163.9 4.4 %copy-start.8 = (f32[2,128,512]{2,1,0:T(8,128)S(1)}, f32[2,128,512]{2,1,0:T(8,128)}, u32[]{:S(2)}) copy-start(f32[2,128,512]{2,1,0:T(8,128)} %refs_4_.1) | copy-start | bytes 1572868
  163.9 4.4 %copy-start.9 = (f32[2,128,512]{2,1,0:T(8,128)S(1)}, f32[2,128,512]{2,1,0:T(8,128)}, u32[]{:S(2)}) copy-start(f32[2,128,512]{2,1,0:T(8,128)} %refs_5_.1) | copy-start | bytes 1572868
  163.9 4.4 %copy-start.10 = (f32[17,512]{1,0:T(8,128)S(1)}, f32[17,512]{1,0:T(8,128)}, u32[]{:S(2)}) copy-start(f32[17,512]{1,0:T(8,128)} %refs_7_.1) | copy-start | bytes 104452
  163.9 4.4 %copy-start.11 = (f32[17,512]{1,0:T(8,128)S(1)}, f32[17,512]{1,0:T(8,128)}, u32[]{:S(2)}) copy-start(f32[17,512]{1,0:T(8,128)} %refs_8_.1) | copy-start | bytes 104452
  163.9 4.4 %copy-start.12 = (f32[17,512]{1,0:T(8,128)S(1)}, f32[17,512]{1,0:T(8,128)}, u32[]{:S(2)}) copy-start(f32[17,512]{1,0:T(8,128)} %refs_9_.1) | copy-start | bytes 104452
  163.9 4.4 %copy-start.13 = (f32[1024]{0:T(1024)S(1)}, f32[1024]{0:T(1024)}, u32[]{:S(2)}) copy-start(f32[1024]{0:T(1024)} %param.37) | copy-start | bytes 12292
  163.9 4.4 %copy-start.14 = (f32[1024]{0:T(1024)S(1)}, f32[1024]{0:T(1024)}, u32[]{:S(2)}) copy-start(f32[1024]{0:T(1024)} %param.38) | copy-start | bytes 12292
  164.0 4.4 %copy-start.15 = (f32[1024]{0:T(1024)S(1)}, f32[1024]{0:T(1024)}, u32[]{:S(2)}) copy-start(f32[1024]{0:T(1024)} %param.39) | copy-start | bytes 12292

commit v4 on v3

--- a/solution.py
+++ b/solution.py
@@ -269,7 +269,7 @@
 
         return carry
 
-    lax.fori_loop(0, TILES, tile_step, 0)
+    lax.fori_loop(0, TILES, tile_step, 0, unroll=4)
 
     def matrix(c):
         return weights_out[c * width : (c + 1) * width, :]

time: 172 us -> 172 us (level)
  transfers between devices with their start and end apart: 40 -> 40, of which waited for: 13 -> 14; matrix products, arithmetic and copies ran while one was open for 0% -> 0% of each run, Pallas kernels for 45% -> 45%
where the time goes in v4:
time: 172 us; the launch traced here: 171 us
  Pallas kernels  93.5 us (54%)
  starting transfers between devices  40.3 us (23%)
  waiting for transfers between devices  35.6 us (21%)
    pallas_call x28, Pallas kernels, run(): pl.pallas_call(kernel, out_shape=tuple(outs), in_specs=in_smem(smem) + in...  69.6 us
    ppermute x6, waiting for transfers between devices, flipped(): lax.ppermute(array, axis, [(i, i ^ bit) for i in range(lax.axis_size(axis...  25.7 us
    pallas_call x4, Pallas kernels, update_feed(): pl.pallas_call(functools.partial(update_kernel, core_away, y_away), out_s...  16.9 us
    ppermute x12, starting transfers between devices, shifted(): lax.ppermute(array, axis, [(i, (i + distance) % count) for i in range(cou...  14.3 us
    ppermute x20, starting transfers between devices, swap(): return lax.ppermute(array, axis, [(0, 1), (1, 0)])  13.5 us
    ppermute x6, starting transfers between devices, flipped(): lax.ppermute(array, axis, [(i, i ^ bit) for i in range(lax.axis_size(axis...  7.8 us
    ppermute x20, waiting for transfers between devices, swap(): return lax.ppermute(array, axis, [(0, 1), (1, 0)])  4.44 us
  transfers between devices with their start and end apart: 40, of which 14 were waited for; matrix products, arithmetic and copies ran while one was open for 0% of the time, Pallas kernels for 45%

profile of v4, /device:TPU:0, one launch (start us, length us, event | category | flops | bytes accessed | tf_op | source)
XLA Modules:
  0.0 171.3 jit_solution(739543210075562400)
XLA Ops:
  0.7 1.1 edges.1
  1.8 3.0 %collective-permute-start.1 = (bf16[128,512]{1,0:T(8,128)(2,1)S(1)}, bf16[128,512]{1,0:T(8,128)(2,1)S(1)}, u32[]{:S(2)}, u32[]{:S(2)}) collective-permute-start(bf16[128,512]{1,0:T(8,128)(2,1)S(1)} %get-tuple-element.221.refs_0_), channel_id=1, source_target_pairs={{0,4},{4,0},{1,5},{5,1},{2,6},{6,2},{3,7},{7,3},{8,12},{12,8},{9,1... | collective-permute-start | bytes 393224 | tf_op jit(solution)/shard_map/ppermute | solution.py:828
  4.8 2.6 %collective-permute-start = (bf16[1,128,512]{2,1,0:T(8,128)(2,1)S(1)}, bf16[1,128,512]{2,1,0:T(8,128)(2,1)S(1)}, u32[]{:S(2)}, u32[]{:S(2)}) collective-permute-start(bf16[1,128,512]{2,1,0:T(8,128)(2,1)S(1)} %bitcast.40), channel_id=1, source_target_pairs={{0,16},{8,24},{16,0},{24,8},{1,17},{9,25},{17,1},{25,9},{2,18},{10... | collective-permute-start | bytes 393224 | tf_op jit(solution)/shard_map/ppermute | solution.py:671
  7.4 3.4 %collective-permute-start.2 = (bf16[48,512]{1,0:T(8,128)(2,1)S(1)}, bf16[48,512]{1,0:T(8,128)(2,1)S(1)}, u32[]{:S(2)}, u32[]{:S(2)}) collective-permute-start(bf16[48,512]{1,0:T(8,128)(2,1)S(1)} %get-tuple-element.222), channel_id=1, source_target_pairs={{0,1},{1,2},{2,3},{3,4},{4,5},{5,6},{6,7},{7,8},{8,9},{9,10},{10,1... | collective-permute-start | bytes 147464 | tf_op jit(solution)/shard_map/ppermute | solution.py:996
  10.8 1.3 collective-permute-start.3
  12.2 1.3 collective-permute-done.second
  13.5 3.3 %collective-permute-done.3.after = bf16[48,512]{1,0:T(8,128)(2,1)S(1)} collective-permute-done((bf16[48,512]{1,0:T(8,128)(2,1)S(1)}, bf16[48,512]{1,0:T(8,128)(2,1)S(1)}, u32[]{:S(2)}, u32[]{:S(2)}) %collective-permute-start.3) | collective-permute-done | bytes 49184 | tf_op jit(solution)/shard_map/ppermute | solution.py:997
  16.8 2.2 %half.1 = bf16[528,1024]{1,0:T(8,128)(2,1)S(1)} custom-call(s32[5]{0:T(128)S(1)} %stack.23.place.refs_0_, f32[2,512,1024]{2,1,0:T(8,128)} %refs_0_.7, f32[1,1024]{1,0:T(1,128)S(1)} %bitcast.42), custom_call_target="tpu_custom_call" | custom-call | flops 1100000000 | bytes 3600000 | tf_op jit(solution)/shard_map/half/pallas_call | solution.py:1009
  19.1 1.6 collective-permute-start.6
  20.7 0.7 collective-permute-start.4
  21.4 9.6 %collective-permute-done.6.second = bf16[2,128,512]{2,1,0:T(8,128)(2,1)S(1)} collective-permute-done((bf16[2,128,512]{2,1,0:T(8,128)(2,1)S(1)}, bf16[2,128,512]{2,1,0:T(8,128)(2,1)S(1)}, u32[]{:S(2)}, u32[]{:S(2)}) %collective-permute-start.6) | collective-permute-done | bytes 262176 | tf_op jit(solution)/shard_map/ppermute | solution.py:671
  31.1 4.7 %collective-permute-done.4.second = bf16[1,2,128,512]{3,2,1,0:T(8,128)(2,1)S(1)} collective-permute-done((bf16[1,2,128,512]{3,2,1,0:T(8,128)(2,1)S(1)}, bf16[1,2,128,512]{3,2,1,0:T(8,128)(2,1)S(1)}, u32[]{:S(2)}, u32[]{:S(2)}) %collective-permute-start.4) | collective-permute-done | bytes 262176 | tf_op jit(solution)/shard_map/ppermute | solution.py:671
  35.9 1.2 tables.1
  37.1 6.7 %norm_conv.1 = (bf16[3,1088,512]{2,1,0:T(8,128)(2,1)S(1)}, bf16[1088,512]{1,0:T(8,128)(2,1)S(1)}, bf16[1056,512]{1,0:T(8,128)(2,1)S(1)}, bf16[1056,512]{1,0:T(8,...) custom-call(bf16[48,512]{1,0:T(8,128)(2,1)S(1)} %collective-permute-done.2.before, ...), custom_call_target="tpu_custom_call" | custom-call | flops 550000000 | bytes 1800000 | tf_op jit(solution)/shard_map/norm_conv/pallas_call | solution.py:860
  43.9 0.5 collective-permute-start.11
  44.4 2.3 %matrices.1 = bf16[2,512,1024]{2,1,0:T(8,128)(2,1)S(1)} custom-call(f32[2,512,1024]{2,1,0:T(8,128)} %refs_0_.7), custom_call_target="tpu_custom_call" | custom-call | flops 550000000 | bytes 1800000 | tf_op jit(solution)/shard_map/matrices/pallas_call | solution.py:1029
  46.8 2.5 %collective-permute-done.5.refs_5_ = bf16[2,2,128,512]{3,2,1,0:T(8,128)(2,1)} collective-permute-done((bf16[2,2,128,512]{3,2,1,0:T(8,128)(2,1)S(1)}, bf16[2,2,128,512]{3,2,1,0:T(8,128)(2,1)}, u32[]{:S(2)}, u32[]{:S(2)}) %collective-permute-start.5) | collective-permute-done | bytes 524320 | tf_op jit(solution)/shard_map/ppermute | solution.py:671
  49.3 0.5 collective-permute-start.12
  49.8 2.1 %collective-permute-done.10.refs_3_ = bf16[4,128,512]{2,1,0:T(8,128)(2,1)S(1)} collective-permute-done((bf16[4,128,512]{2,1,0:T(8,128)(2,1)S(1)}, bf16[4,128,512]{2,1,0:T(8,128)(2,1)S(1)}, u32[]{:S(2)}, u32[]{:S(2)}) %collective-permute-start.10) | collective-permute-done | bytes 524320 | tf_op jit(solution)/shard_map/ppermute | solution.py:828
  52.5 8.6 %attend.1 = (bf16[2048,512]{1,0:T(8,128)(2,1)S(1)}, bf16[1088,512]{1,0:T(8,128)(2,1)S(1)}, bf16[1088,512]{1,0:T(8,128)(2,1)S(1)}, bf16[1088,512]{1,0:T(8,128)(2,...) custom-call(s32[5]{0:T(128)S(1)} %copy-done.4, s32[16]{0:T(128)S(1)} %copy-done.6, ...), custom_call_target="tpu_custom_call" | custom-call | flops 550000000 | bytes 1800000 | tf_op jit(solution)/shard_map/attend/pallas_call | solution.py:860
  61.1 1.6 middle.1
  62.6 9.6 %feed.2 = (bf16[1,2,8,32,1024]{4,3,2,1,0:T(8,128)(2,1)S(1)}, bf16[1,2,8,32,1024]{4,3,2,1,0:T(8,128)(2,1)S(1)}, f32[1,1,1024]{2,1,0:T(1,128)S(1)}, f32[1056,512]{1,0:T(8,128)S(1)}, f32[1056,512]{1,0:T(8,128)S(1)}) custom-call(s32[5]{0:T(128)S(1)} %copy-done.4, bf16[1,528,1024]{2,1,0:T(8,128)(2,1)} %bitcast.8.refs_1_, ...), custom_call_target="tpu_custom_call" | custom-call | flops 15399999488 | bytes 50400000 | tf_op jit(solution)/shard_map/feed/pallas_call | solution.py:860
  72.3 0.4 collective-permute-start.14
  72.7 8.8 %feed.3 = (bf16[1,2,8,32,1024]{4,3,2,1,0:T(8,128)(2,1)S(1)}, bf16[1,2,8,32,1024]{4,3,2,1,0:T(8,128)(2,1)S(1)}, f32[1,1,1024]{2,1,0:T(1,128)S(1)}, f32[1056,512]{1,0:T(8,128)S(1)}, f32[1056,512]{1,0:T(8,128)S(1)}) custom-call(s32[5]{0:T(128)S(1)} %copy-done.4, bf16[1,512,1024]{2,1,0:T(8,128)(2,1)S(1)} %get-tuple-element.423.refs_1_, ...), custom_call_target="tpu_custom_call" | custom-call | flops 15399999488 | bytes 50400000 | tf_op jit(solution)/shard_map/feed/pallas_call | solution.py:860
  81.8 0.4 far_sum.1
  82.2 1.7 collective-permute-start.15
  83.9 1.2 collective-permute-start.18
  85.1 4.6 %middle_back.1 = (bf16[1024,512]{1,0:T(8,128)(2,1)}, f32[1024,512]{1,0:T(8,128)S(1)}, bf16[1056,512]{1,0:T(8,128)(2,1)S(1)}, bf16[512,512]{1,0:T(8,128)(2,1)S(1)}, f32[32,512]{1,0:T(8,128)S(1)}) custom-call(f32[1056,512]{1,0:T(8,128)S(1)} %get-tuple-element.251.middle, bf16[1056,512]{1,0:T(8,128)(2,1)S(1)} %get-tuple-element.252.cot, ...), custom_call_target="tpu_custom_call" | custom-call | flops 550000000 | bytes 1800000 | tf_op jit(solution)/shard_map/middle_back/pallas_call | solution.py:860
  89.7 1.1 collective-permute-done.15.refs_5_
  90.9 0.4 near_sum.1
  91.3 1.6 collective-permute-start.19
  92.9 5.8 %scores_back.2 = (bf16[1056,256]{1,0:T(8,128)(2,1)S(1)}, bf16[1056,256]{1,0:T(8,128)(2,1)S(1)}, bf16[1056,256]{1,0:T(8,128)(2,1)S(1)}, bf16[16,128,256]{2,1,0:T(8,128)(2,1)S(1)}, bf16[16,128,256]{2,1,0:T(8,128)(2,1)S(1)}) custom-call(s32[5]{0:T(128)S(1)} %copy-done.4, s32[16]{0:T(128)S(1)} %copy-done.6, bf16[1088,512]{1,0:T(8,128)(2,1)S(1)} %get-tuple-element.271.query, ...), custom_call_target="tpu_custom_call" | custom-call | flops 8800000000 | bytes 28800000 | tf_op jit(solution)/shard_map/scores_back/pallas_call | solution.py:860
  99.1 0.4 feed_two.1
  99.5 1.6 collective-permute-start.20
  101.1 1.2 collective-permute-start.21
  102.4 5.6 %scores_back.3 = (bf16[1056,256]{1,0:T(8,128)(2,1)S(1)}, bf16[1056,256]{1,0:T(8,128)(2,1)S(1)}, bf16[1056,256]{1,0:T(8,128)(2,1)S(1)}, bf16[16,128,256]{2,1,0:T(8,128)(2,1)S(1)}, bf16[16,128,256]{2,1,0:T(8,128)(2,1)S(1)}) custom-call(s32[5]{0:T(128)S(1)} %copy-done.4, s32[16]{0:T(128)S(1)} %copy-done.6, bf16[1088,512]{1,0:T(8,128)(2,1)S(1)} %get-tuple-element.271.query, ...), custom_call_target="tpu_custom_call" | custom-call | flops 8800000000 | bytes 28800000 | tf_op jit(solution)/shard_map/scores_back/pallas_call | solution.py:860
  108.3 0.4 paired.2
  108.8 0.4 collective-permute-start.23
  109.2 1.3 collective-permute-start.24
  110.5 2.2 %collective-permute-start.25 = (bf16[64,1024]{1,0:T(8,128)(2,1)S(1)}, bf16[64,1024]{1,0:T(8,128)(2,1)S(1)}, u32[]{:S(2)}, u32[]{:S(2)}) collective-permute-start(bf16[64,1024]{1,0:T(8,128)(2,1)S(1)} %get-tuple-element.338), channel_id=1, source_target_pairs={{0,24},{8,0},{16,8},{24,16},{1,25},{9,1},{17,9},{25,17},{2,26},{10... | collective-permute-start | bytes 393224 | tf_op jit(solution)/shard_map/ppermute | solution.py:833
  112.7 1.1 collective-permute-start.26
  113.8 0.4 paired.3
  114.2 1.7 %collective-permute-start.27 = (bf16[8,128,256]{2,1,0:T(8,128)(2,1)S(1)}, bf16[8,128,256]{2,1,0:T(8,128)(2,1)S(1)}, u32[]{:S(2)}, u32[]{:S(2)}) collective-permute-start(bf16[8,128,256]{2,1,0:T(8,128)(2,1)S(1)} %get-tuple-element.343), channel_id=1, source_target_pairs={{0,4},{4,0},{1,5},{5,1},{2,6},{6,2},{3,7},{7,3},{8,12},{12,8},{9,1... | collective-permute-start | bytes 1572872 | tf_op jit(solution)/shard_map/ppermute | solution.py:828
  115.9 1.9 %conv_grad.1 = f32[3,1056,512]{2,1,0:T(8,128)S(1)} custom-call(bf16[1056,256]{1,0:T(8,128)(2,1)S(1)} %get-tuple-element.317.refs_0_.query_grad_0, bf16[1056,256]{1,0:T(8,128)(2,1)S(1)} %get-tuple-element.328.refs_1_, bf16[1056,256]{1,0:T(8,128)(2,1)S(1)} %get-tuple-element.318.refs_2_.value_grad_0, ...), custom_call_target="tpu_custom_call" | custom-call | flops 22000001024 | bytes 72000000 | tf_op jit(solution)/shard_map/conv_grad/pallas_call | solution.py:860
  117.8 6.4 %conv_back.1 = (f32[1024,512]{1,0:T(8,128)S(1)}, f32[32,512]{1,0:T(8,128)S(1)}) custom-call(s32[5]{0:T(128)S(1)} %copy-done.4, bf16[1056,256]{1,0:T(8,128)(2,1)S(1)} %get-tuple-element.317.refs_0_.query_grad_0, bf16[1056,256]{1,0:T(8,128)(2,1)S(1)} %get-tuple-element.318.refs_2_.value_grad_0, bf16[1056,256]{1,0:T(8,128)(2,1)S(1)} %get-tuple-element.326.refs_3_.query_grad_1, ...), custom_call_target="tpu_custom_call" | custom-call | flops 13200000000 | bytes 43200000 | tf_op jit(solution)/shard_map/conv_back/pallas_call | solution.py:860
  124.4 0.6 collective-permute-start.31
  125.0 1.5 collective-permute-start.32
  126.6 2.8 %collective-permute-start.33 = (bf16[64,1024]{1,0:T(8,128)(2,1)S(1)}, bf16[64,1024]{1,0:T(8,128)(2,1)S(1)}, u32[]{:S(2)}, u32[]{:S(2)}) collective-permute-start(bf16[64,1024]{1,0:T(8,128)(2,1)S(1)} %bitcast.34), channel_id=1, source_target_pairs={{0,24},{8,0},{16,8},{24,16},{1,25},{9,1},{17,9},{25,17},{2,26},{10... | collective-permute-start | bytes 393224 | tf_op jit(solution)/shard_map/ppermute | solution.py:833
  129.7 0.4 collective-permute-start.29
  130.1 0.9 collective-permute-start.30
  131.0 4.6 %in_grad.1 = bf16[1024,512]{1,0:T(8,128)(2,1)} custom-call(f32[1024,512]{1,0:T(8,128)S(1)} %get-tuple-element.351.incoming, bf16[1024,512]{1,0:T(8,128)(2,1)} %frames.5, f32[1024,512]{1,0:T(8,128)S(1)} %get-tuple-element.352.middle_grad, f32[17,512]{1,0:T(8,128)S(1)} %copy-done.2), custom_call_target="tpu_custom_call" | custom-call | flops 22000001024 | bytes 72000000 | tf_op jit(solution)/shard_map/in_grad/pallas_call | solution.py:860
  135.6 2.1 %collective-permute-done.30.refs_1_ = bf16[4,128,256]{2,1,0:T(8,128)(2,1)S(1)} collective-permute-done((bf16[4,128,256]{2,1,0:T(8,128)(2,1)S(1)}, bf16[4,128,256]{2,1,0:T(8,128)(2,1)S(1)}, u32[]{:S(2)}, u32[]{:S(2)}) %collective-permute-start.30) | collective-permute-done | bytes 262176 | tf_op jit(solution)/shard_map/ppermute | solution.py:833
  137.7 0.6 collective-permute-done.29.line_got
  138.6 1.1 collective-permute-start.37
  139.7 1.4 collective-permute-start.35
  141.1 4.2 %update_feed.4 = (f32[2,512,1024]{2,1,0:T(8,128)}, f32[2,512,1024]{2,1,0:T(8,128)}, f32[2,512,1024]{2,1,0:T(8,128)}, f32[2,512,1024]{2,1,0:T(8,128)}) custom-call(s32[5]{0:T(128)S(1)} %copy-done.4, bf16[4,64,1024]{2,1,0:T(8,128)(2,1)S(1)} %stacked.3.column, f32[2,512,1024]{2,1,0:T(8,128)} %refs_0_.7, f32[2,512,1024]{2,1,0:T(8,128)} %refs_1_.7, ...), custom_call_target="tpu_custom_call" | custom-call | flops 330000000 | bytes 1080000 | tf_op jit(solution)/shard_map/update_feed/pallas_call | solution.py:912
  145.3 3.4 %collective-permute-done.35.got = bf16[288,512]{1,0:T(8,128)(2,1)S(1)} collective-permute-done((bf16[288,512]{1,0:T(8,128)(2,1)S(1)}, bf16[288,512]{1,0:T(8,128)(2,1)S(1)}, u32[]{:S(2)}, u32[]{:S(2)}) %collective-permute-start.35) | collective-permute-done | bytes 294944 | tf_op jit(solution)/shard_map/ppermute | solution.py:671
  148.8 1.4 collective-permute-start.36
  150.3 4.2 %update_feed.5 = (f32[2,512,1024]{2,1,0:T(8,128)}, f32[2,512,1024]{2,1,0:T(8,128)}, f32[2,512,1024]{2,1,0:T(8,128)}, f32[2,512,1024]{2,1,0:T(8,128)}) custom-call(s32[5]{0:T(128)S(1)} %copy-done.4, bf16[4,64,1024]{2,1,0:T(8,128)(2,1)S(1)} %collective-permute-done.34.column, ...), custom_call_target="tpu_custom_call", output_to_operand_aliasing={{0}: (6, {}), {1}: (7, {}), {2}: (8, {}), {3}: (9, {})} | custom-call | flops 330000000 | bytes 1080000 | tf_op jit(solution)/shard_map/update_feed/pallas_call | solution.py:912
  154.5 4.3 %collective-permute-done.36.got = bf16[160,512]{1,0:T(8,128)(2,1)S(1)} collective-permute-done((bf16[160,512]{1,0:T(8,128)(2,1)S(1)}, bf16[160,512]{1,0:T(8,128)(2,1)S(1)}, u32[]{:S(2)}, u32[]{:S(2)}) %collective-permute-start.36) | collective-permute-done | bytes 163872 | tf_op jit(solution)/shard_map/ppermute | solution.py:671
  158.9 0.9 collective-permute-start.39
  159.8 4.2 %update_feed.6 = (f32[2,512,1024]{2,1,0:T(8,128)}, f32[2,512,1024]{2,1,0:T(8,128)}, f32[2,512,1024]{2,1,0:T(8,128)}, f32[2,512,1024]{2,1,0:T(8,128)}) custom-call(s32[5]{0:T(128)S(1)} %copy-done.4, bf16[4,64,1024]{2,1,0:T(8,128)(2,1)S(1)} %collective-permute-done.37.column, ...), custom_call_target="tpu_custom_call", output_to_operand_aliasing={{0}: (6, {}), {1}: (7, {}), {2}: (8, {}), {3}: (9, {})} | custom-call | flops 330000000 | bytes 1080000 | tf_op jit(solution)/shard_map/update_feed/pallas_call | solution.py:912
  164.2 4.3 %update_feed.7 = (f32[2,512,1024]{2,1,0:T(8,128)}, f32[2,512,1024]{2,1,0:T(8,128)}, f32[2,512,1024]{2,1,0:T(8,128)}, f32[2,512,1024]{2,1,0:T(8,128)}) custom-call(s32[5]{0:T(128)S(1)} %copy-done.4, bf16[4,64,1024]{2,1,0:T(8,128)(2,1)S(1)} %collective-permute-done.38.column, ...), custom_call_target="tpu_custom_call", output_to_operand_aliasing={{0}: (6, {}), {1}: (7, {}), {2}: (8, {}), {3}: (9, {})} | custom-call | flops 330000000 | bytes 1080000 | tf_op jit(solution)/shard_map/update_feed/pallas_call | solution.py:912
  168.5 2.5 %update_rest.1 = (f32[2,128,512]{2,1,0:T(8,128)}, f32[2,128,512]{2,1,0:T(8,128)}, f32[2,128,512]{2,1,0:T(8,128)}, f32[2,128,512]{2,1,0:T(8,128)}, f32[17,512]{1,...) custom-call(s32[5]{0:T(128)S(1)} %copy-done.4, ...), custom_call_target="tpu_custom_call" | custom-call | flops 3300000000 | bytes 10800000 | tf_op jit(solution)/shard_map/update_rest/pallas_call | solution.py:860
  (86 shorter events, 2.9 us)
Async XLA Ops:
  0.7 16.1 %copy-start.5 = (f32[1024]{0:T(1024)S(1)}, f32[1024]{0:T(1024)}, u32[]{:S(2)}) copy-start(f32[1024]{0:T(1024)} %param.36) | copy-start | bytes 12292
  1.8 10.4 %collective-permute-start.1 = (bf16[128,512]{1,0:T(8,128)(2,1)S(1)}, bf16[128,512]{1,0:T(8,128)(2,1)S(1)}, u32[]{:S(2)}, u32[]{:S(2)}) collective-permute-start(bf16[128,512]{1,0:T(8,128)(2,1)S(1)} %get-tuple-element.221.refs_0_), channel_id=1, source_target_pairs={{0,4},{4,0},{1,5},{5,1},{2,6},{6,2},{3,7},{7,3},{8,12},{12,8},{9,1... | collective-permute-start | bytes 393224 | tf_op jit(solution)/shard_map/ppermute | solution.py:828
  4.8 8.7 %collective-permute-start = (bf16[1,128,512]{2,1,0:T(8,128)(2,1)S(1)}, bf16[1,128,512]{2,1,0:T(8,128)(2,1)S(1)}, u32[]{:S(2)}, u32[]{:S(2)}) collective-permute-start(bf16[1,128,512]{2,1,0:T(8,128)(2,1)S(1)} %bitcast.40), channel_id=1, source_target_pairs={{0,16},{8,24},{16,0},{24,8},{1,17},{9,25},{17,1},{25,9},{2,18},{10... | collective-permute-start | bytes 393224 | tf_op jit(solution)/shard_map/ppermute | solution.py:671
  7.4 6.1 %collective-permute-start.2 = (bf16[48,512]{1,0:T(8,128)(2,1)S(1)}, bf16[48,512]{1,0:T(8,128)(2,1)S(1)}, u32[]{:S(2)}, u32[]{:S(2)}) collective-permute-start(bf16[48,512]{1,0:T(8,128)(2,1)S(1)} %get-tuple-element.222), channel_id=1, source_target_pairs={{0,1},{1,2},{2,3},{3,4},{4,5},{5,6},{6,7},{7,8},{8,9},{9,10},{10,1... | collective-permute-start | bytes 147464 | tf_op jit(solution)/shard_map/ppermute | solution.py:996
  10.8 6.0 %collective-permute-start.3 = (bf16[48,512]{1,0:T(8,128)(2,1)S(1)}, bf16[48,512]{1,0:T(8,128)(2,1)S(1)}, u32[]{:S(2)}, u32[]{:S(2)}) collective-permute-start(bf16[48,512]{1,0:T(8,128)(2,1)S(1)} %get-tuple-element.223), channel_id=1, source_target_pairs={{1,0},{2,1},{3,2},{4,3},{5,4},{6,5},{7,6},{8,7},{9,8},{10,9},{11,1... | collective-permute-start | bytes 147464 | tf_op jit(solution)/shard_map/ppermute | solution.py:997
  12.2 6.8 %copy-start.3 = (s32[5]{0:T(128)}, s32[5]{0:T(128)S(1)}, u32[]{:S(2)}) copy-start(s32[5]{0:T(128)S(1)} %stack.23.place.refs_0_) | copy-start | bytes 64
  19.0 30.3 %collective-permute-start.8 = (bf16[528,1024]{1,0:T(8,128)(2,1)S(1)}, bf16[528,1024]{1,0:T(8,128)(2,1)}, u32[]{:S(2)}, u32[]{:S(2)}) collective-permute-start(bf16[528,1024]{1,0:T(8,128)(2,1)S(1)} %half.1), channel_id=1, source_target_pairs={{0,1},{1,0},{2,3},{3,2},{4,5},{5,4},{6,7},{7,6},{8,9},{9,8},{10,11... | collective-permute-start | bytes 3244040 | tf_op jit(solution)/shard_map/ppermute | solution.py:833
  19.1 11.9 %collective-permute-start.6 = (bf16[2,128,512]{2,1,0:T(8,128)(2,1)S(1)}, bf16[2,128,512]{2,1,0:T(8,128)(2,1)S(1)}, u32[]{:S(2)}, u32[]{:S(2)}) collective-permute-start(bf16[2,128,512]{2,1,0:T(8,128)(2,1)S(1)} %joined.3.first), channel_id=1, source_target_pairs={{0,8},{8,0},{16,24},{24,16},{1,9},{9,1},{17,25},{25,17},{2,10},{10... | collective-permute-start | bytes 786440 | tf_op jit(solution)/shard_map/ppermute | solution.py:671
  20.7 15.1 %collective-permute-start.4 = (bf16[1,2,128,512]{3,2,1,0:T(8,128)(2,1)S(1)}, bf16[1,2,128,512]{3,2,1,0:T(8,128)(2,1)S(1)}, u32[]{:S(2)}, u32[]{:S(2)}) collective-permute-start(bf16[1,2,128,512]{3,2,1,0:T(8,128)(2,1)S(1)} %bitcast.30), channel_id=1, source_target_pairs={{0,16},{8,24},{16,0},{24,8},{1,17},{9,25},{17,1},{25,9},{2,18},{10... | collective-permute-start | bytes 786440 | tf_op jit(solution)/shard_map/ppermute | solution.py:671
  31.0 15.8 %collective-permute-start.7 = (bf16[4,128,512]{2,1,0:T(8,128)(2,1)S(1)}, bf16[4,128,512]{2,1,0:T(8,128)(2,1)S(1)}, u32[]{:S(2)}, u32[]{:S(2)}) collective-permute-start(bf16[4,128,512]{2,1,0:T(8,128)(2,1)S(1)} %joined.5.refs_0_), channel_id=1, source_target_pairs={{0,4},{4,0},{1,5},{5,1},{2,6},{6,2},{3,7},{7,3},{8,12},{12,8},{9,1... | collective-permute-start | bytes 1572872 | tf_op jit(solution)/shard_map/ppermute | solution.py:828
  35.8 1.3 copy-start.2
  35.8 13.5 %collective-permute-start.5 = (bf16[2,2,128,512]{3,2,1,0:T(8,128)(2,1)S(1)}, bf16[2,2,128,512]{3,2,1,0:T(8,128)(2,1)}, u32[]{:S(2)}, u32[]{:S(2)}) collective-permute-start(bf16[2,2,128,512]{3,2,1,0:T(8,128)(2,1)S(1)} %joined.4.refs_4_), channel_id=1, source_target_pairs={{0,8},{8,0},{16,24},{24,16},{1,9},{9,1},{17,25},{25,17},{2,10},{10... | collective-permute-start | bytes 1572872 | tf_op jit(solution)/shard_map/ppermute | solution.py:671
  43.8 6.0 %collective-permute-start.9 = (bf16[4,128,512]{2,1,0:T(8,128)(2,1)S(1)}, bf16[4,128,512]{2,1,0:T(8,128)(2,1)S(1)}, u32[]{:S(2)}, u32[]{:S(2)}) collective-permute-start(bf16[4,128,512]{2,1,0:T(8,128)(2,1)S(1)} %joined.5.refs_0_), channel_id=1, source_target_pairs={{0,2},{2,0},{1,3},{3,1},{4,6},{6,4},{5,7},{7,5},{8,10},{10,8},{9,1... | collective-permute-start | bytes 1572872 | tf_op jit(solution)/shard_map/ppermute | solution.py:828
  43.9 5.9 %collective-permute-start.11 = (bf16[2,2,128,512]{3,2,1,0:T(8,128)(2,1)S(1)}, bf16[2,2,128,512]{3,2,1,0:T(8,128)(2,1)S(1)}, u32[]{:S(2)}, u32[]{:S(2)}) collective-permute-start(bf16[2,2,128,512]{3,2,1,0:T(8,128)(2,1)S(1)} %joined.4.refs_4_), channel_id=1, source_target_pairs={{0,2},{2,0},{1,3},{3,1},{4,6},{6,4},{5,7},{7,5},{8,10},{10,8},{9,1... | collective-permute-start | bytes 1572872 | tf_op jit(solution)/shard_map/ppermute | solution.py:828
  46.8 5.7 %copy-start.4 = (s32[5]{0:T(128)S(1)}, s32[5]{0:T(128)}, u32[]{:S(2)}) copy-start(s32[5]{0:T(128)} %copy-done.3) | copy-start | bytes 64
  46.8 5.7 %copy-start.6 = (s32[16]{0:T(128)S(1)}, s32[16]{0:T(128)}, u32[]{:S(2)}) copy-start(s32[16]{0:T(128)} %owners.7) | copy-start | bytes 196
  49.3 2.6 %collective-permute-start.10 = (bf16[4,128,512]{2,1,0:T(8,128)(2,1)S(1)}, bf16[4,128,512]{2,1,0:T(8,128)(2,1)S(1)}, u32[]{:S(2)}, u32[]{:S(2)}) collective-permute-start(bf16[4,128,512]{2,1,0:T(8,128)(2,1)S(1)} %collective-permute-done.7.refs_1_), channel_id=1, source_target_pairs={{0,2},{2,0},{1,3},{3,1},{4,6},{6,4},{5,7},{7,5},{8,10},{10,8},{9,1... | collective-permute-start | bytes 1572872 | tf_op jit(solution)/shard_map/ppermute | solution.py:828
  49.3 2.9 %collective-permute-start.12 = (bf16[2,2,128,512]{3,2,1,0:T(8,128)(2,1)}, bf16[2,2,128,512]{3,2,1,0:T(8,128)(2,1)S(1)}, u32[]{:S(2)}, u32[]{:S(2)}) collective-permute-start(bf16[2,2,128,512]{3,2,1,0:T(8,128)(2,1)} %collective-permute-done.5.refs_5_), channel_id=1, source_target_pairs={{0,2},{2,0},{1,3},{3,1},{4,6},{6,4},{5,7},{7,5},{8,10},{10,8},{9,1... | collective-permute-start | bytes 1572872 | tf_op jit(solution)/shard_map/ppermute | solution.py:828
  52.1 8.9 %collective-permute-start.13 = (bf16[1,528,1024]{2,1,0:T(8,128)(2,1)}, bf16[1,528,1024]{2,1,0:T(8,128)(2,1)S(1)}, u32[]{:S(2)}, u32[]{:S(2)}) collective-permute-start(bf16[1,528,1024]{2,1,0:T(8,128)(2,1)} %bitcast.8.refs_1_), channel_id=1, source_target_pairs={{0,2},{2,0},{1,3},{3,1},{4,6},{6,4},{5,7},{7,5},{8,10},{10,8},{9,1... | collective-permute-start | bytes 3244040 | tf_op jit(solution)/shard_map/ppermute | solution.py:828
  72.3 9.5 %collective-permute-start.14 = (bf16[1,2,8,32,1024]{4,3,2,1,0:T(8,128)(2,1)S(1)}, bf16[1,2,8,32,1024]{4,3,2,1,0:T(8,128)(2,1)S(1)}, u32[]{:S(2)}, u32[]{:S(2)}) collective-permute-start(bf16[1,2,8,32,1024]{4,3,2,1,0:T(8,128)(2,1)S(1)} %get-tuple-element.259), channel_id=1, source_target_pairs={{0,2},{2,0},{1,3},{3,1},{4,6},{6,4},{5,7},{7,5},{8,10},{10,8},{9,1... | collective-permute-start | bytes 3145736 | tf_op jit(solution)/shard_map/ppermute | solution.py:828
  81.6 9.3 %collective-permute-start.16 = (bf16[1,2,8,32,1024]{4,3,2,1,0:T(8,128)(2,1)S(1)}, bf16[1,2,8,32,1024]{4,3,2,1,0:T(8,128)(2,1)S(1)}, u32[]{:S(2)}, u32[]{:S(2)}) collective-permute-start(bf16[1,2,8,32,1024]{4,3,2,1,0:T(8,128)(2,1)S(1)} %get-tuple-element.279), channel_id=1, source_target_pairs={{0,2},{2,0},{1,3},{3,1},{4,6},{6,4},{5,7},{7,5},{8,10},{10,8},{9,1... | collective-permute-start | bytes 3145736 | tf_op jit(solution)/shard_map/ppermute | solution.py:828
  82.2 8.7 %collective-permute-start.15 = (bf16[4,32,1024]{2,1,0:T(8,128)(2,1)S(1)}, bf16[4,32,1024]{2,1,0:T(8,128)(2,1)S(1)}, u32[]{:S(2)}, u32[]{:S(2)}) collective-permute-start(bf16[4,32,1024]{2,1,0:T(8,128)(2,1)S(1)} %get-tuple-element.277), channel_id=1, source_target_pairs={{0,4},{4,0},{1,5},{5,1},{2,6},{6,2},{3,7},{7,3},{8,12},{12,8},{9,1... | collective-permute-start | bytes 786440 | tf_op jit(solution)/shard_map/ppermute | solution.py:828
  83.9 15.0 %collective-permute-start.18 = (bf16[8,32,1024]{2,1,0:T(8,128)(2,1)S(1)}, bf16[8,32,1024]{2,1,0:T(8,128)(2,1)S(1)}, u32[]{:S(2)}, u32[]{:S(2)}) collective-permute-start(bf16[8,32,1024]{2,1,0:T(8,128)(2,1)S(1)} %get-tuple-element.291), channel_id=1, source_target_pairs={{0,1},{1,0},{2,3},{3,2},{4,5},{5,4},{6,7},{7,6},{8,9},{9,8},{10,11... | collective-permute-start | bytes 1572872 | tf_op jit(solution)/shard_map/ppermute | solution.py:833
  91.3 7.8 %collective-permute-start.19 = (bf16[4,32,1024]{2,1,0:T(8,128)(2,1)S(1)}, bf16[4,32,1024]{2,1,0:T(8,128)(2,1)S(1)}, u32[]{:S(2)}, u32[]{:S(2)}) collective-permute-start(bf16[4,32,1024]{2,1,0:T(8,128)(2,1)S(1)} %get-tuple-element.293), channel_id=1, source_target_pairs={{0,4},{4,0},{1,5},{5,1},{2,6},{6,2},{3,7},{7,3},{8,12},{12,8},{9,1... | collective-permute-start | bytes 786440 | tf_op jit(solution)/shard_map/ppermute | solution.py:828
  98.7 9.6 %collective-permute-start.17 = (bf16[16,128,256]{2,1,0:T(8,128)(2,1)S(1)}, bf16[16,128,256]{2,1,0:T(8,128)(2,1)S(1)}, u32[]{:S(2)}, u32[]{:S(2)}) collective-permute-start(bf16[16,128,256]{2,1,0:T(8,128)(2,1)S(1)} %get-tuple-element.287), channel_id=1, source_target_pairs={{0,2},{2,0},{1,3},{3,1},{4,6},{6,4},{5,7},{7,5},{8,10},{10,8},{9,1... | collective-permute-start | bytes 3145736 | tf_op jit(solution)/shard_map/ppermute | solution.py:828
  99.5 8.5 %collective-permute-start.20 = (bf16[4,32,1024]{2,1,0:T(8,128)(2,1)S(1)}, bf16[4,32,1024]{2,1,0:T(8,128)(2,1)S(1)}, u32[]{:S(2)}, u32[]{:S(2)}) collective-permute-start(bf16[4,32,1024]{2,1,0:T(8,128)(2,1)S(1)} %get-tuple-element.304), channel_id=1, source_target_pairs={{0,4},{4,0},{1,5},{5,1},{2,6},{6,2},{3,7},{7,3},{8,12},{12,8},{9,1... | collective-permute-start | bytes 786440 | tf_op jit(solution)/shard_map/ppermute | solution.py:828
  101.1 7.0 %collective-permute-start.21 = (bf16[4,32,1024]{2,1,0:T(8,128)(2,1)S(1)}, bf16[4,32,1024]{2,1,0:T(8,128)(2,1)S(1)}, u32[]{:S(2)}, u32[]{:S(2)}) collective-permute-start(bf16[4,32,1024]{2,1,0:T(8,128)(2,1)S(1)} %get-tuple-element.306), channel_id=1, source_target_pairs={{0,1},{1,0},{2,3},{3,2},{4,5},{5,4},{6,7},{7,6},{8,9},{9,8},{10,11... | collective-permute-start | bytes 786440 | tf_op jit(solution)/shard_map/ppermute | solution.py:833
  108.0 5.8 %collective-permute-start.22 = (bf16[16,128,256]{2,1,0:T(8,128)(2,1)S(1)}, bf16[16,128,256]{2,1,0:T(8,128)(2,1)S(1)}, u32[]{:S(2)}, u32[]{:S(2)}) collective-permute-start(bf16[16,128,256]{2,1,0:T(8,128)(2,1)S(1)} %get-tuple-element.320), channel_id=1, source_target_pairs={{0,2},{2,0},{1,3},{3,1},{4,6},{6,4},{5,7},{7,5},{8,10},{10,8},{9,1... | collective-permute-start | bytes 3145736 | tf_op jit(solution)/shard_map/ppermute | solution.py:828
  108.8 15.4 %collective-permute-start.23 = (bf16[64,1024]{1,0:T(8,128)(2,1)S(1)}, bf16[64,1024]{1,0:T(8,128)(2,1)S(1)}, u32[]{:S(2)}, u32[]{:S(2)}) collective-permute-start(bf16[64,1024]{1,0:T(8,128)(2,1)S(1)} %get-tuple-element.336), channel_id=1, source_target_pairs={{0,8},{8,16},{16,24},{24,0},{1,9},{9,17},{17,25},{25,1},{2,10},{10... | collective-permute-start | bytes 393224 | tf_op jit(solution)/shard_map/ppermute | solution.py:833
  109.2 15.2 %collective-permute-start.24 = (bf16[64,1024]{1,0:T(8,128)(2,1)S(1)}, bf16[64,1024]{1,0:T(8,128)(2,1)S(1)}, u32[]{:S(2)}, u32[]{:S(2)}) collective-permute-start(bf16[64,1024]{1,0:T(8,128)(2,1)S(1)} %get-tuple-element.337), channel_id=1, source_target_pairs={{0,16},{8,24},{16,0},{24,8},{1,17},{9,25},{17,1},{25,9},{2,18},{10... | collective-permute-start | bytes 393224 | tf_op jit(solution)/shard_map/ppermute | solution.py:833
  110.5 13.8 %collective-permute-start.25 = (bf16[64,1024]{1,0:T(8,128)(2,1)S(1)}, bf16[64,1024]{1,0:T(8,128)(2,1)S(1)}, u32[]{:S(2)}, u32[]{:S(2)}) collective-permute-start(bf16[64,1024]{1,0:T(8,128)(2,1)S(1)} %get-tuple-element.338), channel_id=1, source_target_pairs={{0,24},{8,0},{16,8},{24,16},{1,25},{9,1},{17,9},{25,17},{2,26},{10... | collective-permute-start | bytes 393224 | tf_op jit(solution)/shard_map/ppermute | solution.py:833
  112.7 16.7 %collective-permute-start.26 = (bf16[8,128,256]{2,1,0:T(8,128)(2,1)S(1)}, bf16[8,128,256]{2,1,0:T(8,128)(2,1)S(1)}, u32[]{:S(2)}, u32[]{:S(2)}) collective-permute-start(bf16[8,128,256]{2,1,0:T(8,128)(2,1)S(1)} %get-tuple-element.341), channel_id=1, source_target_pairs={{0,1},{1,0},{2,3},{3,2},{4,5},{5,4},{6,7},{7,6},{8,9},{9,8},{10,11... | collective-permute-start | bytes 1572872 | tf_op jit(solution)/shard_map/ppermute | solution.py:833
  114.2 3.6 %copy-start = (bf16[1024,512]{1,0:T(8,128)(2,1)S(1)}, bf16[1024,512]{1,0:T(8,128)(2,1)}, u32[]{:S(2)}) copy-start(bf16[1024,512]{1,0:T(8,128)(2,1)} %frames.5) | copy-start | bytes 3145732
  114.2 15.2 %collective-permute-start.27 = (bf16[8,128,256]{2,1,0:T(8,128)(2,1)S(1)}, bf16[8,128,256]{2,1,0:T(8,128)(2,1)S(1)}, u32[]{:S(2)}, u32[]{:S(2)}) collective-permute-start(bf16[8,128,256]{2,1,0:T(8,128)(2,1)S(1)} %get-tuple-element.343), channel_id=1, source_target_pairs={{0,4},{4,0},{1,5},{5,1},{2,6},{6,2},{3,7},{7,3},{8,12},{12,8},{9,1... | collective-permute-start | bytes 1572872 | tf_op jit(solution)/shard_map/ppermute | solution.py:828
  124.2 2.3 %collective-permute-start.28 = (f32[32,512]{1,0:T(8,128)S(1)}, f32[32,512]{1,0:T(8,128)S(1)}, u32[]{:S(2)}, u32[]{:S(2)}) collective-permute-start(f32[32,512]{1,0:T(8,128)S(1)} %get-tuple-element.344.refs_4_), channel_id=1, source_target_pairs={{0,2},{2,0},{1,3},{3,1},{4,6},{6,4},{5,7},{7,5},{8,10},{10,8},{9,1... | collective-permute-start | bytes 196616 | tf_op jit(solution)/shard_map/ppermute | solution.py:828
  124.4 14.0 %collective-permute-start.31 = (bf16[64,1024]{1,0:T(8,128)(2,1)S(1)}, bf16[64,1024]{1,0:T(8,128)(2,1)S(1)}, u32[]{:S(2)}, u32[]{:S(2)}) collective-permute-start(bf16[64,1024]{1,0:T(8,128)(2,1)S(1)} %bitcast.32), channel_id=1, source_target_pairs={{0,8},{8,16},{16,24},{24,0},{1,9},{9,17},{17,25},{25,1},{2,10},{10... | collective-permute-start | bytes 393224 | tf_op jit(solution)/shard_map/ppermute | solution.py:833
  125.0 13.4 %collective-permute-start.32 = (bf16[64,1024]{1,0:T(8,128)(2,1)S(1)}, bf16[64,1024]{1,0:T(8,128)(2,1)S(1)}, u32[]{:S(2)}, u32[]{:S(2)}) collective-permute-start(bf16[64,1024]{1,0:T(8,128)(2,1)S(1)} %bitcast.33), channel_id=1, source_target_pairs={{0,16},{8,24},{16,0},{24,8},{1,17},{9,25},{17,1},{25,9},{2,18},{10... | collective-permute-start | bytes 393224 | tf_op jit(solution)/shard_map/ppermute | solution.py:833
  126.6 11.9 %collective-permute-start.33 = (bf16[64,1024]{1,0:T(8,128)(2,1)S(1)}, bf16[64,1024]{1,0:T(8,128)(2,1)S(1)}, u32[]{:S(2)}, u32[]{:S(2)}) collective-permute-start(bf16[64,1024]{1,0:T(8,128)(2,1)S(1)} %bitcast.34), channel_id=1, source_target_pairs={{0,24},{8,0},{16,8},{24,16},{1,25},{9,1},{17,9},{25,17},{2,26},{10... | collective-permute-start | bytes 393224 | tf_op jit(solution)/shard_map/ppermute | solution.py:833
  129.7 8.6 %collective-permute-start.29 = (bf16[576,256]{1,0:T(8,128)(2,1)S(1)}, bf16[576,256]{1,0:T(8,128)(2,1)S(1)}, u32[]{:S(2)}, u32[]{:S(2)}) collective-permute-start(bf16[576,256]{1,0:T(8,128)(2,1)S(1)} %get-tuple-element.356.line), channel_id=1, source_target_pairs={{0,4},{4,0},{1,5},{5,1},{2,6},{6,2},{3,7},{7,3},{8,12},{12,8},{9,1... | collective-permute-start | bytes 884744 | tf_op jit(solution)/shard_map/ppermute | solution.py:828
  130.1 7.6 %collective-permute-start.30 = (bf16[4,128,256]{2,1,0:T(8,128)(2,1)S(1)}, bf16[4,128,256]{2,1,0:T(8,128)(2,1)S(1)}, u32[]{:S(2)}, u32[]{:S(2)}) collective-permute-start(bf16[4,128,256]{2,1,0:T(8,128)(2,1)S(1)} %get-tuple-element.358), channel_id=1, source_target_pairs={{0,1},{1,0},{2,3},{3,2},{4,5},{5,4},{6,7},{7,6},{8,9},{9,8},{10,11... | collective-permute-start | bytes 786440 | tf_op jit(solution)/shard_map/ppermute | solution.py:833
  138.5 11.8 %collective-permute-start.34 = (bf16[4,64,1024]{2,1,0:T(8,128)(2,1)S(1)}, bf16[4,64,1024]{2,1,0:T(8,128)(2,1)S(1)}, u32[]{:S(2)}, u32[]{:S(2)}) collective-permute-start(bf16[4,64,1024]{2,1,0:T(8,128)(2,1)S(1)} %stacked.3.column), channel_id=1, source_target_pairs={{0,2},{2,0},{1,3},{3,1},{4,6},{6,4},{5,7},{7,5},{8,10},{10,8},{9,1... | collective-permute-start | bytes 1572872 | tf_op jit(solution)/shard_map/ppermute | solution.py:828
  138.6 20.2 %collective-permute-start.37 = (bf16[4,64,1024]{2,1,0:T(8,128)(2,1)S(1)}, bf16[4,64,1024]{2,1,0:T(8,128)(2,1)S(1)}, u32[]{:S(2)}, u32[]{:S(2)}) collective-permute-start(bf16[4,64,1024]{2,1,0:T(8,128)(2,1)S(1)} %stacked.3.column), channel_id=1, source_target_pairs={{0,4},{4,0},{1,5},{5,1},{2,6},{6,2},{3,7},{7,3},{8,12},{12,8},{9,1... | collective-permute-start | bytes 1572872 | tf_op jit(solution)/shard_map/ppermute | solution.py:828
  139.7 9.1 %collective-permute-start.35 = (bf16[288,512]{1,0:T(8,128)(2,1)S(1)}, bf16[288,512]{1,0:T(8,128)(2,1)S(1)}, u32[]{:S(2)}, u32[]{:S(2)}) collective-permute-start(bf16[288,512]{1,0:T(8,128)(2,1)S(1)} %get-tuple-element.372.sent), channel_id=1, source_target_pairs={{0,8},{8,0},{16,24},{24,16},{1,9},{9,1},{17,25},{25,17},{2,10},{10... | collective-permute-start | bytes 884744 | tf_op jit(solution)/shard_map/ppermute | solution.py:671
  148.8 9.9 %collective-permute-start.36 = (bf16[160,512]{1,0:T(8,128)(2,1)S(1)}, bf16[160,512]{1,0:T(8,128)(2,1)S(1)}, u32[]{:S(2)}, u32[]{:S(2)}) collective-permute-start(bf16[160,512]{1,0:T(8,128)(2,1)S(1)} %get-tuple-element.385.sent), channel_id=1, source_target_pairs={{0,16},{8,24},{16,0},{24,8},{1,17},{9,25},{17,1},{25,9},{2,18},{10... | collective-permute-start | bytes 491528 | tf_op jit(solution)/shard_map/ppermute | solution.py:671
  158.8 5.2 %collective-permute-start.38 = (bf16[4,64,1024]{2,1,0:T(8,128)(2,1)S(1)}, bf16[4,64,1024]{2,1,0:T(8,128)(2,1)S(1)}, u32[]{:S(2)}, u32[]{:S(2)}) collective-permute-start(bf16[4,64,1024]{2,1,0:T(8,128)(2,1)S(1)} %collective-permute-done.37.column), channel_id=1, source_target_pairs={{0,2},{2,0},{1,3},{3,1},{4,6},{6,4},{5,7},{7,5},{8,10},{10,8},{9,1... | collective-permute-start | bytes 1572872 | tf_op jit(solution)/shard_map/ppermute | solution.py:828
  158.9 9.5 %collective-permute-start.39 = (bf16[160,512]{1,0:T(8,128)(2,1)S(1)}, bf16[160,512]{1,0:T(8,128)(2,1)S(1)}, u32[]{:S(2)}, u32[]{:S(2)}) collective-permute-start(bf16[160,512]{1,0:T(8,128)(2,1)S(1)} %mine.1.refs_0_), channel_id=1, source_target_pairs={{0,1},{1,0},{2,3},{3,2},{4,5},{5,4},{6,7},{7,6},{8,9},{9,8},{10,11... | collective-permute-start | bytes 491528 | tf_op jit(solution)/shard_map/ppermute | solution.py:833
  164.0 4.4 %copy-start.1 = (f32[2,128,512]{2,1,0:T(8,128)S(1)}, f32[2,128,512]{2,1,0:T(8,128)}, u32[]{:S(2)}) copy-start(f32[2,128,512]{2,1,0:T(8,128)} %refs_2_.8) | copy-start | bytes 1572868
  164.0 4.4 %copy-start.7 = (f32[2,128,512]{2,1,0:T(8,128)S(1)}, f32[2,128,512]{2,1,0:T(8,128)}, u32[]{:S(2)}) copy-start(f32[2,128,512]{2,1,0:T(8,128)} %refs_3_.8) | copy-start | bytes 1572868
  164.1 4.4 %copy-start.8 = (f32[2,128,512]{2,1,0:T(8,128)S(1)}, f32[2,128,512]{2,1,0:T(8,128)}, u32[]{:S(2)}) copy-start(f32[2,128,512]{2,1,0:T(8,128)} %refs_4_.1) | copy-start | bytes 1572868
  164.1 4.4 %copy-start.9 = (f32[2,128,512]{2,1,0:T(8,128)S(1)}, f32[2,128,512]{2,1,0:T(8,128)}, u32[]{:S(2)}) copy-start(f32[2,128,512]{2,1,0:T(8,128)} %refs_5_.1) | copy-start | bytes 1572868
  164.1 4.4 %copy-start.10 = (f32[17,512]{1,0:T(8,128)S(1)}, f32[17,512]{1,0:T(8,128)}, u32[]{:S(2)}) copy-start(f32[17,512]{1,0:T(8,128)} %refs_7_.1) | copy-start | bytes 104452
  164.1 4.4 %copy-start.11 = (f32[17,512]{1,0:T(8,128)S(1)}, f32[17,512]{1,0:T(8,128)}, u32[]{:S(2)}) copy-start(f32[17,512]{1,0:T(8,128)} %refs_8_.1) | copy-start | bytes 104452
  164.1 4.4 %copy-start.12 = (f32[17,512]{1,0:T(8,128)S(1)}, f32[17,512]{1,0:T(8,128)}, u32[]{:S(2)}) copy-start(f32[17,512]{1,0:T(8,128)} %refs_9_.1) | copy-start | bytes 104452
  164.1 4.4 %copy-start.13 = (f32[1024]{0:T(1024)S(1)}, f32[1024]{0:T(1024)}, u32[]{:S(2)}) copy-start(f32[1024]{0:T(1024)} %param.37) | copy-start | bytes 12292
  164.1 4.4 %copy-start.14 = (f32[1024]{0:T(1024)S(1)}, f32[1024]{0:T(1024)}, u32[]{:S(2)}) copy-start(f32[1024]{0:T(1024)} %param.38) | copy-start | bytes 12292
  164.1 4.4 %copy-start.15 = (f32[1024]{0:T(1024)S(1)}, f32[1024]{0:T(1024)}, u32[]{:S(2)}) copy-start(f32[1024]{0:T(1024)} %param.39) | copy-start | bytes 12292
